TPU v7x, 512 devices: a whole 4x8x8 slice. The times are simulated.
512 devices in a mesh: dp: 32 (over x_hi, z, core), graph: 16 (over y, x_lo).
Axes of the slice: x: 4 (x_hi: 2, x_lo: 2; x = x_hi * 2 + x_lo), y: 8, z: 8, core: 2. Of those that a mesh axis runs over, the one named last changes fastest.
Arguments:
- embeddings: bfloat16 [32, 64, 49, 128], P('dp', 'graph'), may hold values from -6 to 6
- atom_counts: int32 [32], P('dp'), may hold values from 32 to 64, as said below
- edge_counts: int32 [32, 16], P('dp', 'graph'), may hold values from 1 to 128, 1024 in all within a row
- source: int32 [32, 2048], P('dp', 'graph'), may hold values from 0 to 63, as said below
- target: int32 [32, 2048], P('dp', 'graph'), may hold values from 0 to 63, as said below
- wigner: bfloat16 [32, 29, 49, 2048], P('dp', None, None, 'graph'), may hold values from -4 to 4, as said below
- cotangent: float32 [32, 64, 49, 128], P('dp', 'graph'), may hold values from -6 to 6
- w_zero: bfloat16 [896, 896], P('graph', 'dp'), may hold values from -0.1875 to 0.1875
- w_one_real: bfloat16 [768, 768], P('graph', 'dp'), may hold values from -0.15625 to 0.15625
- w_one_imag: bfloat16 [768, 768], P('graph', 'dp'), may hold values from -0.15625 to 0.15625
- w_two_real: bfloat16 [640, 640], P('graph', 'dp'), may hold values from -0.15625 to 0.15625
- w_two_imag: bfloat16 [640, 640], P('graph', 'dp'), may hold values from -0.15625 to 0.15625
- attention: bfloat16 [128, 8], replicated, may hold values from -1 to 1
Outputs:
- node_update: bfloat16 [32, 64, 49, 128], P('dp', 'graph')
- grad_nodes: bfloat16 [32, 64, 49, 128], P('dp', 'graph')
- grad_w_zero: float32 [896, 896], P('graph', 'dp')
- grad_attention: float32 [128, 8], replicated
Inputs may be any that keep to these rules, and one draw needn't show every extreme that they name: Atoms 0 to atom_counts[b] - 1 of batch b are real; the first batch fills all 64 rows and the second holds the fewest allowed. `source`: below the batch's atom count; never equal to the slot's target. `target`: below the batch's atom count; never equal to the slot's source. `wigner`: entry [k, j, e] is zero unless reduced row k and coefficient j have the same degree l.
All inputs are finite; a program needn't handle non-finite values. No bound on the sum of `edge_counts` on one device may be relied on, other than what follows from the above.
Results may differ from a plain program's by a relative error of at most 0.039.
Values may be sent and summed in bfloat16 or wider, within the bound.
No kernel may reach another device: no remote copies, remote signals or barrier semaphores. Data moves between devices by JAX's collectives and lax.ppermute only.
A program may use at most 64 MiB of HBM per device.

v0:
```python
import functools

import jax
import jax.numpy as jnp
from jax import lax
from jax.experimental import pallas as pl
from jax.experimental.pallas import tpu as pltpu
from jax.sharding import Mesh, PartitionSpec as P

LMAX = 6
LANES = 128
DP = ("xh", "z", "core")
COLUMN_GROUP = ("xh", "z")
GRAPH = ("y", "xl")
precise = lax.Precision.HIGHEST
f32 = jnp.float32
bf16 = jnp.bfloat16


def half_dot(left, right):
    return jnp.dot(left, right, preferred_element_type=f32)


def full_dot(left, right):
    return jnp.dot(left, right, precision=precise, preferred_element_type=f32)


def gather(block, axes):
    count = lax.axis_size(axes)
    copies = jnp.broadcast_to(block[None], (count,) + block.shape)
    return lax.all_to_all(copies, axes, split_axis=0, concat_axis=0, tiled=True)


def exchange(blocks, axes):
    return lax.all_to_all(blocks, axes, split_axis=0, concat_axis=0, tiled=True)


ROW_DEGREE = (
    list(range(LMAX + 1)) + list(range(1, LMAX + 1)) * 2 + list(range(2, LMAX + 1)) * 2
)
ROWS_OF = [[k for k, d in enumerate(ROW_DEGREE) if d == l] for l in range(LMAX + 1)]
COEFS_OF = [list(range(l * l, (l + 1) * (l + 1))) for l in range(LMAX + 1)]
REDUCED = len(ROW_DEGREE)
COEF = (LMAX + 1) ** 2
ZERO = (0, LMAX + 1)
ONE = (LMAX + 1, LMAX)
TWO = (3 * LMAX + 1, LMAX - 1)
CHUNK = 32
VMEM = pl.BlockSpec(memory_space=pltpu.VMEM)
ANY = pl.BlockSpec(memory_space=pl.ANY)
PARAMS = pltpu.CompilerParams(vmem_limit_bytes=48 * 1024 * 1024)


def nt_dot(left, right):
    return lax.dot_general(left, right, (((1,), (1,)), ((), ())), preferred_element_type=f32)


def nt_full(left, right):
    return lax.dot_general(
        left, right, (((1,), (1,)), ((), ())), precision=precise, preferred_element_type=f32
    )


def hot_rows(ids, count):
    rows = lax.broadcasted_iota(jnp.int32, (count, ids.shape[1]), 0)
    return (rows == ids).astype(f32)


def widen(values, channels):
    heads, edges = values.shape
    wide = jnp.broadcast_to(values[:, None, :], (heads, channels // heads, edges))
    return wide.reshape(channels, edges)


def chunks(channels, body):
    def step(i, carry):
        body(pl.ds(pl.multiple_of(i * CHUNK, CHUNK), CHUNK))
        return carry

    lax.fori_loop(0, channels // CHUNK, step, 0)


def copy_weights(first, mine, other, held, sems):
    def go(low, high):
        one = pltpu.make_async_copy(low, held.at[0], sems.at[0])
        two = pltpu.make_async_copy(high, held.at[1], sems.at[1])
        one.start()
        two.start()
        one.wait()
        two.wait()

    @pl.when(first == 0)
    def _():
        go(mine, other)

    @pl.when(first != 0)
    def _():
        go(other, mine)


def map_tiles(held, place, tiles):
    half, at, rows = place
    parts = []
    for t in tiles:
        part = held[half, :, at + t * rows : at + (t + 1) * rows, :]
        parts.append(part.reshape(-1, LANES))
    return parts[0] if len(parts) == 1 else jnp.concatenate(parts, axis=1)


def pairs(count):
    return [tuple(range(i, min(i + 2, count))) for i in range(0, count, 2)]


def rotate_kernel(ids, nodes, cots, wigner, z, grad_edge, paired, wide):
    count, edges = nodes.shape[0], wigner.shape[2]
    channels = LANES
    target = hot_rows(ids[1:2, :], count)
    both = (target + hot_rows(ids[0:1, :], count)).astype(bf16)
    target = target.astype(bf16)
    wide[...] = wigner[...].astype(f32)
    for j in range(COEF):
        at = slice(j * channels, (j + 1) * channels)
        paired[j] = half_dot(nodes[:, at].T, both).astype(bf16).astype(f32)
        grad_edge[j] = half_dot(cots[:, at].T, target).astype(bf16)
    for l in range(LMAX + 1):
        for k in ROWS_OF[l]:
            acc = None
            for j in COEFS_OF[l]:
                term = wide[k, j : j + 1, :] * paired[j]
                acc = term if acc is None else acc + term
            z[:, k * channels : (k + 1) * channels] = acc.T.astype(bf16)


def forward_kernel(
    places,
    first,
    ids,
    z,
    wigner,
    grad_edge,
    attention_t,
    mine,
    other,
    message,
    stats,
    scalar,
    per_edge,
    held,
    y,
    wide,
    norm,
    msg,
    heads_acc,
    sems,
):
    channels, edges = LANES, wigner.shape[2]
    heads = attention_t.shape[0]
    count = stats.shape[1]
    copy_weights(first[0, 0], mine, other, held, sems)
    wide[...] = wigner[...].astype(f32)
    base, rows = ZERO
    left = z[:, : rows * channels]
    for tiles in pairs(rows):
        out = half_dot(left, map_tiles(held, places[0], tiles))
        for i, t in enumerate(tiles):
            turned = out[:, i * channels : (i + 1) * channels].T
            if t == 0:
                scalar[...] = turned
            y[t] = turned.astype(bf16).astype(f32)
    for (base, rows), real, imag in ((ONE, places[1], places[2]), (TWO, places[3], places[4])):
        plus = z[:, base * channels : (base + rows) * channels]
        minus = z[:, (base + rows) * channels : (base + 2 * rows) * channels]
        left = jnp.concatenate([plus, minus], axis=0)
        crossed = jnp.concatenate([-minus, plus], axis=0)
        for tiles in pairs(rows):
            out = half_dot(left, map_tiles(held, real, tiles))
            out = out + half_dot(crossed, map_tiles(held, imag, tiles))
            for i, t in enumerate(tiles):
                at = slice(i * channels, (i + 1) * channels)
                y[base + t] = out[:edges, at].T.astype(bf16).astype(f32)
                y[base + rows + t] = out[edges:, at].T.astype(bf16).astype(f32)
    value = scalar[...]
    gating = (value / (1.0 + jnp.exp(-value))).astype(bf16)
    logits = half_dot(attention_t[...], gating)
    weight = jnp.where(ids[2:3, :] > 0, jnp.exp(logits), 0.0)
    target = hot_rows(ids[1:2, :], count)
    own_sum = nt_full(weight, target)
    at_edges = full_dot(own_sum, target)
    own_norm = weight / jnp.where(at_edges > 0.0, at_edges, 1.0)
    norm[...] = widen(own_norm, channels)

    def body(at):
        own = norm[at, :]
        total = jnp.zeros((CHUNK, edges), f32)
        for l in range(LMAX + 1):
            for j in COEFS_OF[l]:
                acc = None
                for k in ROWS_OF[l]:
                    term = wide[k, j : j + 1, :] * y[k, at, :]
                    acc = term if acc is None else acc + term
                total = total + acc * grad_edge[j, at, :].astype(f32)
                msg[j, at, :] = (acc * own).astype(bf16)
        heads_acc[at, :] = total

    chunks(channels, body)
    grad_norm = jnp.sum(heads_acc[...].reshape(heads, channels // heads, edges), axis=1)
    own_shared = nt_full(own_norm * grad_norm, target)
    stats[:heads, :] = own_sum
    stats[heads:, :] = own_shared
    per_edge[:heads, :] = own_norm
    per_edge[heads:, :] = grad_norm
    low = target.astype(bf16)
    for j in range(COEF):
        message[:, j * channels : (j + 1) * channels] = nt_dot(low, msg[j]).astype(bf16)


def backward_kernel(
    ids, stats, every, scalar, per_edge, wigner, grad_edge, attention, attention_t, z,
    grad_conv, zero, wide, norm, grad, turned,
):
    channels, edges = LANES, wigner.shape[2]
    heads = attention_t.shape[0]
    count = stats.shape[1]
    wide[...] = wigner[...].astype(f32)
    total = jnp.sum(every[:, :heads, :], axis=0)
    total = jnp.where(total > 0.0, total, 1.0)
    shared = jnp.sum(every[:, :heads, :] / total[None] * every[:, heads:, :], axis=0)
    own_share = stats[:heads, :] / total
    target = hot_rows(ids[1:2, :], count)
    normalized = per_edge[:heads, :] * full_dot(own_share, target)
    grad_logit = normalized * (per_edge[heads:, :] - full_dot(shared, target))
    value = scalar[...]
    sigmoid = 1.0 / (1.0 + jnp.exp(-value))
    gating = (value / (1.0 + jnp.exp(-value))).astype(bf16).astype(f32)
    att = nt_full(grad_logit, gating)
    grad_gating = full_dot(attention[...].astype(f32), grad_logit)
    grad_scalar = grad_gating * sigmoid * (1.0 + value * (1.0 - sigmoid))
    norm[...] = widen(normalized, channels)

    def body(at):
        own = norm[at, :]
        for l in range(LMAX + 1):
            fields = [
                (grad_edge[j, at, :].astype(f32) * own).astype(bf16).astype(f32)
                for j in COEFS_OF[l]
            ]
            for k in ROWS_OF[l]:
                acc = None
                for j, field in zip(COEFS_OF[l], fields):
                    term = wide[k, j : j + 1, :] * field
                    acc = term if acc is None else acc + term
                grad[k, at, :] = acc

    chunks(channels, body)
    grad[0] = grad[0] + grad_scalar
    grad_conv[...] = grad[...].astype(bf16)
    depth = (LMAX + 1) * channels
    parts, share = zero.shape[1], depth // (2 * zero.shape[1])
    order_zero = grad_conv[: LMAX + 1].reshape(depth, edges)
    turned[:depth, :] = half_dot(order_zero, z[:, :depth])
    turned[depth:, :] = jnp.zeros((turned.shape[0] - depth, depth), f32)
    padded = zero.shape[2]
    tail_row = lax.broadcasted_iota(jnp.int32, (padded, depth), 0)
    first = jnp.concatenate([att[h : h + 1, :] for h in range(LMAX + 1)], axis=1)
    rest = [att[h : h + 1, :] for h in range(LMAX + 1, heads)]
    rest = jnp.concatenate(rest + [jnp.zeros((1, depth - len(rest) * channels), f32)], axis=1)
    for core in range(2):
        for part in range(parts):
            at = (2 * part + core) * share
            block = turned[at : at + padded, :]
            block = jnp.where(tail_row == share, first, block)
            block = jnp.where(tail_row == share + 1, rest, block)
            zero[core, part] = block.astype(bf16)


def scatter_kernel(places, first, ids, grad_conv, wigner, mine, other, grads, held, wide, dz, gp, sems):
    channels, edges = LANES, wigner.shape[2]
    count = grads.shape[0]
    copy_weights(first[0, 0], mine, other, held, sems)
    wide[...] = wigner[...].astype(f32)
    base, rows = ZERO
    acc = None
    for tiles in pairs(rows):
        right = grad_conv[tiles[0] : tiles[-1] + 1].reshape(-1, edges)
        term = half_dot(map_tiles(held, places[0], tiles), right)
        acc = term if acc is None else acc + term
    dz[:rows] = acc.astype(bf16).astype(f32).reshape(rows, channels, edges)
    for (base, rows), real, imag in ((ONE, places[1], places[2]), (TWO, places[3], places[4])):
        acc = None
        for tiles in pairs(rows):
            lo, hi = base + tiles[0], base + tiles[-1] + 1
            plus = grad_conv[lo:hi].reshape(-1, edges)
            minus = grad_conv[lo + rows : hi + rows].reshape(-1, edges)
            term = half_dot(map_tiles(held, real, tiles), jnp.concatenate([plus, minus], axis=1))
            term = term + half_dot(
                map_tiles(held, imag, tiles), jnp.concatenate([minus, -plus], axis=1)
            )
            acc = term if acc is None else acc + term
        acc = acc.astype(bf16).astype(f32)
        dz[base : base + rows] = acc[:, :edges].reshape(rows, channels, edges)
        dz[base + rows : base + 2 * rows] = acc[:, edges:].reshape(rows, channels, edges)

    def body(at):
        for l in range(LMAX + 1):
            for j in COEFS_OF[l]:
                acc = None
                for k in ROWS_OF[l]:
                    term = wide[k, j : j + 1, :] * dz[k, at, :]
                    acc = term if acc is None else acc + term
                gp[j, at, :] = acc.astype(bf16)

    chunks(channels, body)
    both = (hot_rows(ids[1:2, :], count) + hot_rows(ids[0:1, :], count)).astype(bf16)
    for j in range(COEF):
        grads[:, j * channels : (j + 1) * channels] = nt_dot(both, gp[j]).astype(bf16)


def per_channel(values, channels):
    rows, head_count = values.shape
    return jnp.broadcast_to(values[:, :, None], (rows, head_count, channels // head_count)).reshape(
        rows, channels
    )


def pad_to(block, rows, columns):
    return jnp.pad(block, ((0, rows - block.shape[0]), (0, columns - block.shape[1])))


def whole_lanes(count):
    return -(-count // LANES) * LANES


def column_tiles(block):
    rows, columns = block.shape
    tiles = block.reshape(rows, columns // LANES, LANES)
    return jnp.transpose(tiles, (1, 0, 2)).reshape(-1, LANES)


def gather_weights(shards):
    rows = [w.shape[0] for w in shards]
    columns = [w.shape[1] for w in shards]
    most = max(rows)
    packed = jnp.concatenate([pad_to(w, most, w.shape[1]) for w in shards], axis=1)
    packed = pad_to(packed, most, whole_lanes(packed.shape[1]))
    near = lax.all_gather(lax.all_gather(packed, "core"), "xl")
    blocks, at = [], 0
    for r, n in zip(rows, columns):
        piece = near[:, :, :r, at : at + n]
        blocks.append(jnp.transpose(piece, (0, 2, 1, 3)).reshape(2 * r, 2 * n))
        at += n
    first = lax.axis_index("core") == 0
    sets = ((0, 1), (2, 3, 4))
    lanes = whole_lanes(max(sum(2 * columns[i] for i in s) for s in sets))
    sent = [
        pad_to(
            jnp.concatenate([pad_to(blocks[i], 2 * most, 2 * columns[i]) for i in s], axis=1),
            2 * most,
            lanes,
        )
        for s in sets
    ]
    slabs = gather(jnp.where(first, sent[0], sent[1]), COLUMN_GROUP)
    whole = [2 * n * slabs.shape[0] for n in columns]
    tiled = []
    for s in sets:
        at, parts = 0, []
        for i in s:
            piece = slabs[:, : 2 * rows[i], at : at + 2 * columns[i]]
            at += 2 * columns[i]
            parts.append(
                column_tiles(jnp.transpose(piece, (1, 0, 2)).reshape(2 * rows[i], whole[i]))
            )
        tiled.append(jnp.concatenate(parts, axis=0))
    depth = max(t.shape[0] for t in tiled)
    tiled = [pad_to(t, depth, LANES) for t in tiled]
    half = lax.all_gather(jnp.where(first, tiled[0], tiled[1]), "y")
    places = [None] * len(shards)
    for half_index, s in enumerate(sets):
        at = 0
        for i in s:
            places[i] = (half_index, at, 2 * rows[i])
            at += whole[i] // LANES * 2 * rows[i]
    return half, places, slabs


def on_device(
    embeddings,
    atom_counts,
    edge_counts,
    source,
    target,
    wigner,
    cotangent,
    w_zero,
    w_one_real,
    w_one_imag,
    w_two_real,
    w_two_imag,
    attention,
):
    half, places, slabs = gather_weights((w_zero, w_one_real, w_one_imag, w_two_real, w_two_imag))
    row_count = embeddings.shape[1]
    harmonics = embeddings.shape[2]
    channels = embeddings.shape[3]
    width = harmonics * channels
    edge_rows = source.shape[1]
    head_count = attention.shape[1]
    group = lax.axis_size(GRAPH)
    all_nodes = row_count * group
    rotation = wigner[0]
    in_use = (lax.iota(jnp.int32, edge_rows) < edge_counts[0, 0]).astype(jnp.int32)
    ids = jnp.stack([source[0], target[0], in_use] + [jnp.zeros_like(in_use)] * 5)
    attention_t = attention.T
    core = lax.axis_index("core")
    first = core.astype(jnp.int32).reshape(1, 1)
    own_first = lax.axis_index(GRAPH) * row_count
    present = ((own_first + lax.iota(jnp.int32, row_count)) < atom_counts[0])[:, None]
    cot_rows = jnp.where(present, cotangent[0].reshape(row_count, width), 0.0).astype(bf16)
    node_rows = embeddings[0].reshape(row_count, width)
    node_rows, cot_rows, slabs = lax.optimization_barrier((node_rows, cot_rows, slabs))
    nodes = gather(node_rows, GRAPH).reshape(all_nodes, width)
    cot_nodes = gather(cot_rows, GRAPH).reshape(all_nodes, width)

    smem = pl.BlockSpec(memory_space=pltpu.SMEM)
    field = (channels, edge_rows)
    wide = pltpu.VMEM(rotation.shape, f32)
    z, grad_edge = pl.pallas_call(
        rotate_kernel,
        out_shape=(
            jax.ShapeDtypeStruct((edge_rows, REDUCED * channels), bf16),
            jax.ShapeDtypeStruct((COEF,) + field, bf16),
        ),
        in_specs=[VMEM] * 4,
        out_specs=[VMEM] * 2,
        scratch_shapes=[pltpu.VMEM((COEF,) + field, f32), wide],
        compiler_params=PARAMS,
    )(ids, nodes, cot_nodes, rotation)
    half, z, grad_edge = lax.optimization_barrier((half, z, grad_edge))
    other = lax.ppermute(half, "core", [(0, 1), (1, 0)])
    held = pltpu.VMEM((2,) + half.shape, bf16)
    copies = pltpu.SemaphoreType.DMA((2,))

    message_sums, stats, scalar, per_edge = pl.pallas_call(
        functools.partial(forward_kernel, places),
        out_shape=(
            jax.ShapeDtypeStruct((all_nodes, width), bf16),
            jax.ShapeDtypeStruct((2 * head_count, all_nodes), f32),
            jax.ShapeDtypeStruct(field, f32),
            jax.ShapeDtypeStruct((2 * head_count, edge_rows), f32),
        ),
        in_specs=[smem] + [VMEM] * 5 + [ANY] * 2,
        out_specs=[VMEM] * 4,
        scratch_shapes=[
            held,
            pltpu.VMEM((REDUCED,) + field, f32),
            wide,
            pltpu.VMEM(field, f32),
            pltpu.VMEM((COEF,) + field, bf16),
            pltpu.VMEM(field, f32),
            copies,
        ],
        compiler_params=PARAMS,
    )(first, ids, z, rotation, grad_edge, attention_t, half, other)
    every = gather(stats, GRAPH)
    message_parts = exchange(message_sums.reshape(group, row_count, width), GRAPH)

    columns = lax.axis_size(COLUMN_GROUP)
    depth = channels * (LMAX + 1)
    share = depth // (2 * columns)
    padded = -(-(share + 2) // 16) * 16
    grad_conv, zero = pl.pallas_call(
        backward_kernel,
        out_shape=(
            jax.ShapeDtypeStruct((REDUCED,) + field, bf16),
            jax.ShapeDtypeStruct((2, columns, padded, depth), bf16),
        ),
        in_specs=[VMEM] * 10,
        out_specs=[VMEM] * 2,
        scratch_shapes=[
            wide,
            pltpu.VMEM(field, f32),
            pltpu.VMEM((REDUCED,) + field, f32),
            pltpu.VMEM((depth + padded, depth), f32),
        ],
        compiler_params=PARAMS,
    )(ids, stats, every, scalar, per_edge, rotation, grad_edge, attention, attention_t, z)

    mine = jnp.where(core == 0, zero[0], zero[1])
    theirs = jnp.where(core == 0, zero[1], zero[0])
    theirs = lax.ppermute(theirs, "core", [(0, 1), (1, 0)])
    mine = (mine.astype(f32) + theirs.astype(f32)).astype(bf16)
    zero_parts = exchange(mine, COLUMN_GROUP)
    zero_sum = jnp.sum(zero_parts.astype(f32), axis=0)
    att_flat = zero_sum[share : share + 2].reshape(-1)[: head_count * channels]
    zero_send = jnp.transpose(zero_sum[:share].reshape(share, group, -1), (1, 0, 2))
    lanes = whole_lanes(zero_send.shape[2])
    zero_send = jnp.pad(zero_send, ((0, 0), (0, 0), (0, lanes - zero_send.shape[2])))
    att_rows = att_flat.size // LANES
    att_send = jnp.broadcast_to(att_flat.reshape(1, att_rows, LANES), (group, att_rows, LANES))
    att_send = jnp.pad(att_send, ((0, 0), (0, 0), (0, lanes - LANES)))

    grad_blocks = pl.pallas_call(
        functools.partial(scatter_kernel, places),
        out_shape=jax.ShapeDtypeStruct((all_nodes, width), bf16),
        in_specs=[smem] + [VMEM] * 3 + [ANY] * 2,
        out_specs=VMEM,
        scratch_shapes=[
            held,
            wide,
            pltpu.VMEM((REDUCED,) + field, f32),
            pltpu.VMEM((COEF,) + field, bf16),
            copies,
        ],
        compiler_params=PARAMS,
    )(first, ids, grad_conv, rotation, half, other)
    grad_parts = exchange(grad_blocks.reshape(group, row_count, width), GRAPH)
    grad_nodes = jnp.sum(grad_parts.astype(f32), axis=0).astype(bf16)

    last = exchange(jnp.concatenate([zero_send, att_send], axis=1), GRAPH)
    last = jnp.sum(last, axis=0) * (1.0 / (2 * columns))
    grad_zero = last[:share, : depth // group].T
    grad_att = last[share:, :LANES].reshape(head_count, channels).T

    sums = lax.dynamic_slice_in_dim(every[:, :head_count], own_first, row_count, axis=2)
    sums = jnp.transpose(sums, (0, 2, 1))
    total = jnp.sum(sums, axis=0)
    own_shares = sums / jnp.where(total > 0.0, total, 1.0)[None]
    wide = per_channel(own_shares.reshape(-1, head_count), channels)
    wide = wide.reshape(group, row_count, 1, channels)
    parts = message_parts.reshape(group, row_count, harmonics, channels).astype(f32)
    summed = jnp.sum(parts * wide, axis=0)
    update = jnp.where(present[:, :, None], summed, 0.0).astype(bf16)

    shape = (1, row_count, harmonics, channels)
    return (update.reshape(shape), grad_nodes.reshape(shape), grad_zero, grad_att)


def solution(mesh):
    columns, group = mesh.shape["dp"], mesh.shape["graph"]
    devices = mesh.devices.reshape(2, columns // 4, 2, group // 2, 2)
    fine = Mesh(devices, DP + GRAPH)
    in_specs = (
        P(DP, GRAPH, None, None),
        P(DP),
        P(DP, GRAPH),
        P(DP, GRAPH),
        P(DP, GRAPH),
        P(DP, None, None, GRAPH),
        P(DP, GRAPH, None, None),
        P(GRAPH, DP),
        P(GRAPH, DP),
        P(GRAPH, DP),
        P(GRAPH, DP),
        P(GRAPH, DP),
        P(),
    )
    out_specs = (P(DP, GRAPH, None, None), P(DP, GRAPH, None, None), P(GRAPH, DP), P())
    return jax.shard_map(
        on_device, mesh=fine, in_specs=in_specs, out_specs=out_specs, check_vma=False
    )
```

profile of v0, /device:TPU:1, one launch (start us, length us, event | category | flops | bytes accessed | tf_op | source)
XLA Modules:
  0.0 261.0 jit_solution(17847344381599497271)
XLA Ops:
  11.3 8.4 %all-gather = bf16[112,128]{1,0:T(8,128)(2,1)S(1)} all-gather(bf16[56,128]{1,0:T(8,128)(2,1)S(1)} %pad.48), channel_id=2, replica_groups=mesh['xh'=2,'z'=8,'core'=2,'y'=8,'xl'=2] {'core'}, dimensions={0}, use_global_device_ids=true | all-gather | bytes 43008 | tf_op jit(solution)/shard_map/all_gather | solution.py:345
  19.7 3.4 %all-gather.1 = bf16[4,56,128]{2,1,0:T(8,128)(2,1)S(1)} all-gather(bf16[2,56,128]{2,1,0:T(8,128)(2,1)S(1)} %bitcast.110), channel_id=3, replica_groups=mesh['xh'=2,'z'=8,'core'=2,'y'=8,'xl'=2] {'xl'}, dimensions={0}, use_global_device_ids=true | all-gather | bytes 86016 | tf_op jit(solution)/shard_map/all_gather | solution.py:345
  24.5 20.3 %all_to_all.40 = bf16[16,112,128]{2,1,0:T(8,128)(2,1)S(1)} all-to-all(bf16[16,112,128]{2,1,0:T(8,128)(2,1)S(1)} %broadcast_in_dim.67), channel_id=1, replica_groups=mesh['xh'=2,'z'=8,'core'=2,'y'=8,'xl'=2] {'xh','z'}, dimensions={0} | all-to-all | bytes 917504 | tf_op jit(solution)/shard_map/all_to_all | solution.py:31
  48.8 31.1 %all_to_all.41 = bf16[16,4,6272]{2,1,0:T(4,128)(2,1)S(1)} all-to-all(bf16[16,4,6272]{2,1,0:T(4,128)(2,1)S(1)} %broadcast_in_dim.70), channel_id=1, replica_groups=mesh['xh'=2,'z'=8,'core'=2,'y'=8,'xl'=2] {'y','xl'}, dimensions={0} | all-to-all | bytes 1605632 | tf_op jit(solution)/shard_map/all_to_all | solution.py:31
  81.1 4.4 %all-to-all-start.2 = ((bf16[16,4,6272]{2,1,0:T(4,128)(2,1)}), bf16[16,4,6272]{2,1,0:T(4,128)(2,1)S(1)}, u32[]{:S(2)}, u32[]{:S(2)}) async-start(bf16[16,4,6272]{2,1,0:T(4,128)(2,1)} %broadcast_in_dim.71), calls=%async_computation.2 | async-start | bytes 1605632 | tf_op jit(solution)/shard_map/all_to_all | solution.py:31
  87.4 24.9 %all-to-all-done.2 = bf16[16,4,6272]{2,1,0:T(4,128)(2,1)S(1)} async-done(((bf16[16,4,6272]{2,1,0:T(4,128)(2,1)}), bf16[16,4,6272]{2,1,0:T(4,128)(2,1)S(1)}, u32[]{:S(2)}, u32[]{:S(2)}) %all-to-all-start.2) | async-done | bytes 802848 | tf_op jit(solution)/shard_map/all_to_all | solution.py:31
  115.7 1.9 shard_map.156
  117.6 3.5 %all-gather.5.cloned.1.call-done = bf16[11008,128]{1,0:T(8,128)(2,1)} async-done(((bf16[1376,128]{1,0:T(8,128)(2,1)}), bf16[11008,128]{1,0:T(8,128)(2,1)}) %all-gather.5.cloned.1.call-update) | async-done | bytes 2818064 | tf_op jit(solution)/shard_map/all_gather | solution.py:376
  121.1 7.6 %collective-permute-start = (bf16[8,1376,128]{2,1,0:T(8,128)(2,1)}, bf16[8,1376,128]{2,1,0:T(8,128)(2,1)S(1)}, u32[]{:S(2)}, u32[]{:S(2)}) collective-permute-start(bf16[8,1376,128]{2,1,0:T(8,128)(2,1)} %bitcast.85), channel_id=1, source_target_pairs={{0,16},{16,0},{1,17},{17,1},{2,18},{18,2},{3,19},{19,3},{4,20},{20... | collective-permute-start | bytes 8454152 | tf_op jit(solution)/shard_map/ppermute | solution.py:439
  128.7 5.0 %collective-permute-done.other = bf16[8,1376,128]{2,1,0:T(8,128)(2,1)S(1)} collective-permute-done((bf16[8,1376,128]{2,1,0:T(8,128)(2,1)}, bf16[8,1376,128]{2,1,0:T(8,128)(2,1)S(1)}, u32[]{:S(2)}, u32[]{:S(2)}) %collective-permute-start) | collective-permute-done | bytes 2818080 | tf_op jit(solution)/shard_map/ppermute | solution.py:439
  133.7 1.6 copy-done.8
  135.2 7.2 %shard_map.157 = (bf16[64,6272]{1,0:T(8,128)(2,1)S(1)}, f32[16,64]{1,0:T(8,128)S(1)}, f32[128,128]{1,0:T(8,128)S(1)}, f32[16,128]{1,0:T(8,128)S(1)}) custom-call(s32[1,1]{1,0:T(1,128)} %bitcast.1.first, s32[8,128]{1,0:T(8,128)S(1)} %stack.8.ids, bf16[128,3712]{1,0:T(8,128)(2,1)S(1)} %get-tuple-element.21.z, bf16[29,49,128]{2,1,0:T(8,128)(2,1)S(1)} %bitcast.89, ...), custom_call_target="tpu_custom_call" | custom-call | tf_op jit(solution)/shard_map/pallas_call | solution.py:443
  144.1 3.5 %all-to-all-start.4 = ((f32[16,1,1024]{2,1,0:T(1,128)}), f32[16,1,1024]{2,1,0:T(1,128)S(1)}, u32[]{:S(2)}, u32[]{:S(2)}) async-start(f32[16,1,1024]{2,1,0:T(1,128)} %reshape.139), calls=%async_computation.4 | async-start | bytes 131072 | tf_op jit(solution)/shard_map/all_to_all | solution.py:31
  147.6 2.5 reshape.131
  150.1 5.4 %all-to-all-done.4 = f32[16,1,1024]{2,1,0:T(1,128)S(1)} async-done(((f32[16,1,1024]{2,1,0:T(1,128)}), f32[16,1,1024]{2,1,0:T(1,128)S(1)}, u32[]{:S(2)}, u32[]{:S(2)}) %all-to-all-start.4) | async-done | bytes 65568 | tf_op jit(solution)/shard_map/all_to_all | solution.py:31
  155.6 4.5 %all-to-all-start.3 = ((bf16[16,4,6272]{2,1,0:T(4,128)(2,1)}), bf16[16,4,6272]{2,1,0:T(4,128)(2,1)}, u32[]{:S(2)}, u32[]{:S(2)}) async-start(bf16[16,4,6272]{2,1,0:T(4,128)(2,1)} %reshape.131), calls=%async_computation.3 | async-start | bytes 1605632 | tf_op jit(solution)/shard_map/all_to_all | solution.py:35
  161.6 2.7 %shard_map.158 = (bf16[29,128,128]{2,1,0:T(8,128)(2,1)S(1)}, bf16[2,16,32,896]{3,2,1,0:T(8,128)(2,1)S(1)}) custom-call(s32[8,128]{1,0:T(8,128)S(1)} %stack.8.ids, f32[16,64]{1,0:T(8,128)S(1)} %get-tuple-element.25.stats, f32[16,16,64]{2,1,0:T(8,128)S(1)} %reshape.140.every, f32[128,128]{1,0:T(8,128)S(1)} %get-tuple-element.26.scalar, ...), custom_call_target="tpu_custom_call" | custom-call | tf_op jit(solution)/shard_map/pallas_call | solution.py:471
  164.4 3.5 %collective-permute-start.1 = (bf16[16,32,896]{2,1,0:T(8,128)(2,1)S(1)}, bf16[16,32,896]{2,1,0:T(8,128)(2,1)S(1)}, u32[]{:S(2)}, u32[]{:S(2)}) collective-permute-start(bf16[16,32,896]{2,1,0:T(8,128)(2,1)S(1)} %select_bitcast_fusion), channel_id=1, source_target_pairs={{0,16},{16,0},{1,17},{17,1},{2,18},{18,2},{3,19},{19,3},{4,20},{20... | collective-permute-start | bytes 2752520 | tf_op jit(solution)/shard_map/ppermute | solution.py:490
  167.8 2.1 collective-permute-done.1
  169.9 1.3 fusion
  171.2 8.7 %all-to-all-done.3 = bf16[16,4,6272]{2,1,0:T(4,128)(2,1)} async-done(((bf16[16,4,6272]{2,1,0:T(4,128)(2,1)}), bf16[16,4,6272]{2,1,0:T(4,128)(2,1)}, u32[]{:S(2)}, u32[]{:S(2)}) %all-to-all-start.3) | async-done | bytes 802848 | tf_op jit(solution)/shard_map/all_to_all | solution.py:35
  179.9 7.1 %all-to-all-start.6 = ((bf16[16,32,896]{2,1,0:T(8,128)(2,1)}), bf16[16,32,896]{2,1,0:T(8,128)(2,1)}, u32[]{:S(2)}, u32[]{:S(2)}) async-start(bf16[16,32,896]{2,1,0:T(8,128)(2,1)} %fusion), calls=%async_computation.6 | async-start | bytes 1835008 | tf_op jit(solution)/shard_map/all_to_all | solution.py:35
  187.0 1.2 copy-done.5
  188.2 6.0 %shard_map.159 = bf16[64,6272]{1,0:T(8,128)(2,1)S(1)} custom-call(s32[1,1]{1,0:T(1,128)} %bitcast.1.first, s32[8,128]{1,0:T(8,128)S(1)} %stack.8.ids, bf16[29,128,128]{2,1,0:T(8,128)(2,1)S(1)} %copy-done.5, bf16[29,49,128]{2,1,0:T(8,128)(2,1)S(1)} %bitcast.91, bf16[8,1376,128]{2,1,0:T(8,128)(2,1)S(1)} %bitcast.87, bf16[8,1376,128]{2,1,0:T(8,128)(2,1)} %copy-done.8), custom_call_target="tpu_custom_call" | custom-call | tf_op jit(solution)/shard_map/pallas_call | solution.py:502
  195.1 2.4 reshape.132
  197.5 8.9 %all-to-all-done.6 = bf16[16,32,896]{2,1,0:T(8,128)(2,1)} async-done(((bf16[16,32,896]{2,1,0:T(8,128)(2,1)}), bf16[16,32,896]{2,1,0:T(8,128)(2,1)}, u32[]{:S(2)}, u32[]{:S(2)}) %all-to-all-start.6) | async-done | bytes 917536 | tf_op jit(solution)/shard_map/all_to_all | solution.py:35
  206.5 10.1 %all-to-all-start.5 = ((bf16[16,4,6272]{2,1,0:T(4,128)(2,1)}), bf16[16,4,6272]{2,1,0:T(4,128)(2,1)S(1)}, u32[]{:S(2)}, u32[]{:S(2)}) async-start(bf16[16,4,6272]{2,1,0:T(4,128)(2,1)} %reshape.132), calls=%async_computation.5 | async-start | bytes 1605632 | tf_op jit(solution)/shard_map/all_to_all | solution.py:35
  216.7 1.3 convert_reduce_fusion
  219.1 17.4 %all-to-all-done.5 = bf16[16,4,6272]{2,1,0:T(4,128)(2,1)S(1)} async-done(((bf16[16,4,6272]{2,1,0:T(4,128)(2,1)}), bf16[16,4,6272]{2,1,0:T(4,128)(2,1)S(1)}, u32[]{:S(2)}, u32[]{:S(2)}) %all-to-all-start.5) | async-done | bytes 802848 | tf_op jit(solution)/shard_map/all_to_all | solution.py:35
  236.5 5.0 %all-to-all-start.7 = ((f32[16,36,128]{2,1,0:T(8,128)}), f32[16,36,128]{2,1,0:T(8,128)}, u32[]{:S(2)}, u32[]{:S(2)}) async-start(f32[16,36,128]{2,1,0:T(8,128)} %copy.106), calls=%async_computation.7 | async-start | bytes 655360 | tf_op jit(solution)/shard_map/all_to_all | solution.py:35
  242.4 1.6 multiply_reduce_fusion
  245.7 6.3 %all-to-all-done.7 = f32[16,36,128]{2,1,0:T(8,128)} async-done(((f32[16,36,128]{2,1,0:T(8,128)}), f32[16,36,128]{2,1,0:T(8,128)}, u32[]{:S(2)}, u32[]{:S(2)}) %all-to-all-start.7) | async-done | bytes 294944 | tf_op jit(solution)/shard_map/all_to_all | solution.py:35
  (114 shorter events, 24.6 us)
Async XLA Ops:
  7.2 113.9 %all-gather.5.cloned.1.call-start = ((), (), s32[]{:S(2)}) async-start(), calls=%async_computation.8 | async-start | bytes 3170304 | tf_op jit(solution)/shard_map/all_gather | solution.py:376
  46.4 2.1 copy-start.12
  46.5 2.1 copy-start.13
  48.8 36.6 %copy-start.11 = (bf16[1,29,49,128]{3,1,2,0:T(8,128)(2,1)S(1)}, bf16[1,29,49,128]{3,1,2,0:T(8,128)(2,1)}, u32[]{:S(2)}) copy-start(bf16[1,29,49,128]{3,1,2,0:T(8,128)(2,1)} %param.18) | copy-start | bytes 1091332
  79.9 6.3 %copy-start.14 = (s32[1,128]{1,0:T(1,128)S(1)}, s32[1,128]{1,0:T(1,128)}, u32[]{:S(2)}) copy-start(s32[1,128]{1,0:T(1,128)} %param.16) | copy-start | bytes 1540
  79.9 6.3 %copy-start.15 = (s32[1,128]{1,0:T(1,128)S(1)}, s32[1,128]{1,0:T(1,128)}, u32[]{:S(2)}) copy-start(s32[1,128]{1,0:T(1,128)} %param.17) | copy-start | bytes 1540
  81.1 31.2 %all-to-all-start.2 = ((bf16[16,4,6272]{2,1,0:T(4,128)(2,1)}), bf16[16,4,6272]{2,1,0:T(4,128)(2,1)S(1)}, u32[]{:S(2)}, u32[]{:S(2)}) async-start(bf16[16,4,6272]{2,1,0:T(4,128)(2,1)} %broadcast_in_dim.71), calls=%async_computation.2 | async-start | bytes 1605632 | tf_op jit(solution)/shard_map/all_to_all | solution.py:31
  87.4 47.9 %copy-start.7 = (bf16[128,8]{0,1:T(8,128)(2,1)S(1)}, bf16[128,8]{0,1:T(8,128)(2,1)}, u32[]{:S(2)}) copy-start(bf16[128,8]{0,1:T(8,128)(2,1)} %param.25) | copy-start | bytes 6148
  113.4 1.2 copy-start.2
  114.5 1.1 copy-start.3
  121.1 12.6 %collective-permute-start = (bf16[8,1376,128]{2,1,0:T(8,128)(2,1)}, bf16[8,1376,128]{2,1,0:T(8,128)(2,1)S(1)}, u32[]{:S(2)}, u32[]{:S(2)}) collective-permute-start(bf16[8,1376,128]{2,1,0:T(8,128)(2,1)} %bitcast.85), channel_id=1, source_target_pairs={{0,16},{16,0},{1,17},{17,1},{2,18},{18,2},{3,19},{19,3},{4,20},{20... | collective-permute-start | bytes 8454152 | tf_op jit(solution)/shard_map/ppermute | solution.py:439
  133.7 1.6 copy-start.8
  142.5 0.9 copy-start.6
  144.1 11.4 %all-to-all-start.4 = ((f32[16,1,1024]{2,1,0:T(1,128)}), f32[16,1,1024]{2,1,0:T(1,128)S(1)}, u32[]{:S(2)}, u32[]{:S(2)}) async-start(f32[16,1,1024]{2,1,0:T(1,128)} %reshape.139), calls=%async_computation.4 | async-start | bytes 131072 | tf_op jit(solution)/shard_map/all_to_all | solution.py:31
  155.6 24.3 %all-to-all-start.3 = ((bf16[16,4,6272]{2,1,0:T(4,128)(2,1)}), bf16[16,4,6272]{2,1,0:T(4,128)(2,1)}, u32[]{:S(2)}, u32[]{:S(2)}) async-start(bf16[16,4,6272]{2,1,0:T(4,128)(2,1)} %reshape.131), calls=%async_computation.3 | async-start | bytes 1605632 | tf_op jit(solution)/shard_map/all_to_all | solution.py:35
  164.2 3.6 %copy-start.4 = (bf16[29,128,128]{2,1,0:T(8,128)(2,1)}, bf16[29,128,128]{2,1,0:T(8,128)(2,1)S(1)}, u32[]{:S(2)}) copy-start(bf16[29,128,128]{2,1,0:T(8,128)(2,1)S(1)} %get-tuple-element.28.grad_conv) | copy-start | bytes 2850820
  164.4 5.6 %collective-permute-start.1 = (bf16[16,32,896]{2,1,0:T(8,128)(2,1)S(1)}, bf16[16,32,896]{2,1,0:T(8,128)(2,1)S(1)}, u32[]{:S(2)}, u32[]{:S(2)}) collective-permute-start(bf16[16,32,896]{2,1,0:T(8,128)(2,1)S(1)} %select_bitcast_fusion), channel_id=1, source_target_pairs={{0,16},{16,0},{1,17},{17,1},{2,18},{18,2},{3,19},{19,3},{4,20},{20... | collective-permute-start | bytes 2752520 | tf_op jit(solution)/shard_map/ppermute | solution.py:490
  169.9 17.1 %copy-start = (bf16[11008,128]{1,0:T(8,128)(2,1)S(1)}, bf16[11008,128]{1,0:T(8,128)(2,1)}, u32[]{:S(2)}) copy-start(bf16[11008,128]{1,0:T(8,128)(2,1)} %all-gather.5.cloned.1.call-done) | copy-start | bytes 8454148
  179.9 26.5 %all-to-all-start.6 = ((bf16[16,32,896]{2,1,0:T(8,128)(2,1)}), bf16[16,32,896]{2,1,0:T(8,128)(2,1)}, u32[]{:S(2)}, u32[]{:S(2)}) async-start(bf16[16,32,896]{2,1,0:T(8,128)(2,1)} %fusion), calls=%async_computation.6 | async-start | bytes 1835008 | tf_op jit(solution)/shard_map/all_to_all | solution.py:35
  187.0 1.2 copy-start.5
  194.2 0.9 copy-start.1
  206.5 30.0 %all-to-all-start.5 = ((bf16[16,4,6272]{2,1,0:T(4,128)(2,1)}), bf16[16,4,6272]{2,1,0:T(4,128)(2,1)S(1)}, u32[]{:S(2)}, u32[]{:S(2)}) async-start(bf16[16,4,6272]{2,1,0:T(4,128)(2,1)} %reshape.132), calls=%async_computation.5 | async-start | bytes 1605632 | tf_op jit(solution)/shard_map/all_to_all | solution.py:35
  236.5 5.6 %copy-start.9 = (bf16[16,4,6272]{2,1,0:T(4,128)(2,1)}, bf16[16,4,6272]{2,1,0:T(4,128)(2,1)S(1)}, u32[]{:S(2)}) copy-start(bf16[16,4,6272]{2,1,0:T(4,128)(2,1)S(1)} %all-to-all-done.5) | copy-start | bytes 2408452
  236.5 15.5 %all-to-all-start.7 = ((f32[16,36,128]{2,1,0:T(8,128)}), f32[16,36,128]{2,1,0:T(8,128)}, u32[]{:S(2)}, u32[]{:S(2)}) async-start(f32[16,36,128]{2,1,0:T(8,128)} %copy.106), calls=%async_computation.7 | async-start | bytes 655360 | tf_op jit(solution)/shard_map/all_to_all | solution.py:35
  242.4 2.3 copy-start.10
Sparse Core Ops, SparseCore 0:
  47.9 73.0 all-gather.4
where the time goes:
time: 264 us; the launch traced here: 261 us
  waiting for transfers between devices  82.1 us (31%)
  blocking collectives  63.2 us (24%)
  starting transfers between devices  45.7 us (17%)
  local copies, waits for them, and re-layouts  27.5 us (10%)
  Pallas kernels  17.8 us (7%)
  between operations  15.9 us (6%)
  other arithmetic  8.91 us (3%)
    all_to_all x2, blocking collectives, gather(): return lax.all_to_all(copies, axes, split_axis=0, concat_axis=0, tiled=True)  51.4 us
    all_to_all x4, waiting for transfers between devices, exchange(): return lax.all_to_all(blocks, axes, split_axis=0, concat_axis=0, tiled=True)  41.3 us
    all_to_all x2, waiting for transfers between devices, gather(): return lax.all_to_all(copies, axes, split_axis=0, concat_axis=0, tiled=True)  30.3 us
    all_to_all x4, starting transfers between devices, exchange(): return lax.all_to_all(blocks, axes, split_axis=0, concat_axis=0, tiled=True)  26.7 us
    unnamed x46, local copies, waits for them, and re-layouts  12.5 us
    all_gather x2, blocking collectives, gather_weights(): near = lax.all_gather(lax.all_gather(packed, 'core'), 'xl')  11.8 us
    all_to_all x2, starting transfers between devices, gather(): return lax.all_to_all(copies, axes, split_axis=0, concat_axis=0, tiled=True)  7.86 us
    ppermute x1, starting transfers between devices, on_device(): other = lax.ppermute(half, 'core', [(0, 1), (1, 0)])  7.6 us
  transfers between devices with their start and end apart: 9, of which 9 were waited for; matrix products, arithmetic and copies ran while one was open for 7% of the time, Pallas kernels for 4%

commit v1 on v0

v1 whole, which is shorter than its diff:
```python
import functools

import jax
import jax.numpy as jnp
from jax import lax
from jax.experimental import pallas as pl
from jax.experimental.pallas import tpu as pltpu
from jax.sharding import Mesh, PartitionSpec as P

LMAX = 6
LANES = 128
DP = ("xh", "z", "core")
COLUMN_GROUP = ("xh", "z")
ROW_GROUP = ("xh", "y", "xl")
GRAPH = ("y", "xl")
precise = lax.Precision.HIGHEST
f32 = jnp.float32
bf16 = jnp.bfloat16


def half_dot(left, right):
    return jnp.dot(left, right, preferred_element_type=f32)


def full_dot(left, right):
    return jnp.dot(left, right, precision=precise, preferred_element_type=f32)


def gather(block, axes):
    count = lax.axis_size(axes)
    copies = jnp.broadcast_to(block[None], (count,) + block.shape)
    return lax.all_to_all(copies, axes, split_axis=0, concat_axis=0, tiled=True)


def exchange(blocks, axes):
    return lax.all_to_all(blocks, axes, split_axis=0, concat_axis=0, tiled=True)


ROW_DEGREE = (
    list(range(LMAX + 1)) + list(range(1, LMAX + 1)) * 2 + list(range(2, LMAX + 1)) * 2
)
ROWS_OF = [[k for k, d in enumerate(ROW_DEGREE) if d == l] for l in range(LMAX + 1)]
COEFS_OF = [list(range(l * l, (l + 1) * (l + 1))) for l in range(LMAX + 1)]
REDUCED = len(ROW_DEGREE)
COEF = (LMAX + 1) ** 2
ZERO = (0, LMAX + 1)
ONE = (LMAX + 1, LMAX)
TWO = (3 * LMAX + 1, LMAX - 1)
CHUNK = 32
VMEM = pl.BlockSpec(memory_space=pltpu.VMEM)
ANY = pl.BlockSpec(memory_space=pl.ANY)
PARAMS = pltpu.CompilerParams(vmem_limit_bytes=48 * 1024 * 1024)


def nt_dot(left, right):
    return lax.dot_general(left, right, (((1,), (1,)), ((), ())), preferred_element_type=f32)


def nt_full(left, right):
    return lax.dot_general(
        left, right, (((1,), (1,)), ((), ())), precision=precise, preferred_element_type=f32
    )


def hot_rows(ids, count):
    rows = lax.broadcasted_iota(jnp.int32, (count, ids.shape[1]), 0)
    return (rows == ids).astype(f32)


def widen(values, channels):
    heads, edges = values.shape
    wide = jnp.broadcast_to(values[:, None, :], (heads, channels // heads, edges))
    return wide.reshape(channels, edges)


def chunks(channels, body):
    def step(i, carry):
        body(pl.multiple_of(i * CHUNK, CHUNK))
        return carry

    lax.fori_loop(0, channels // CHUNK, step, 0)


def rows_at(k, start):
    return pl.ds(pl.multiple_of(k * LANES + start, CHUNK), CHUNK)


def copy_weights(first, mine, other, held, sems):
    def go(low, high):
        one = pltpu.make_async_copy(low, held.at[0], sems.at[0])
        two = pltpu.make_async_copy(high, held.at[1], sems.at[1])
        one.start()
        two.start()
        one.wait()
        two.wait()

    @pl.when(first == 0)
    def _():
        go(mine, other)

    @pl.when(first != 0)
    def _():
        go(other, mine)


def map_tiles(held, place, tiles):
    half, at, rows = place
    parts = []
    for t in tiles:
        part = held[half, :, at + t * rows : at + (t + 1) * rows, :]
        parts.append(part.reshape(-1, LANES))
    return parts[0] if len(parts) == 1 else jnp.concatenate(parts, axis=1)


def pairs(count):
    return [tuple(range(i, min(i + 2, count))) for i in range(0, count, 2)]


def spread(blocks, held, rows, base, out):
    zs = held.shape[1]
    size = rows // 2
    for z in range(zs):
        for xh in range(2):
            to = base + (xh * zs + z) * size
            at = (z * 2 + xh) * size
            out[to : to + size, :] = blocks[at : at + size, :]


def by_owner(target, turned, out, group):
    channels = turned.shape[1]
    own = target.shape[0] // group
    per = 16 // own
    for first in range(0, COEF, per):
        parts = []
        for j in range(first, first + per):
            if j < COEF:
                part = nt_dot(target, turned[j])
            else:
                part = jnp.zeros((target.shape[0], channels), f32)
            parts.append(part.reshape(group, 1, own, channels))
        block = jnp.concatenate(parts, axis=1).reshape(group, 16, channels)
        out[:, first * own : first * own + 16, :] = block.astype(bf16)


def rotate_kernel(ids, nodes, wigner, z, grad_edge, paired, wide):
    count, edges = nodes.shape[0], wigner.shape[2]
    channels = LANES
    target = hot_rows(ids[1:2, :], count)
    both = (target + hot_rows(ids[0:1, :], count)).astype(bf16)
    target = target.astype(bf16)
    wide[...] = wigner[...].astype(f32)
    for j in range(COEF):
        at = slice(j * channels, (j + 1) * channels)
        paired[j] = half_dot(nodes[:, at].T, both).astype(bf16).astype(f32)
        at = slice((COEF + j) * channels, (COEF + j + 1) * channels)
        grad_edge[j] = half_dot(nodes[:, at].T, target).astype(bf16)
    for l in range(LMAX + 1):
        for k in ROWS_OF[l]:
            acc = None
            for j in COEFS_OF[l]:
                term = wide[k, j : j + 1, :] * paired[j]
                acc = term if acc is None else acc + term
            z[k] = acc.astype(bf16)


def forward_kernel(
    places,
    group,
    first,
    ids,
    z,
    wigner,
    grad_edge,
    attention_t,
    mine,
    other,
    message,
    stats,
    scalar,
    per_edge,
    held,
    y,
    wide,
    norm,
    msg,
    heads_acc,
    sems,
):
    channels, edges = LANES, wigner.shape[2]
    heads = attention_t.shape[0]
    count = stats.shape[1] // 2
    copy_weights(first[0, 0], mine, other, held, sems)
    wide[...] = wigner[...].astype(f32)
    base, rows = ZERO
    acc = None
    for tiles in pairs(rows):
        right = z[tiles[0] : tiles[-1] + 1].reshape(-1, edges)
        term = half_dot(map_tiles(held, places[0], tiles), right)
        acc = term if acc is None else acc + term
    spread(acc, held, places[0][2], base, y)
    for (base, rows), real, imag in ((ONE, places[1], places[2]), (TWO, places[3], places[4])):
        acc = None
        for tiles in pairs(rows):
            lo, hi = base + tiles[0], base + tiles[-1] + 1
            plus = z[lo:hi].reshape(-1, edges)
            minus = z[lo + rows : hi + rows].reshape(-1, edges)
            term = half_dot(map_tiles(held, real, tiles), jnp.concatenate([plus, minus], axis=1))
            term = term + half_dot(
                map_tiles(held, imag, tiles), jnp.concatenate([-minus, plus], axis=1)
            )
            acc = term if acc is None else acc + term
        spread(acc[:, :edges], held, real[2], base * channels, y)
        spread(acc[:, edges:], held, real[2], (base + rows) * channels, y)
    value = y[:channels, :]
    scalar[...] = value
    y[...] = y[...].astype(bf16).astype(f32)
    gating = (value / (1.0 + jnp.exp(-value))).astype(bf16)
    logits = half_dot(attention_t[...], gating)
    weight = jnp.where(ids[2:3, :] > 0, jnp.exp(logits), 0.0)
    target = hot_rows(ids[1:2, :], count)
    own_sum = nt_full(weight, target)
    at_edges = full_dot(own_sum, target)
    own_norm = weight / jnp.where(at_edges > 0.0, at_edges, 1.0)
    norm[...] = widen(own_norm, channels)

    def body(start):
        at = pl.ds(start, CHUNK)
        own = norm[at, :]
        total = jnp.zeros((CHUNK, edges), f32)
        for l in range(LMAX + 1):
            for j in COEFS_OF[l]:
                acc = None
                for k in ROWS_OF[l]:
                    term = wide[k, j : j + 1, :] * y[rows_at(k, start), :]
                    acc = term if acc is None else acc + term
                total = total + acc * grad_edge[j, at, :].astype(f32)
                msg[j, at, :] = (acc * own).astype(bf16)
        heads_acc[at, :] = total

    chunks(channels, body)
    grad_norm = jnp.sum(heads_acc[...].reshape(heads, channels // heads, edges), axis=1)
    own_shared = nt_full(own_norm * grad_norm, target)
    both = jnp.concatenate([own_sum, own_shared], axis=1)
    stats[...] = both
    per_edge[:heads, :] = own_norm
    per_edge[heads:, :] = grad_norm
    by_owner(target.astype(bf16), msg, message, group)
    rest = both
    if 2 * count < channels:
        rest = jnp.concatenate([both, jnp.zeros((heads, channels - 2 * count), f32)], axis=1)
    terms = []
    for _ in range(3):
        low = rest.astype(bf16).astype(f32)
        terms.append(low)
        rest = rest - low
    tail = jnp.concatenate(terms + [jnp.zeros((heads, channels), f32)], axis=0).astype(bf16)
    for owner in range(group):
        message[owner, message.shape[1] - 4 * heads :, :] = tail


def backward_kernel(
    zs,
    first,
    ids,
    stats,
    received,
    scalar,
    per_edge,
    wigner,
    grad_edge,
    attention,
    attention_t,
    z,
    grad_rows,
    mine,
    theirs,
    every,
    wide,
    norm,
    grad,
    turned,
):
    channels, edges = LANES, wigner.shape[2]
    heads = attention_t.shape[0]
    count = stats.shape[1] // 2
    wide[...] = wigner[...].astype(f32)
    tail = received[:, received.shape[1] - 4 * heads :, :].astype(f32)
    decoded = tail[:, :heads] + tail[:, heads : 2 * heads] + tail[:, 2 * heads : 3 * heads]
    every[...] = decoded
    total = jnp.sum(decoded[:, :, :count], axis=0)
    total = jnp.where(total > 0.0, total, 1.0)
    shares = decoded[:, :, :count] / total[None]
    shared = jnp.sum(shares * decoded[:, :, count : 2 * count], axis=0)
    own_share = stats[:, :count] / total
    target = hot_rows(ids[1:2, :], count)
    normalized = per_edge[:heads, :] * full_dot(own_share, target)
    grad_logit = normalized * (per_edge[heads:, :] - full_dot(shared, target))
    value = scalar[...]
    sigmoid = 1.0 / (1.0 + jnp.exp(-value))
    gating = (value / (1.0 + jnp.exp(-value))).astype(bf16).astype(f32)
    att = nt_full(grad_logit, gating)
    grad_gating = full_dot(attention[...].astype(f32), grad_logit)
    grad_scalar = grad_gating * sigmoid * (1.0 + value * (1.0 - sigmoid))
    norm[...] = widen(normalized, channels)

    def body(start):
        at = pl.ds(start, CHUNK)
        own = norm[at, :]
        for l in range(LMAX + 1):
            fields = [
                (grad_edge[j, at, :].astype(f32) * own).astype(bf16).astype(f32)
                for j in COEFS_OF[l]
            ]
            for k in ROWS_OF[l]:
                acc = None
                for j, field in zip(COEFS_OF[l], fields):
                    term = wide[k, j : j + 1, :] * field
                    acc = term if acc is None else acc + term
                grad[rows_at(k, start), :] = acc

    chunks(channels, body)
    grad[:channels, :] = grad[:channels, :] + grad_scalar
    depth = (LMAX + 1) * channels
    parts, share = mine.shape[0], depth // (2 * mine.shape[0])
    turned[:depth, :] = nt_dot(grad[:depth, :].astype(bf16), z[: LMAX + 1].reshape(depth, edges))
    turned[depth:, :] = jnp.zeros((turned.shape[0] - depth, depth), f32)
    padded = mine.shape[1]
    tail_row = lax.broadcasted_iota(jnp.int32, (padded, depth), 0)
    one = jnp.concatenate([att[h : h + 1, :] for h in range(LMAX + 1)], axis=1)
    two = [att[h : h + 1, :] for h in range(LMAX + 1, heads)]
    two = jnp.concatenate(two + [jnp.zeros((1, depth - len(two) * channels), f32)], axis=1)

    def store(outs):
        for core in range(2):
            for part in range(parts):
                at = (2 * part + core) * share
                block = turned[at : at + padded, :]
                block = jnp.where(tail_row == share, one, block)
                block = jnp.where(tail_row == share + 1, two, block)
                outs[core][part] = block.astype(bf16)

    @pl.when(first[0, 0] == 0)
    def _():
        store((mine, theirs))

    @pl.when(first[0, 0] != 0)
    def _():
        store((theirs, mine))

    for base, rows in (ZERO, ONE, (ONE[0] + ONE[1], ONE[1]), TWO, (TWO[0] + TWO[1], TWO[1])):
        size = rows * channels // (2 * zs)
        blocks = []
        for zz in range(zs):
            for xh in range(2):
                at = base * channels + (xh * zs + zz) * size
                blocks.append(grad[at : at + size, :])
        ordered = jnp.concatenate(blocks, axis=0)
        for t in range(rows):
            at = slice(t * channels, (t + 1) * channels)
            to = (base + t) * channels
            grad_rows[:, to : to + channels] = ordered[at, :].T.astype(bf16)


def scatter_kernel(
    places, group, own, first, ids, grad_rows, wigner, mine, other, grads, held, wide, dz, gp, sems
):
    channels, edges = LANES, wigner.shape[2]
    count = own * group
    copy_weights(first[0, 0], mine, other, held, sems)
    wide[...] = wigner[...].astype(f32)
    base, rows = ZERO
    left = grad_rows[:, : rows * channels]
    for tiles in pairs(rows):
        out = half_dot(left, map_tiles(held, places[0], tiles)).astype(bf16).astype(f32)
        for i, t in enumerate(tiles):
            dz[t] = out[:, i * channels : (i + 1) * channels].T
    for (base, rows), real, imag in ((ONE, places[1], places[2]), (TWO, places[3], places[4])):
        plus = grad_rows[:, base * channels : (base + rows) * channels]
        minus = grad_rows[:, (base + rows) * channels : (base + 2 * rows) * channels]
        left = jnp.concatenate([plus, minus], axis=0)
        crossed = jnp.concatenate([minus, -plus], axis=0)
        for tiles in pairs(rows):
            out = half_dot(left, map_tiles(held, real, tiles))
            out = out + half_dot(crossed, map_tiles(held, imag, tiles))
            out = out.astype(bf16).astype(f32)
            for i, t in enumerate(tiles):
                at = slice(i * channels, (i + 1) * channels)
                dz[base + t] = out[:edges, at].T
                dz[base + rows + t] = out[edges:, at].T

    def body(start):
        at = pl.ds(start, CHUNK)
        for l in range(LMAX + 1):
            for j in COEFS_OF[l]:
                acc = None
                for k in ROWS_OF[l]:
                    term = wide[k, j : j + 1, :] * dz[k, at, :]
                    acc = term if acc is None else acc + term
                gp[j, at, :] = acc.astype(bf16)

    chunks(channels, body)
    both = (hot_rows(ids[1:2, :], count) + hot_rows(ids[0:1, :], count)).astype(bf16)
    by_owner(both, gp, grads, group)
    grads[:, node_rows(own) :, :] = jnp.zeros(
        (group, grads.shape[1] - node_rows(own), channels), bf16
    )


def node_rows(own):
    return -(-COEF * own // 16) * 16


def sum_kernel(parts, scale, nodes, tail, acc):
    group, own = parts.shape[0], nodes.shape[0]
    span = node_rows(own)
    total = jnp.zeros((span, LANES), f32)
    for g in range(group):
        part = parts[g, :span, :].astype(f32).reshape(span // 8, 8, LANES)
        total = total + (part * scale[g][None]).reshape(span, LANES)
    acc[...] = total
    for n in range(own):
        nodes[n] = acc[pl.ds(n, COEF, stride=own), :].astype(bf16)
    tail[...] = jnp.sum(parts[:, span:, :].astype(f32), axis=0)


def per_channel(values, channels):
    rows, head_count = values.shape
    return jnp.broadcast_to(values[:, :, None], (rows, head_count, channels // head_count)).reshape(
        rows, channels
    )


def pad_to(block, rows, columns):
    return jnp.pad(block, ((0, rows - block.shape[0]), (0, columns - block.shape[1])))


def whole_lanes(count):
    return -(-count // LANES) * LANES


def column_tiles(block):
    rows, columns = block.shape
    tiles = block.reshape(rows, columns // LANES, LANES)
    return jnp.transpose(tiles, (1, 0, 2)).reshape(-1, LANES)


def gather_weights(shards):
    rows = [w.shape[0] for w in shards]
    columns = [w.shape[1] for w in shards]
    most = max(columns)
    packed = jnp.concatenate([pad_to(w.T, most, w.shape[0]) for w in shards], axis=1)
    packed = pad_to(packed, most, whole_lanes(packed.shape[1]))
    near = lax.all_gather(packed, "core")
    blocks, at = [], 0
    for r, n in zip(rows, columns):
        blocks.append(near[:, :n, at : at + r].reshape(2 * n, r))
        at += r
    first = lax.axis_index("core") == 0
    sets = ((0, 1), (2, 3, 4))
    lanes = whole_lanes(max(sum(rows[i] for i in s) for s in sets))
    sent = [
        pad_to(
            jnp.concatenate([pad_to(blocks[i], 2 * most, rows[i]) for i in s], axis=1),
            2 * most,
            lanes,
        )
        for s in sets
    ]
    slabs = gather(jnp.where(first, sent[0], sent[1]), ROW_GROUP)
    pieces = slabs.reshape(2, -1, 2 * most, lanes)
    whole = [r * pieces.shape[1] for r in rows]
    tiled = []
    for s in sets:
        at, parts = 0, []
        for i in s:
            piece = pieces[:, :, : 2 * columns[i], at : at + rows[i]]
            at += rows[i]
            piece = jnp.transpose(piece, (0, 2, 1, 3)).reshape(4 * columns[i], whole[i])
            parts.append(column_tiles(piece))
        tiled.append(jnp.concatenate(parts, axis=0))
    depth = max(t.shape[0] for t in tiled)
    tiled = [pad_to(t, depth, LANES) for t in tiled]
    half = lax.all_gather(jnp.where(first, tiled[0], tiled[1]), "z")
    places = [None] * len(shards)
    for half_index, s in enumerate(sets):
        at = 0
        for i in s:
            places[i] = (half_index, at, 4 * columns[i])
            at += whole[i] // LANES * 4 * columns[i]
    return half, places, slabs


def on_device(
    embeddings,
    atom_counts,
    edge_counts,
    source,
    target,
    wigner,
    cotangent,
    w_zero,
    w_one_real,
    w_one_imag,
    w_two_real,
    w_two_imag,
    attention,
):
    half, places, slabs = gather_weights((w_zero, w_one_real, w_one_imag, w_two_real, w_two_imag))
    row_count = embeddings.shape[1]
    harmonics = embeddings.shape[2]
    channels = embeddings.shape[3]
    width = harmonics * channels
    edge_rows = source.shape[1]
    head_count = attention.shape[1]
    group = lax.axis_size(GRAPH)
    all_nodes = row_count * group
    rotation = wigner[0]
    in_use = (lax.iota(jnp.int32, edge_rows) < edge_counts[0, 0]).astype(jnp.int32)
    ids = jnp.stack([source[0], target[0], in_use] + [jnp.zeros_like(in_use)] * 5)
    attention_t = attention.T
    core = lax.axis_index("core")
    first = core.astype(jnp.int32).reshape(1, 1)
    own_first = lax.axis_index(GRAPH) * row_count
    present = ((own_first + lax.iota(jnp.int32, row_count)) < atom_counts[0])[:, None]
    cot_rows = jnp.where(present, cotangent[0].reshape(row_count, width), 0.0).astype(bf16)
    own_rows = jnp.concatenate([embeddings[0].reshape(row_count, width), cot_rows], axis=1)
    own_rows, slabs = lax.optimization_barrier((own_rows, slabs))
    nodes = gather(own_rows, GRAPH).reshape(all_nodes, 2 * width)

    smem = pl.BlockSpec(memory_space=pltpu.SMEM)
    field = (channels, edge_rows)
    wide = pltpu.VMEM(rotation.shape, f32)
    z, grad_edge = pl.pallas_call(
        rotate_kernel,
        out_shape=(
            jax.ShapeDtypeStruct((REDUCED,) + field, bf16),
            jax.ShapeDtypeStruct((COEF,) + field, bf16),
        ),
        in_specs=[VMEM] * 3,
        out_specs=[VMEM] * 2,
        scratch_shapes=[pltpu.VMEM((COEF,) + field, f32), wide],
        compiler_params=PARAMS,
    )(ids, nodes, rotation)
    half, z, grad_edge = lax.optimization_barrier((half, z, grad_edge))
    other = lax.ppermute(half, "core", [(0, 1), (1, 0)])
    held = pltpu.VMEM((2,) + half.shape, bf16)
    copies = pltpu.SemaphoreType.DMA((2,))

    span = node_rows(row_count)
    message_sums, stats, scalar, per_edge = pl.pallas_call(
        functools.partial(forward_kernel, places, group),
        out_shape=(
            jax.ShapeDtypeStruct((group, span + 4 * head_count, channels), bf16),
            jax.ShapeDtypeStruct((head_count, 2 * all_nodes), f32),
            jax.ShapeDtypeStruct(field, f32),
            jax.ShapeDtypeStruct((2 * head_count, edge_rows), f32),
        ),
        in_specs=[smem] + [VMEM] * 5 + [ANY] * 2,
        out_specs=[VMEM] * 4,
        scratch_shapes=[
            held,
            pltpu.VMEM((REDUCED * channels, edge_rows), f32),
            wide,
            pltpu.VMEM(field, f32),
            pltpu.VMEM((COEF,) + field, bf16),
            pltpu.VMEM(field, f32),
            copies,
        ],
        compiler_params=PARAMS,
    )(first, ids, z, rotation, grad_edge, attention_t, half, other)
    received = exchange(message_sums, GRAPH)

    columns = lax.axis_size(COLUMN_GROUP)
    depth = channels * (LMAX + 1)
    share = depth // (2 * columns)
    padded = -(-(share + 2) // 16) * 16
    partial = jax.ShapeDtypeStruct((columns, padded, depth), bf16)
    grad_rows, mine, theirs, every = pl.pallas_call(
        functools.partial(backward_kernel, half.shape[0]),
        out_shape=(
            jax.ShapeDtypeStruct((edge_rows, REDUCED * channels), bf16),
            partial,
            partial,
            jax.ShapeDtypeStruct((group, head_count, channels), f32),
        ),
        in_specs=[smem] + [VMEM] * 10,
        out_specs=[VMEM] * 4,
        scratch_shapes=[
            wide,
            pltpu.VMEM(field, f32),
            pltpu.VMEM((REDUCED * channels, edge_rows), f32),
            pltpu.VMEM((depth + padded, depth), f32),
        ],
        compiler_params=PARAMS,
    )(first, ids, stats, received, scalar, per_edge, rotation, grad_edge, attention, attention_t, z)

    theirs = lax.ppermute(theirs, "core", [(0, 1), (1, 0)])
    mine = (mine.astype(f32) + theirs.astype(f32)).astype(bf16)
    zero_parts = exchange(mine, COLUMN_GROUP)
    zero_sum = jnp.sum(zero_parts.astype(f32), axis=0)
    att_flat = zero_sum[share : share + 2].reshape(-1)[: head_count * channels]
    zero_send = jnp.transpose(zero_sum[:share].reshape(share, group, -1), (1, 0, 2))
    inner = zero_send.shape[2]
    lanes = whole_lanes(inner)
    zero_send = jnp.pad(zero_send, ((0, 0), (0, 0), (0, lanes - inner)))
    zero_send = zero_send.reshape(group, share * lanes // LANES, LANES)
    att_send = jnp.broadcast_to(
        att_flat.reshape(1, head_count, channels), (group, head_count, channels)
    )
    last_rows = jnp.concatenate([zero_send, att_send], axis=1).astype(bf16)
    rest = -last_rows.shape[1] % 16
    last_rows = jnp.pad(last_rows, ((0, 0), (0, rest), (0, 0)))

    grad_sums = pl.pallas_call(
        functools.partial(scatter_kernel, places, group, row_count),
        out_shape=jax.ShapeDtypeStruct((group, span + last_rows.shape[1], channels), bf16),
        in_specs=[smem] + [VMEM] * 3 + [ANY] * 2,
        out_specs=VMEM,
        scratch_shapes=[
            held,
            wide,
            pltpu.VMEM((REDUCED,) + field, f32),
            pltpu.VMEM((COEF,) + field, bf16),
            copies,
        ],
        compiler_params=PARAMS,
    )(first, ids, grad_rows, rotation, half, other)
    grad_sums = lax.dynamic_update_slice(grad_sums, last_rows, (0, span, 0))
    last = exchange(grad_sums, GRAPH)

    def sum_parts(parts, scale):
        return pl.pallas_call(
            sum_kernel,
            out_shape=(
                jax.ShapeDtypeStruct((row_count, harmonics, channels), bf16),
                jax.ShapeDtypeStruct((parts.shape[1] - span, channels), f32),
            ),
            in_specs=[VMEM] * 2,
            out_specs=[VMEM] * 2,
            scratch_shapes=[pltpu.VMEM((span, channels), f32)],
            compiler_params=PARAMS,
        )(parts, scale)

    sums = lax.dynamic_slice_in_dim(every, own_first, row_count, axis=2)
    sums = jnp.transpose(sums, (0, 2, 1))
    total = jnp.sum(sums, axis=0)
    own_shares = jnp.where(present, sums / jnp.where(total > 0.0, total, 1.0), 0.0)
    scale = per_channel(own_shares.reshape(-1, head_count), channels)
    scale = jnp.tile(scale.reshape(group, row_count, channels), (1, 8 // row_count, 1))
    update, _ = sum_parts(received, scale)
    grad_nodes, tail = sum_parts(last, jnp.ones_like(scale))
    tail = tail * (1.0 / (2 * columns))
    zero_rows = share * lanes // LANES
    grad_zero = tail[:zero_rows].reshape(share, lanes)[:, :inner].T
    grad_att = tail[zero_rows : zero_rows + head_count].T

    shape = (1, row_count, harmonics, channels)
    return (update.reshape(shape), grad_nodes.reshape(shape), grad_zero, grad_att)


def solution(mesh):
    columns, group = mesh.shape["dp"], mesh.shape["graph"]
    devices = mesh.devices.reshape(2, columns // 4, 2, group // 2, 2)
    fine = Mesh(devices, DP + GRAPH)
    in_specs = (
        P(DP, GRAPH, None, None),
        P(DP),
        P(DP, GRAPH),
        P(DP, GRAPH),
        P(DP, GRAPH),
        P(DP, None, None, GRAPH),
        P(DP, GRAPH, None, None),
        P(GRAPH, DP),
        P(GRAPH, DP),
        P(GRAPH, DP),
        P(GRAPH, DP),
        P(GRAPH, DP),
        P(),
    )
    out_specs = (P(DP, GRAPH, None, None), P(DP, GRAPH, None, None), P(GRAPH, DP), P())
    return jax.shard_map(
        on_device, mesh=fine, in_specs=in_specs, out_specs=out_specs, check_vma=False
    )
```

time: 264 us -> 233 us (0.88)
  blocking collectives: 63.2 us -> 8.37 us
  waiting for transfers between devices: 82.1 us -> 120 us
  starting transfers between devices: 45.7 us -> 38.6 us
  local copies, waits for them, and re-layouts: 27.5 us -> 22 us
  other arithmetic: 8.91 us -> 3.9 us
  Pallas kernels: 17.8 us -> 20.9 us
    all_to_all x2 -> x0, blocking collectives: 51.4 us -> none  [gather(): return lax.all_to_all(copies, axes, split_axis=0, concat_axis=0, tiled=True)]
    all_to_all x2, waiting for transfers between devices: 30.3 us -> 50.8 us  [gather(): return lax.all_to_all(copies, axes, split_axis=0, concat_axis=0, tiled=True)]
    all_to_all x4 -> x3, waiting for transfers between devices: 41.3 us -> 61.7 us  [exchange(): return lax.all_to_all(blocks, axes, split_axis=0, concat_axis=0, tiled=True)]
    all_to_all x4 -> x3, starting transfers between devices: 26.7 us -> 17.9 us  [exchange(): return lax.all_to_all(blocks, axes, split_axis=0, concat_axis=0, tiled=True)]
    reshape x9 -> x4, local copies, waits for them, and re-layouts: 7.5 us -> 1.39 us  [the longest x1 1.34 us: on_device(): nodes = gather(own_rows, GRAPH).reshape(all_nodes, 2 * width)]
    unnamed x46 -> x37, local copies, waits for them, and re-layouts: 12.5 us -> 8.67 us
    reduce_sum x3 -> x0, other arithmetic: 3.53 us -> none  [the longest x1 1.57 us: on_device(): summed = jnp.sum(parts * wide, axis=0)]
    all_gather x1, waiting for transfers between devices: 3.45 us -> 0.02 us  [gather_weights(): half = lax.all_gather(jnp.where(first, tiled[0], tiled[1]), 'z')]
  transfers between devices with their start and end apart: 9 -> 8, of which waited for: 9 -> 7; matrix products, arithmetic and copies ran while one was open for 7% -> 2% of each run, Pallas kernels for 4% -> 4%
where the time goes in v1:
time: 233 us; the launch traced here: 229 us
  waiting for transfers between devices  120 us (52%)
  starting transfers between devices  38.6 us (17%)
  local copies, waits for them, and re-layouts  22 us (9%)
  Pallas kernels  20.9 us (9%)
  between operations  15.9 us (7%)
  blocking collectives  8.37 us (4%)
  other arithmetic  3.9 us (2%)
    all_to_all x3, waiting for transfers between devices, exchange(): return lax.all_to_all(blocks, axes, split_axis=0, concat_axis=0, tiled=True)  61.7 us
    all_to_all x2, waiting for transfers between devices, gather(): return lax.all_to_all(copies, axes, split_axis=0, concat_axis=0, tiled=True)  50.8 us
    all_to_all x3, starting transfers between devices, exchange(): return lax.all_to_all(blocks, axes, split_axis=0, concat_axis=0, tiled=True)  17.9 us
    unnamed x37, local copies, waits for them, and re-layouts  8.67 us
    all_gather x1, blocking collectives, gather_weights(): near = lax.all_gather(packed, 'core')  8.37 us
    all_to_all x2, starting transfers between devices, gather(): return lax.all_to_all(copies, axes, split_axis=0, concat_axis=0, tiled=True)  8.13 us
    pallas_call x1, Pallas kernels, on_device(): pl.pallas_call(functools.partial(forward_kernel, places, group), out_shap...  7.24 us
    ppermute x1, starting transfers between devices, on_device(): other = lax.ppermute(half, 'core', [(0, 1), (1, 0)])  6.91 us
  transfers between devices with their start and end apart: 8, of which 7 were waited for; matrix products, arithmetic and copies ran while one was open for 2% of the time, Pallas kernels for 4%

profile of v1, /device:TPU:1, one launch (start us, length us, event | category | flops | bytes accessed | tf_op | source)
XLA Modules:
  0.0 229.2 jit_solution(2635747520412054479)
XLA Ops:
  10.8 8.4 %all-gather.2 = bf16[2,28,256]{2,1,0:T(8,128)(2,1)S(1)} all-gather(bf16[1,28,256]{2,1,0:T(8,128)(2,1)S(1)} %pad_bitcast_fusion), channel_id=2, replica_groups=mesh['xh'=2,'z'=8,'core'=2,'y'=8,'xl'=2] {'core'}, dimensions={0}, use_global_device_ids=true | all-gather | bytes 43008 | tf_op jit(solution)/shard_map/all_gather | solution.py:453
  19.5 0.8 broadcast_in_dim.57
  20.4 4.3 %all-to-all-start = ((bf16[32,56,128]{2,1,0:T(8,128)(2,1)}), bf16[32,56,128]{2,1,0:T(8,128)(2,1)S(1)}, u32[]{:S(2)}, u32[]{:S(2)}) async-start(bf16[32,56,128]{2,1,0:T(8,128)(2,1)} %broadcast_in_dim.57), calls=%async_computation | async-start | bytes 917504 | tf_op jit(solution)/shard_map/all_to_all | solution.py:32
  25.4 15.4 %all-to-all-done = bf16[32,56,128]{2,1,0:T(8,128)(2,1)S(1)} async-done(((bf16[32,56,128]{2,1,0:T(8,128)(2,1)}), bf16[32,56,128]{2,1,0:T(8,128)(2,1)S(1)}, u32[]{:S(2)}, u32[]{:S(2)}) %all-to-all-start) | async-done | bytes 458784 | tf_op jit(solution)/shard_map/all_to_all | solution.py:32
  44.0 0.8 fusion.3
  45.1 1.6 broadcast_in_dim.60
  46.6 3.8 %all-to-all-start.1 = ((bf16[16,4,12544]{2,1,0:T(4,128)(2,1)}), bf16[16,4,12544]{2,1,0:T(4,128)(2,1)S(1)}, u32[]{:S(2)}, u32[]{:S(2)}) async-start(bf16[16,4,12544]{2,1,0:T(4,128)(2,1)} %broadcast_in_dim.60), calls=%async_computation.1 | async-start | bytes 3211264 | tf_op jit(solution)/shard_map/all_to_all | solution.py:32
  51.4 35.4 %all-to-all-done.1 = bf16[16,4,12544]{2,1,0:T(4,128)(2,1)S(1)} async-done(((bf16[16,4,12544]{2,1,0:T(4,128)(2,1)}), bf16[16,4,12544]{2,1,0:T(4,128)(2,1)S(1)}, u32[]{:S(2)}, u32[]{:S(2)}) %all-to-all-start.1) | async-done | bytes 1605664 | tf_op jit(solution)/shard_map/all_to_all | solution.py:32
  86.8 1.3 reshape.100.nodes
  88.1 1.4 copy-done.4
  89.5 1.7 shard_map.156
  91.3 6.9 %collective-permute-start = (bf16[8,1376,128]{2,1,0:T(8,128)(2,1)}, bf16[8,1376,128]{2,1,0:T(8,128)(2,1)S(1)}, u32[]{:S(2)}, u32[]{:S(2)}) collective-permute-start(bf16[8,1376,128]{2,1,0:T(8,128)(2,1)} %bitcast.72), channel_id=1, source_target_pairs={{0,16},{16,0},{1,17},{17,1},{2,18},{18,2},{3,19},{19,3},{4,20},{20... | collective-permute-start | bytes 8454152 | tf_op jit(solution)/shard_map/ppermute | solution.py:545
  98.2 5.0 %collective-permute-done.other = bf16[8,1376,128]{2,1,0:T(8,128)(2,1)S(1)} collective-permute-done((bf16[8,1376,128]{2,1,0:T(8,128)(2,1)}, bf16[8,1376,128]{2,1,0:T(8,128)(2,1)S(1)}, u32[]{:S(2)}, u32[]{:S(2)}) %collective-permute-start) | collective-permute-done | bytes 2818080 | tf_op jit(solution)/shard_map/ppermute | solution.py:545
  103.2 1.6 copy-done.10
  104.8 7.2 %shard_map.157 = (bf16[16,240,128]{2,1,0:T(8,128)(2,1)S(1)}, f32[8,128]{1,0:T(8,128)S(1)}, f32[128,128]{1,0:T(8,128)S(1)}, f32[16,128]{1,0:T(8,128)S(1)}) custom-call(s32[1,1]{1,0:T(1,128)} %bitcast.first, s32[8,128]{1,0:T(8,128)S(1)} %stack.8.ids, bf16[29,128,128]{2,1,0:T(8,128)(2,1)S(1)} %get-tuple-element.24.z, bf16[29,49,128]{2,1,0:T(8,128)(2,1)S(1)} %bitcast.76, ...), custom_call_target="tpu_custom_call" | custom-call | tf_op jit(solution)/shard_map/pallas_call | solution.py:550
  112.1 1.0 copy-done.6
  113.0 3.6 %all-to-all-start.2 = ((bf16[16,240,128]{2,1,0:T(8,128)(2,1)}), bf16[16,240,128]{2,1,0:T(8,128)(2,1)S(1)}, u32[]{:S(2)}, u32[]{:S(2)}) async-start(bf16[16,240,128]{2,1,0:T(8,128)(2,1)} %copy-done.6), calls=%async_computation.2 | async-start | bytes 1966080 | tf_op jit(solution)/shard_map/all_to_all | solution.py:36
  116.8 24.5 %all-to-all-done.2.received.parts = bf16[16,240,128]{2,1,0:T(8,128)(2,1)S(1)} async-done(((bf16[16,240,128]{2,1,0:T(8,128)(2,1)}), bf16[16,240,128]{2,1,0:T(8,128)(2,1)S(1)}, u32[]{:S(2)}, u32[]{:S(2)}) %all-to-all-start.2) | async-done | bytes 983072 | tf_op jit(solution)/shard_map/all_to_all | solution.py:36
  141.4 5.1 %shard_map.158 = (bf16[128,3712]{1,0:T(8,128)(2,1)S(1)}, bf16[16,32,896]{2,1,0:T(8,128)(2,1)S(1)}, bf16[16,32,896]{2,1,0:T(8,128)(2,1)S(1)}, f32[16,8,128]{2,1,0:T(8,128)S(1)}) custom-call(s32[1,1]{1,0:T(1,128)} %bitcast.first, s32[8,128]{1,0:T(8,128)S(1)} %stack.8.ids, f32[8,128]{1,0:T(8,128)S(1)} %get-tuple-element.28.stats, ...), custom_call_target="tpu_custom_call" | custom-call | tf_op jit(solution)/shard_map/pallas_call | solution.py:578
  146.5 1.0 copy-done.7
  147.4 5.6 %collective-permute-start.1 = (bf16[16,32,896]{2,1,0:T(8,128)(2,1)S(1)}, bf16[16,32,896]{2,1,0:T(8,128)(2,1)S(1)}, u32[]{:S(2)}, u32[]{:S(2)}) collective-permute-start(bf16[16,32,896]{2,1,0:T(8,128)(2,1)S(1)} %get-tuple-element.35), channel_id=1, source_target_pairs={{0,16},{16,0},{1,17},{17,1},{2,18},{18,2},{3,19},{19,3},{4,20},{20... | collective-permute-start | bytes 2752520 | tf_op jit(solution)/shard_map/ppermute | solution.py:597
  153.0 2.1 collective-permute-done.1
  155.1 1.2 add_convert_fusion
  156.3 10.6 %all-to-all-start.3 = ((bf16[16,32,896]{2,1,0:T(8,128)(2,1)}), bf16[16,32,896]{2,1,0:T(8,128)(2,1)}, u32[]{:S(2)}, u32[]{:S(2)}) async-start(bf16[16,32,896]{2,1,0:T(8,128)(2,1)} %add_convert_fusion), calls=%async_computation.3 | async-start | bytes 1835008 | tf_op jit(solution)/shard_map/all_to_all | solution.py:36
  167.0 1.2 copy-done.8
  168.2 5.8 %shard_map.160 = bf16[16,256,128]{2,1,0:T(8,128)(2,1)S(1)} custom-call(s32[1,1]{1,0:T(1,128)} %bitcast.first, s32[8,128]{1,0:T(8,128)S(1)} %stack.8.ids, bf16[128,3712]{1,0:T(8,128)(2,1)S(1)} %copy-done.8, bf16[29,49,128]{2,1,0:T(8,128)(2,1)S(1)} %bitcast.78, bf16[8,1376,128]{2,1,0:T(8,128)(2,1)S(1)} %bitcast.74, bf16[8,1376,128]{2,1,0:T(8,128)(2,1)} %copy-done.10), custom_call_target="tpu_custom_call" | custom-call | tf_op jit(solution)/shard_map/pallas_call | solution.py:614
  174.0 1.0 copy-done.5
  174.9 15.4 %all-to-all-done.3 = bf16[16,32,896]{2,1,0:T(8,128)(2,1)} async-done(((bf16[16,32,896]{2,1,0:T(8,128)(2,1)}), bf16[16,32,896]{2,1,0:T(8,128)(2,1)}, u32[]{:S(2)}, u32[]{:S(2)}) %all-to-all-start.3) | async-done | bytes 917536 | tf_op jit(solution)/shard_map/all_to_all | solution.py:36
  190.3 1.3 convert_reduce_fusion
  192.7 3.7 %all-to-all-start.4 = ((bf16[16,256,128]{2,1,0:T(8,128)(2,1)}), bf16[16,256,128]{2,1,0:T(8,128)(2,1)S(1)}, u32[]{:S(2)}, u32[]{:S(2)}) async-start(bf16[16,256,128]{2,1,0:T(8,128)(2,1)} %pad_dynamic-update-slice_fusion), calls=%async_computation.4 | async-start | bytes 2097152 | tf_op jit(solution)/shard_map/all_to_all | solution.py:36
  197.0 0.8 shard_map.159
  198.5 21.8 %all-to-all-done.4.parts = bf16[16,256,128]{2,1,0:T(8,128)(2,1)S(1)} async-done(((bf16[16,256,128]{2,1,0:T(8,128)(2,1)}), bf16[16,256,128]{2,1,0:T(8,128)(2,1)S(1)}, u32[]{:S(2)}, u32[]{:S(2)}) %all-to-all-start.4) | async-done | bytes 1048608 | tf_op jit(solution)/shard_map/all_to_all | solution.py:36
  (92 shorter events, 12.0 us)
Async XLA Ops:
  20.4 20.4 %all-to-all-start = ((bf16[32,56,128]{2,1,0:T(8,128)(2,1)}), bf16[32,56,128]{2,1,0:T(8,128)(2,1)S(1)}, u32[]{:S(2)}, u32[]{:S(2)}) async-start(bf16[32,56,128]{2,1,0:T(8,128)(2,1)} %broadcast_in_dim.57), calls=%async_computation | async-start | bytes 917504 | tf_op jit(solution)/shard_map/all_to_all | solution.py:32
  24.7 66.7 %all-gather.5.cloned.1.call-start = ((), (), s32[]{:S(2)}) async-start(), calls=%async_computation.5 | async-start | bytes 3170304 | tf_op jit(solution)/shard_map/all_gather | solution.py:483
  43.3 1.6 copy-start.12
  43.3 1.7 copy-start.13
  46.6 3.9 %copy-start.11 = (bf16[1,29,49,128]{3,1,2,0:T(8,128)(2,1)S(1)}, bf16[1,29,49,128]{3,1,2,0:T(8,128)(2,1)}, u32[]{:S(2)}) copy-start(bf16[1,29,49,128]{3,1,2,0:T(8,128)(2,1)} %param.18) | copy-start | bytes 1091332
  46.6 4.7 %copy-start.14 = (s32[1,128]{1,0:T(1,128)S(1)}, s32[1,128]{1,0:T(1,128)}, u32[]{:S(2)}) copy-start(s32[1,128]{1,0:T(1,128)} %param.16) | copy-start | bytes 1540
  46.6 4.7 %copy-start.15 = (s32[1,128]{1,0:T(1,128)S(1)}, s32[1,128]{1,0:T(1,128)}, u32[]{:S(2)}) copy-start(s32[1,128]{1,0:T(1,128)} %param.17) | copy-start | bytes 1540
  46.6 40.1 %all-to-all-start.1 = ((bf16[16,4,12544]{2,1,0:T(4,128)(2,1)}), bf16[16,4,12544]{2,1,0:T(4,128)(2,1)S(1)}, u32[]{:S(2)}, u32[]{:S(2)}) async-start(bf16[16,4,12544]{2,1,0:T(4,128)(2,1)} %broadcast_in_dim.60), calls=%async_computation.1 | async-start | bytes 3211264 | tf_op jit(solution)/shard_map/all_to_all | solution.py:32
  51.4 53.4 %copy-start.9 = (bf16[128,8]{0,1:T(8,128)(2,1)S(1)}, bf16[128,8]{0,1:T(8,128)(2,1)}, u32[]{:S(2)}) copy-start(bf16[128,8]{0,1:T(8,128)(2,1)} %param.25) | copy-start | bytes 6148
  88.1 1.4 copy-start.4
  91.3 20.8 %copy-start.3 = (bf16[49,128,128]{2,1,0:T(8,128)(2,1)}, bf16[49,128,128]{2,1,0:T(8,128)(2,1)S(1)}, u32[]{:S(2)}) copy-start(bf16[49,128,128]{2,1,0:T(8,128)(2,1)S(1)} %get-tuple-element.25.grad_edge) | copy-start | bytes 4816900
  91.3 11.9 %collective-permute-start = (bf16[8,1376,128]{2,1,0:T(8,128)(2,1)}, bf16[8,1376,128]{2,1,0:T(8,128)(2,1)S(1)}, u32[]{:S(2)}, u32[]{:S(2)}) collective-permute-start(bf16[8,1376,128]{2,1,0:T(8,128)(2,1)} %bitcast.72), channel_id=1, source_target_pairs={{0,16},{16,0},{1,17},{17,1},{2,18},{18,2},{3,19},{19,3},{4,20},{20... | collective-permute-start | bytes 8454152 | tf_op jit(solution)/shard_map/ppermute | solution.py:545
  103.2 1.6 copy-start.10
  112.1 1.0 copy-start.6
  113.0 28.3 %all-to-all-start.2 = ((bf16[16,240,128]{2,1,0:T(8,128)(2,1)}), bf16[16,240,128]{2,1,0:T(8,128)(2,1)S(1)}, u32[]{:S(2)}, u32[]{:S(2)}) async-start(bf16[16,240,128]{2,1,0:T(8,128)(2,1)} %copy-done.6), calls=%async_computation.2 | async-start | bytes 1966080 | tf_op jit(solution)/shard_map/all_to_all | solution.py:36
  141.4 5.1 %copy-start.1 = (bf16[16,240,128]{2,1,0:T(8,128)(2,1)}, bf16[16,240,128]{2,1,0:T(8,128)(2,1)S(1)}, u32[]{:S(2)}) copy-start(bf16[16,240,128]{2,1,0:T(8,128)(2,1)S(1)} %all-to-all-done.2.received.parts) | copy-start | bytes 2949124
  146.5 1.0 copy-start.7
  147.4 7.7 %collective-permute-start.1 = (bf16[16,32,896]{2,1,0:T(8,128)(2,1)S(1)}, bf16[16,32,896]{2,1,0:T(8,128)(2,1)S(1)}, u32[]{:S(2)}, u32[]{:S(2)}) collective-permute-start(bf16[16,32,896]{2,1,0:T(8,128)(2,1)S(1)} %get-tuple-element.35), channel_id=1, source_target_pairs={{0,16},{16,0},{1,17},{17,1},{2,18},{18,2},{3,19},{19,3},{4,20},{20... | collective-permute-start | bytes 2752520 | tf_op jit(solution)/shard_map/ppermute | solution.py:597
  155.1 11.9 %copy-start = (bf16[11008,128]{1,0:T(8,128)(2,1)S(1)}, bf16[11008,128]{1,0:T(8,128)(2,1)}, u32[]{:S(2)}) copy-start(bf16[11008,128]{1,0:T(8,128)(2,1)} %all-gather.5.cloned.1.call-done) | copy-start | bytes 8454148
  156.3 34.0 %all-to-all-start.3 = ((bf16[16,32,896]{2,1,0:T(8,128)(2,1)}), bf16[16,32,896]{2,1,0:T(8,128)(2,1)}, u32[]{:S(2)}, u32[]{:S(2)}) async-start(bf16[16,32,896]{2,1,0:T(8,128)(2,1)} %add_convert_fusion), calls=%async_computation.3 | async-start | bytes 1835008 | tf_op jit(solution)/shard_map/all_to_all | solution.py:36
  167.0 1.2 copy-start.8
  174.0 1.0 copy-start.5
  191.9 5.1 %copy-start.2 = (bf16[16,240,128]{2,1,0:T(8,128)(2,1)S(1)}, bf16[16,240,128]{2,1,0:T(8,128)(2,1)}, u32[]{:S(2)}) copy-start(bf16[16,240,128]{2,1,0:T(8,128)(2,1)} %copy-done.1) | copy-start | bytes 2949124
  192.7 27.6 %all-to-all-start.4 = ((bf16[16,256,128]{2,1,0:T(8,128)(2,1)}), bf16[16,256,128]{2,1,0:T(8,128)(2,1)S(1)}, u32[]{:S(2)}, u32[]{:S(2)}) async-start(bf16[16,256,128]{2,1,0:T(8,128)(2,1)} %pad_dynamic-update-slice_fusion), calls=%async_computation.4 | async-start | bytes 2097152 | tf_op jit(solution)/shard_map/all_to_all | solution.py:36
Sparse Core Ops, SparseCore 0:
  45.0 44.2 all-gather.4

commit v2 on v1

--- a/solution.py
+++ b/solution.py
@@ -140,6 +140,33 @@
             parts.append(part.reshape(group, 1, own, channels))
         block = jnp.concatenate(parts, axis=1).reshape(group, 16, channels)
         out[:, first * own : first * own + 16, :] = block.astype(bf16)
+
+
+def pack_kernel(places, *refs):
+    shards, out, acc = refs[:-2], refs[-2], refs[-1]
+    acc[...] = jnp.zeros_like(acc)
+    for shard, at in zip(shards, places):
+        rows, columns = shard.shape
+        lane = lax.broadcasted_iota(jnp.int32, (rows, acc.shape[1]), 1)
+        row = lax.broadcasted_iota(jnp.int32, (rows, acc.shape[1]), 0)
+        place = (lane == row + at).astype(bf16)
+        acc[:columns, :] += lax.dot_general(
+            shard[...], place, (((0,), (0,)), ((), ())), preferred_element_type=f32
+        )
+    out[...] = acc[...].astype(bf16)
+
+
+def share_kernel(stats, every, message, out):
+    group = message.shape[0]
+    count = stats.shape[1] // 2
+    total = jnp.sum(every[:, :, :count], axis=0)
+    share = stats[:, :count] / jnp.where(total > 0.0, total, 1.0)
+    scale = widen(share, LANES).T.reshape(group, 1, count // group, LANES)
+    per = 16 * group // count
+    scale = jnp.broadcast_to(scale, (group, per, count // group, LANES)).reshape(group, 16, LANES)
+    for at in range(0, message.shape[1], 16):
+        part = message[:, at : at + 16, :].astype(f32) * scale
+        out[:, at : at + 16, :] = part.astype(bf16)
 
 
 def rotate_kernel(ids, nodes, wigner, z, grad_edge, paired, wide):
@@ -240,30 +267,17 @@
     chunks(channels, body)
     grad_norm = jnp.sum(heads_acc[...].reshape(heads, channels // heads, edges), axis=1)
     own_shared = nt_full(own_norm * grad_norm, target)
-    both = jnp.concatenate([own_sum, own_shared], axis=1)
-    stats[...] = both
+    stats[...] = jnp.concatenate([own_sum, own_shared], axis=1)
     per_edge[:heads, :] = own_norm
     per_edge[heads:, :] = grad_norm
     by_owner(target.astype(bf16), msg, message, group)
-    rest = both
-    if 2 * count < channels:
-        rest = jnp.concatenate([both, jnp.zeros((heads, channels - 2 * count), f32)], axis=1)
-    terms = []
-    for _ in range(3):
-        low = rest.astype(bf16).astype(f32)
-        terms.append(low)
-        rest = rest - low
-    tail = jnp.concatenate(terms + [jnp.zeros((heads, channels), f32)], axis=0).astype(bf16)
-    for owner in range(group):
-        message[owner, message.shape[1] - 4 * heads :, :] = tail
 
 
 def backward_kernel(
-    zs,
     first,
     ids,
     stats,
-    received,
+    every,
     scalar,
     per_edge,
     wigner,
@@ -271,10 +285,9 @@
     attention,
     attention_t,
     z,
-    grad_rows,
+    grad_conv,
     mine,
     theirs,
-    every,
     wide,
     norm,
     grad,
@@ -284,13 +297,10 @@
     heads = attention_t.shape[0]
     count = stats.shape[1] // 2
     wide[...] = wigner[...].astype(f32)
-    tail = received[:, received.shape[1] - 4 * heads :, :].astype(f32)
-    decoded = tail[:, :heads] + tail[:, heads : 2 * heads] + tail[:, 2 * heads : 3 * heads]
-    every[...] = decoded
-    total = jnp.sum(decoded[:, :, :count], axis=0)
+    total = jnp.sum(every[:, :, :count], axis=0)
     total = jnp.where(total > 0.0, total, 1.0)
-    shares = decoded[:, :, :count] / total[None]
-    shared = jnp.sum(shares * decoded[:, :, count : 2 * count], axis=0)
+    shares = every[:, :, :count] / total[None]
+    shared = jnp.sum(shares * every[:, :, count:], axis=0)
     own_share = stats[:, :count] / total
     target = hot_rows(ids[1:2, :], count)
     normalized = per_edge[:heads, :] * full_dot(own_share, target)
@@ -322,7 +332,8 @@
     grad[:channels, :] = grad[:channels, :] + grad_scalar
     depth = (LMAX + 1) * channels
     parts, share = mine.shape[0], depth // (2 * mine.shape[0])
-    turned[:depth, :] = nt_dot(grad[:depth, :].astype(bf16), z[: LMAX + 1].reshape(depth, edges))
+    grad_conv[...] = grad[...].astype(bf16)
+    turned[:depth, :] = nt_dot(grad_conv[:depth, :], z[: LMAX + 1].reshape(depth, edges))
     turned[depth:, :] = jnp.zeros((turned.shape[0] - depth, depth), f32)
     padded = mine.shape[1]
     tail_row = lax.broadcasted_iota(jnp.int32, (padded, depth), 0)
@@ -347,6 +358,32 @@
     def _():
         store((theirs, mine))
 
+
+def scatter_kernel(
+    places,
+    group,
+    own,
+    first,
+    ids,
+    grad_conv,
+    wigner,
+    mine,
+    other,
+    grads,
+    held,
+    wide,
+    dz,
+    gp,
+    grad,
+    grad_rows,
+    sems,
+):
+    channels, edges = LANES, wigner.shape[2]
+    count = own * group
+    copy_weights(first[0, 0], mine, other, held, sems)
+    wide[...] = wigner[...].astype(f32)
+    grad[...] = grad_conv[...].astype(f32)
+    zs = held.shape[1]
     for base, rows in (ZERO, ONE, (ONE[0] + ONE[1], ONE[1]), TWO, (TWO[0] + TWO[1], TWO[1])):
         size = rows * channels // (2 * zs)
         blocks = []
@@ -359,15 +396,6 @@
             at = slice(t * channels, (t + 1) * channels)
             to = (base + t) * channels
             grad_rows[:, to : to + channels] = ordered[at, :].T.astype(bf16)
-
-
-def scatter_kernel(
-    places, group, own, first, ids, grad_rows, wigner, mine, other, grads, held, wide, dz, gp, sems
-):
-    channels, edges = LANES, wigner.shape[2]
-    count = own * group
-    copy_weights(first[0, 0], mine, other, held, sems)
-    wide[...] = wigner[...].astype(f32)
     base, rows = ZERO
     left = grad_rows[:, : rows * channels]
     for tiles in pairs(rows):
@@ -401,33 +429,20 @@
     chunks(channels, body)
     both = (hot_rows(ids[1:2, :], count) + hot_rows(ids[0:1, :], count)).astype(bf16)
     by_owner(both, gp, grads, group)
-    grads[:, node_rows(own) :, :] = jnp.zeros(
-        (group, grads.shape[1] - node_rows(own), channels), bf16
-    )
 
 
 def node_rows(own):
     return -(-COEF * own // 16) * 16
 
 
-def sum_kernel(parts, scale, nodes, tail, acc):
+def sum_kernel(parts, nodes, total):
     group, own = parts.shape[0], nodes.shape[0]
-    span = node_rows(own)
-    total = jnp.zeros((span, LANES), f32)
-    for g in range(group):
-        part = parts[g, :span, :].astype(f32).reshape(span // 8, 8, LANES)
-        total = total + (part * scale[g][None]).reshape(span, LANES)
-    acc[...] = total
+    acc = parts[0].astype(f32)
+    for g in range(1, group):
+        acc = acc + parts[g].astype(f32)
+    total[...] = acc
     for n in range(own):
-        nodes[n] = acc[pl.ds(n, COEF, stride=own), :].astype(bf16)
-    tail[...] = jnp.sum(parts[:, span:, :].astype(f32), axis=0)
-
-
-def per_channel(values, channels):
-    rows, head_count = values.shape
-    return jnp.broadcast_to(values[:, :, None], (rows, head_count, channels // head_count)).reshape(
-        rows, channels
-    )
+        nodes[n] = total[pl.ds(n, COEF, stride=own), :].astype(bf16)
 
 
 def pad_to(block, rows, columns):
@@ -447,35 +462,35 @@
 def gather_weights(shards):
     rows = [w.shape[0] for w in shards]
     columns = [w.shape[1] for w in shards]
-    most = max(columns)
-    packed = jnp.concatenate([pad_to(w.T, most, w.shape[0]) for w in shards], axis=1)
-    packed = pad_to(packed, most, whole_lanes(packed.shape[1]))
-    near = lax.all_gather(packed, "core")
-    blocks, at = [], 0
-    for r, n in zip(rows, columns):
-        blocks.append(near[:, :n, at : at + r].reshape(2 * n, r))
-        at += r
-    first = lax.axis_index("core") == 0
+    most = -(-max(columns) // 16) * 16
     sets = ((0, 1), (2, 3, 4))
     lanes = whole_lanes(max(sum(rows[i] for i in s) for s in sets))
-    sent = [
-        pad_to(
-            jnp.concatenate([pad_to(blocks[i], 2 * most, rows[i]) for i in s], axis=1),
-            2 * most,
-            lanes,
-        )
-        for s in sets
-    ]
-    slabs = gather(jnp.where(first, sent[0], sent[1]), ROW_GROUP)
-    pieces = slabs.reshape(2, -1, 2 * most, lanes)
+    starts = [0] * len(shards)
+    for half_index, s in enumerate(sets):
+        for n, i in enumerate(s):
+            starts[i] = half_index * lanes + sum(rows[j] for j in s[:n])
+    packed = pl.pallas_call(
+        functools.partial(pack_kernel, starts),
+        out_shape=jax.ShapeDtypeStruct((most, 2 * lanes), bf16),
+        in_specs=[VMEM] * len(shards),
+        out_specs=VMEM,
+        scratch_shapes=[pltpu.VMEM((most, 2 * lanes), f32)],
+        compiler_params=PARAMS,
+    )(*shards)
+    near = lax.all_gather(packed, "core")
+    core = lax.axis_index("core")
+    first = core == 0
+    sent = lax.dynamic_slice_in_dim(near, core * lanes, lanes, axis=2)
+    slabs = gather(sent.reshape(2 * most, lanes), ROW_GROUP)
+    pieces = slabs.reshape(2, -1, 2, most, lanes)
     whole = [r * pieces.shape[1] for r in rows]
     tiled = []
     for s in sets:
         at, parts = 0, []
         for i in s:
-            piece = pieces[:, :, : 2 * columns[i], at : at + rows[i]]
+            piece = pieces[:, :, :, : columns[i], at : at + rows[i]]
             at += rows[i]
-            piece = jnp.transpose(piece, (0, 2, 1, 3)).reshape(4 * columns[i], whole[i])
+            piece = jnp.transpose(piece, (0, 2, 3, 1, 4)).reshape(4 * columns[i], whole[i])
             parts.append(column_tiles(piece))
         tiled.append(jnp.concatenate(parts, axis=0))
     depth = max(t.shape[0] for t in tiled)
@@ -526,6 +541,8 @@
     own_rows = jnp.concatenate([embeddings[0].reshape(row_count, width), cot_rows], axis=1)
     own_rows, slabs = lax.optimization_barrier((own_rows, slabs))
     nodes = gather(own_rows, GRAPH).reshape(all_nodes, 2 * width)
+    half, nodes = lax.optimization_barrier((half, nodes))
+    other = lax.ppermute(half, "core", [(0, 1), (1, 0)])
 
     smem = pl.BlockSpec(memory_space=pltpu.SMEM)
     field = (channels, edge_rows)
@@ -541,8 +558,6 @@
         scratch_shapes=[pltpu.VMEM((COEF,) + field, f32), wide],
         compiler_params=PARAMS,
     )(ids, nodes, rotation)
-    half, z, grad_edge = lax.optimization_barrier((half, z, grad_edge))
-    other = lax.ppermute(half, "core", [(0, 1), (1, 0)])
     held = pltpu.VMEM((2,) + half.shape, bf16)
     copies = pltpu.SemaphoreType.DMA((2,))
 
@@ -550,7 +565,7 @@
     message_sums, stats, scalar, per_edge = pl.pallas_call(
         functools.partial(forward_kernel, places, group),
         out_shape=(
-            jax.ShapeDtypeStruct((group, span + 4 * head_count, channels), bf16),
+            jax.ShapeDtypeStruct((group, span, channels), bf16),
             jax.ShapeDtypeStruct((head_count, 2 * all_nodes), f32),
             jax.ShapeDtypeStruct(field, f32),
             jax.ShapeDtypeStruct((2 * head_count, edge_rows), f32),
@@ -568,23 +583,31 @@
         ],
         compiler_params=PARAMS,
     )(first, ids, z, rotation, grad_edge, attention_t, half, other)
-    received = exchange(message_sums, GRAPH)
+    every = gather(stats, GRAPH)
+    shared_sums = pl.pallas_call(
+        share_kernel,
+        out_shape=jax.ShapeDtypeStruct(message_sums.shape, bf16),
+        in_specs=[VMEM] * 3,
+        out_specs=VMEM,
+        compiler_params=PARAMS,
+    )(stats, every, message_sums)
+    every, shared_sums = lax.optimization_barrier((every, shared_sums))
+    summed = lax.psum_scatter(shared_sums, GRAPH, scatter_dimension=0, tiled=True)
 
     columns = lax.axis_size(COLUMN_GROUP)
     depth = channels * (LMAX + 1)
     share = depth // (2 * columns)
     padded = -(-(share + 2) // 16) * 16
     partial = jax.ShapeDtypeStruct((columns, padded, depth), bf16)
-    grad_rows, mine, theirs, every = pl.pallas_call(
-        functools.partial(backward_kernel, half.shape[0]),
+    grad_conv, mine, theirs = pl.pallas_call(
+        backward_kernel,
         out_shape=(
-            jax.ShapeDtypeStruct((edge_rows, REDUCED * channels), bf16),
+            jax.ShapeDtypeStruct((REDUCED * channels, edge_rows), bf16),
             partial,
             partial,
-            jax.ShapeDtypeStruct((group, head_count, channels), f32),
         ),
         in_specs=[smem] + [VMEM] * 10,
-        out_specs=[VMEM] * 4,
+        out_specs=[VMEM] * 3,
         scratch_shapes=[
             wide,
             pltpu.VMEM(field, f32),
@@ -592,7 +615,7 @@
             pltpu.VMEM((depth + padded, depth), f32),
         ],
         compiler_params=PARAMS,
-    )(first, ids, stats, received, scalar, per_edge, rotation, grad_edge, attention, attention_t, z)
+    )(first, ids, stats, every, scalar, per_edge, rotation, grad_edge, attention, attention_t, z)
 
     theirs = lax.ppermute(theirs, "core", [(0, 1), (1, 0)])
     mine = (mine.astype(f32) + theirs.astype(f32)).astype(bf16)
@@ -604,16 +627,24 @@
     lanes = whole_lanes(inner)
     zero_send = jnp.pad(zero_send, ((0, 0), (0, 0), (0, lanes - inner)))
     zero_send = zero_send.reshape(group, share * lanes // LANES, LANES)
-    att_send = jnp.broadcast_to(
-        att_flat.reshape(1, head_count, channels), (group, head_count, channels)
-    )
-    last_rows = jnp.concatenate([zero_send, att_send], axis=1).astype(bf16)
-    rest = -last_rows.shape[1] % 16
-    last_rows = jnp.pad(last_rows, ((0, 0), (0, rest), (0, 0)))
-
+    att = att_flat.reshape(head_count, channels)
+    spare = lanes - channels // 2
+    beside = spare >= max(inner, channels // 2) and share >= 2 * head_count
+    if beside:
+        att = jnp.pad(att.reshape(2 * head_count, -1), ((0, share - 2 * head_count), (spare, 0)))
+        last_rows = zero_send + att[None]
+    else:
+        att = jnp.broadcast_to(att[None], (group, head_count, channels))
+        last_rows = jnp.concatenate([zero_send, att], axis=1)
+    last_rows = last_rows.astype(bf16)
+
+    used = harmonics * row_count
+    zero_rows = share * lanes // LANES
     grad_sums = pl.pallas_call(
         functools.partial(scatter_kernel, places, group, row_count),
-        out_shape=jax.ShapeDtypeStruct((group, span + last_rows.shape[1], channels), bf16),
+        out_shape=jax.ShapeDtypeStruct(
+            (group, -(-(used + last_rows.shape[1]) // 16) * 16, channels), bf16
+        ),
         in_specs=[smem] + [VMEM] * 3 + [ANY] * 2,
         out_specs=VMEM,
         scratch_shapes=[
@@ -621,38 +652,34 @@
             wide,
             pltpu.VMEM((REDUCED,) + field, f32),
             pltpu.VMEM((COEF,) + field, bf16),
+            pltpu.VMEM((REDUCED * channels, edge_rows), f32),
+            pltpu.VMEM((edge_rows, REDUCED * channels), bf16),
             copies,
         ],
         compiler_params=PARAMS,
-    )(first, ids, grad_rows, rotation, half, other)
-    grad_sums = lax.dynamic_update_slice(grad_sums, last_rows, (0, span, 0))
+    )(first, ids, grad_conv, rotation, half, other)
+    grad_sums = lax.dynamic_update_slice(grad_sums, last_rows, (0, used, 0))
     last = exchange(grad_sums, GRAPH)
 
-    def sum_parts(parts, scale):
-        return pl.pallas_call(
-            sum_kernel,
-            out_shape=(
-                jax.ShapeDtypeStruct((row_count, harmonics, channels), bf16),
-                jax.ShapeDtypeStruct((parts.shape[1] - span, channels), f32),
-            ),
-            in_specs=[VMEM] * 2,
-            out_specs=[VMEM] * 2,
-            scratch_shapes=[pltpu.VMEM((span, channels), f32)],
-            compiler_params=PARAMS,
-        )(parts, scale)
-
-    sums = lax.dynamic_slice_in_dim(every, own_first, row_count, axis=2)
-    sums = jnp.transpose(sums, (0, 2, 1))
-    total = jnp.sum(sums, axis=0)
-    own_shares = jnp.where(present, sums / jnp.where(total > 0.0, total, 1.0), 0.0)
-    scale = per_channel(own_shares.reshape(-1, head_count), channels)
-    scale = jnp.tile(scale.reshape(group, row_count, channels), (1, 8 // row_count, 1))
-    update, _ = sum_parts(received, scale)
-    grad_nodes, tail = sum_parts(last, jnp.ones_like(scale))
-    tail = tail * (1.0 / (2 * columns))
-    zero_rows = share * lanes // LANES
+    grad_nodes, total = pl.pallas_call(
+        sum_kernel,
+        out_shape=(
+            jax.ShapeDtypeStruct((row_count, harmonics, channels), bf16),
+            jax.ShapeDtypeStruct(last.shape[1:], f32),
+        ),
+        in_specs=[VMEM],
+        out_specs=[VMEM] * 2,
+        compiler_params=PARAMS,
+    )(last)
+    tail = total[used : used + last_rows.shape[1]] * (1.0 / (2 * columns))
     grad_zero = tail[:zero_rows].reshape(share, lanes)[:, :inner].T
-    grad_att = tail[zero_rows : zero_rows + head_count].T
+    if beside:
+        grad_att = tail[: 2 * head_count, spare:].reshape(head_count, channels).T
+    else:
+        grad_att = tail[zero_rows:].T
+    update = summed[0, :used].reshape(harmonics, row_count, channels)
+    update = jnp.where(present[None], update, jnp.zeros_like(update))
+    update = jnp.transpose(update, (1, 0, 2))
 
     shape = (1, row_count, harmonics, channels)
     return (update.reshape(shape), grad_nodes.reshape(shape), grad_zero, grad_att)

time: 233 us -> 236 us (1.013)
  the two profiles are of different devices: /device:TPU:1 before, /device:TPU:68 now
where the time goes in v2:
time: 236 us; the launch traced here: 235 us
  waiting for transfers between devices  92.9 us (39%)
  blocking collectives  45.9 us (19%)
  starting transfers between devices  33.8 us (14%)
  local copies, waits for them, and re-layouts  22.6 us (10%)
  Pallas kernels  19.7 us (8%)
  between operations  15.8 us (7%)
  other arithmetic  4.28 us (2%)
    reduce_scatter x1, waiting for transfers between devices, on_device(): lax.psum_scatter(shared_sums, GRAPH, scatter_dimension=0, tiled=True)  48.7 us
    all_to_all x1, blocking collectives, gather(): return lax.all_to_all(copies, axes, split_axis=0, concat_axis=0, tiled=True)  44.1 us
    all_to_all x2, waiting for transfers between devices, gather(): return lax.all_to_all(copies, axes, split_axis=0, concat_axis=0, tiled=True)  24.9 us
    all_to_all x2, starting transfers between devices, gather(): return lax.all_to_all(copies, axes, split_axis=0, concat_axis=0, tiled=True)  17.7 us
    all_to_all x2, waiting for transfers between devices, exchange(): return lax.all_to_all(blocks, axes, split_axis=0, concat_axis=0, tiled=True)  14.7 us
    all_to_all x2, starting transfers between devices, exchange(): return lax.all_to_all(blocks, axes, split_axis=0, concat_axis=0, tiled=True)  12.2 us
    unnamed x34, local copies, waits for them, and re-layouts  11.4 us
    pallas_call x1, Pallas kernels, on_device(): pl.pallas_call(functools.partial(forward_kernel, places, group), out_shap...  7.25 us
  transfers between devices with their start and end apart: 8, of which 6 were waited for; matrix products, arithmetic and copies ran while one was open for 3% of the time, Pallas kernels for 4%

profile of v2, /device:TPU:68, one launch (start us, length us, event | category | flops | bytes accessed | tf_op | source)
XLA Modules:
  0.0 235.0 jit_solution(12650826125643763839)
XLA Ops:
  10.3 0.8 copy.34.refs_0_
  11.3 1.8 all-gather
  13.1 0.9 broadcast_in_dim.46
  14.1 10.2 %all-to-all-start = ((bf16[32,64,128]{2,1,0:T(8,128)(2,1)}), bf16[32,64,128]{2,1,0:T(8,128)(2,1)S(1)}, u32[]{:S(2)}, u32[]{:S(2)}) async-start(bf16[32,64,128]{2,1,0:T(8,128)(2,1)} %broadcast_in_dim.46), calls=%async_computation | async-start | bytes 1048576 | tf_op jit(solution)/shard_map/all_to_all | solution.py:32
  25.0 16.0 %all-to-all-done = bf16[32,64,128]{2,1,0:T(8,128)(2,1)S(1)} async-done(((bf16[32,64,128]{2,1,0:T(8,128)(2,1)}), bf16[32,64,128]{2,1,0:T(8,128)(2,1)S(1)}, u32[]{:S(2)}, u32[]{:S(2)}) %all-to-all-start) | async-done | bytes 524320 | tf_op jit(solution)/shard_map/all_to_all | solution.py:32
  44.7 0.8 fusion.3
  46.1 44.1 %all_to_all.25 = bf16[16,4,12544]{2,1,0:T(4,128)(2,1)S(1)} all-to-all(bf16[16,4,12544]{2,1,0:T(4,128)(2,1)S(1)} %broadcast_in_dim.49), channel_id=1, replica_groups=mesh['xh'=2,'z'=8,'core'=2,'y'=8,'xl'=2] {'y','xl'}, dimensions={0} | all-to-all | bytes 3211264 | tf_op jit(solution)/shard_map/all_to_all | solution.py:32
  90.2 1.4 reshape.78.nodes
  91.6 1.9 collective-permute-start
  94.5 1.4 copy-done.1
  95.9 1.7 shard_map.157
  97.6 1.4 collective-permute-done.other
  99.1 7.2 %shard_map.158 = (bf16[16,208,128]{2,1,0:T(8,128)(2,1)S(1)}, f32[8,128]{1,0:T(8,128)S(1)}, f32[128,128]{1,0:T(8,128)S(1)}, f32[16,128]{1,0:T(8,128)S(1)}) custom-call(s32[1,1]{1,0:T(1,128)} %bitcast.1.first, s32[8,128]{1,0:T(8,128)S(1)} %stack.8.ids, bf16[29,128,128]{2,1,0:T(8,128)(2,1)S(1)} %get-tuple-element.22.z, bf16[29,49,128]{2,1,0:T(8,128)(2,1)S(1)} %bitcast.64, ...), custom_call_target="tpu_custom_call" | custom-call | tf_op jit(solution)/shard_map/pallas_call | solution.py:565
  106.3 0.9 copy-done.5
  107.9 7.5 %all-to-all-start.2 = ((f32[16,8,128]{2,1,0:T(8,128)}), f32[16,8,128]{2,1,0:T(8,128)S(1)}, u32[]{:S(2)}, u32[]{:S(2)}) async-start(f32[16,8,128]{2,1,0:T(8,128)} %broadcast_in_dim.50), calls=%async_computation.2 | async-start | bytes 131072 | tf_op jit(solution)/shard_map/all_to_all | solution.py:32
  115.5 8.9 %all-to-all-done.2.every = f32[16,8,128]{2,1,0:T(8,128)S(1)} async-done(((f32[16,8,128]{2,1,0:T(8,128)}), f32[16,8,128]{2,1,0:T(8,128)S(1)}, u32[]{:S(2)}, u32[]{:S(2)}) %all-to-all-start.2) | async-done | bytes 65568 | tf_op jit(solution)/shard_map/all_to_all | solution.py:32
  124.4 1.2 copy-done.6
  125.8 1.0 copy-done.2
  126.7 2.9 %shard_map.160 = (bf16[3712,128]{1,0:T(8,128)(2,1)S(1)}, bf16[16,32,896]{2,1,0:T(8,128)(2,1)S(1)}, bf16[16,32,896]{2,1,0:T(8,128)(2,1)S(1)}) custom-call(s32[1,1]{1,0:T(1,128)} %bitcast.1.first, s32[8,128]{1,0:T(8,128)S(1)} %stack.8.ids, f32[8,128]{1,0:T(8,128)S(1)} %get-tuple-element.25.stats, f32[16,8,128]{2,1,0:T(8,128)S(1)} %all-to-all-done.2.every, ...), custom_call_target="tpu_custom_call" | custom-call | tf_op jit(solution)/shard_map/pallas_call | solution.py:602
  129.6 0.9 copy-done.3
  130.6 1.9 collective-permute-start.1
  132.5 2.4 %collective-permute-done.1 = bf16[16,32,896]{2,1,0:T(8,128)(2,1)S(1)} collective-permute-done((bf16[16,32,896]{2,1,0:T(8,128)(2,1)S(1)}, bf16[16,32,896]{2,1,0:T(8,128)(2,1)S(1)}, u32[]{:S(2)}, u32[]{:S(2)}) %collective-permute-start.1) | collective-permute-done | bytes 917536 | tf_op jit(solution)/shard_map/ppermute | solution.py:620
  134.9 1.2 add_convert_fusion
  136.2 8.6 %all-to-all-start.3 = ((bf16[16,32,896]{2,1,0:T(8,128)(2,1)}), bf16[16,32,896]{2,1,0:T(8,128)(2,1)}, u32[]{:S(2)}, u32[]{:S(2)}) async-start(bf16[16,32,896]{2,1,0:T(8,128)(2,1)} %add_convert_fusion), calls=%async_computation.4 | async-start | bytes 1835008 | tf_op jit(solution)/shard_map/all_to_all | solution.py:36
  145.5 1.2 copy-done.4
  146.7 7.2 %shard_map.161 = bf16[16,224,128]{2,1,0:T(8,128)(2,1)} custom-call(s32[1,1]{1,0:T(1,128)} %bitcast.1.first, s32[8,128]{1,0:T(8,128)S(1)} %stack.8.ids, bf16[3712,128]{1,0:T(8,128)(2,1)S(1)} %copy-done.4, bf16[29,49,128]{2,1,0:T(8,128)(2,1)S(1)} %bitcast.66, bf16[8,1376,128]{2,1,0:T(8,128)(2,1)S(1)} %bitcast.62, bf16[8,1376,128]{2,1,0:T(8,128)(2,1)} %collective-permute-done.other), custom_call_target="tpu_custom_call" | custom-call | tf_op jit(solution)/shard_map/pallas_call | solution.py:643
  153.9 14.7 %all-to-all-done.3 = bf16[16,32,896]{2,1,0:T(8,128)(2,1)} async-done(((bf16[16,32,896]{2,1,0:T(8,128)(2,1)}), bf16[16,32,896]{2,1,0:T(8,128)(2,1)}, u32[]{:S(2)}, u32[]{:S(2)}) %all-to-all-start.3) | async-done | bytes 917536 | tf_op jit(solution)/shard_map/all_to_all | solution.py:36
  168.6 1.3 convert_reduce_fusion
  170.4 1.7 dynamic_update_slice.3
  172.1 3.6 %all-to-all-start.4 = ((bf16[16,224,128]{2,1,0:T(8,128)(2,1)}), bf16[16,224,128]{2,1,0:T(8,128)(2,1)S(1)}, u32[]{:S(2)}, u32[]{:S(2)}) async-start(bf16[16,224,128]{2,1,0:T(8,128)(2,1)} %dynamic_update_slice.3), calls=%async_computation.5 | async-start | bytes 1835008 | tf_op jit(solution)/shard_map/all_to_all | solution.py:36
  175.7 48.7 %reduce-scatter.2.cloned.1.call-done = bf16[1,208,128]{2,1,0:T(8,128)(2,1)} async-done(((bf16[16,208,128]{2,1,0:T(8,128)(2,1)}), bf16[1,208,128]{2,1,0:T(8,128)(2,1)}) %reduce-scatter.2.cloned.1.call-update) | async-done | bytes 53264 | tf_op jit(solution)/shard_map/reduce_scatter | solution.py:595
  224.4 0.8 slice.57
  (77 shorter events, 12.7 us)
Async XLA Ops:
  14.1 27.0 %all-to-all-start = ((bf16[32,64,128]{2,1,0:T(8,128)(2,1)}), bf16[32,64,128]{2,1,0:T(8,128)(2,1)S(1)}, u32[]{:S(2)}, u32[]{:S(2)}) async-start(bf16[32,64,128]{2,1,0:T(8,128)(2,1)} %broadcast_in_dim.46), calls=%async_computation | async-start | bytes 1048576 | tf_op jit(solution)/shard_map/all_to_all | solution.py:32
  24.3 67.3 %all-gather.4.cloned.1.call-start = ((), (), s32[]{:S(2)}) async-start(), calls=%async_computation.7 | async-start | bytes 3170304 | tf_op jit(solution)/shard_map/all_gather | solution.py:498
  43.7 1.9 copy-start.9
  44.1 1.6 copy-start.10
  90.2 4.0 %copy-start.8 = (bf16[1,29,49,128]{3,1,2,0:T(8,128)(2,1)S(1)}, bf16[1,29,49,128]{3,1,2,0:T(8,128)(2,1)}, u32[]{:S(2)}) copy-start(bf16[1,29,49,128]{3,1,2,0:T(8,128)(2,1)} %param.18) | copy-start | bytes 1091332
  90.2 4.2 %copy-start.11 = (s32[1,128]{1,0:T(1,128)S(1)}, s32[1,128]{1,0:T(1,128)}, u32[]{:S(2)}) copy-start(s32[1,128]{1,0:T(1,128)} %param.16) | copy-start | bytes 1540
  90.2 4.2 %copy-start.12 = (s32[1,128]{1,0:T(1,128)S(1)}, s32[1,128]{1,0:T(1,128)}, u32[]{:S(2)}) copy-start(s32[1,128]{1,0:T(1,128)} %param.17) | copy-start | bytes 1540
  91.6 7.4 %copy-start.7 = (bf16[128,8]{0,1:T(8,128)(2,1)S(1)}, bf16[128,8]{0,1:T(8,128)(2,1)}, u32[]{:S(2)}) copy-start(bf16[128,8]{0,1:T(8,128)(2,1)} %param.25) | copy-start | bytes 6148
  91.6 7.4 %collective-permute-start = (bf16[8,1376,128]{2,1,0:T(8,128)(2,1)}, bf16[8,1376,128]{2,1,0:T(8,128)(2,1)}, u32[]{:S(2)}, u32[]{:S(2)}) collective-permute-start(bf16[8,1376,128]{2,1,0:T(8,128)(2,1)} %bitcast.60), channel_id=1, source_target_pairs={{0,16},{16,0},{1,17},{17,1},{2,18},{18,2},{3,19},{19,3},{4,20},{20... | collective-permute-start | bytes 8454152 | tf_op jit(solution)/shard_map/ppermute | solution.py:545
  94.4 1.4 copy-start.1
  106.3 0.9 copy-start.5
  107.9 16.5 %all-to-all-start.2 = ((f32[16,8,128]{2,1,0:T(8,128)}), f32[16,8,128]{2,1,0:T(8,128)S(1)}, u32[]{:S(2)}, u32[]{:S(2)}) async-start(f32[16,8,128]{2,1,0:T(8,128)} %broadcast_in_dim.50), calls=%async_computation.2 | async-start | bytes 131072 | tf_op jit(solution)/shard_map/all_to_all | solution.py:32
  124.4 1.2 copy-start.6
  125.8 1.0 copy-start.2
  129.6 0.9 copy-start.3
  130.6 4.4 %collective-permute-start.1 = (bf16[16,32,896]{2,1,0:T(8,128)(2,1)S(1)}, bf16[16,32,896]{2,1,0:T(8,128)(2,1)S(1)}, u32[]{:S(2)}, u32[]{:S(2)}) collective-permute-start(bf16[16,32,896]{2,1,0:T(8,128)(2,1)S(1)} %get-tuple-element.33), channel_id=1, source_target_pairs={{0,16},{16,0},{1,17},{17,1},{2,18},{18,2},{3,19},{19,3},{4,20},{20... | collective-permute-start | bytes 2752520 | tf_op jit(solution)/shard_map/ppermute | solution.py:620
  134.9 10.6 %copy-start = (bf16[11008,128]{1,0:T(8,128)(2,1)S(1)}, bf16[11008,128]{1,0:T(8,128)(2,1)}, u32[]{:S(2)}) copy-start(bf16[11008,128]{1,0:T(8,128)(2,1)} %all-gather.4.cloned.1.call-done) | copy-start | bytes 8454148
  136.2 32.4 %all-to-all-start.3 = ((bf16[16,32,896]{2,1,0:T(8,128)(2,1)}), bf16[16,32,896]{2,1,0:T(8,128)(2,1)}, u32[]{:S(2)}, u32[]{:S(2)}) async-start(bf16[16,32,896]{2,1,0:T(8,128)(2,1)} %add_convert_fusion), calls=%async_computation.4 | async-start | bytes 1835008 | tf_op jit(solution)/shard_map/all_to_all | solution.py:36
  144.7 79.7 %reduce-scatter.2.cloned.1.call-start = ((), (), s32[]{:S(2)}) async-start(), calls=%async_computation.6 | async-start | bytes 905216 | tf_op jit(solution)/shard_map/reduce_scatter | solution.py:595
  145.5 1.2 copy-start.4
  172.1 53.9 %all-to-all-start.4 = ((bf16[16,224,128]{2,1,0:T(8,128)(2,1)}), bf16[16,224,128]{2,1,0:T(8,128)(2,1)S(1)}, u32[]{:S(2)}, u32[]{:S(2)}) async-start(bf16[16,224,128]{2,1,0:T(8,128)(2,1)} %dynamic_update_slice.3), calls=%async_computation.5 | async-start | bytes 1835008 | tf_op jit(solution)/shard_map/all_to_all | solution.py:36
Sparse Core Ops, SparseCore 0:
  45.6 45.9 all-gather.3
  148.4 75.9 reduce-scatter.1

commit v3 on v2

--- a/solution.py
+++ b/solution.py
@@ -85,26 +85,32 @@
     return pl.ds(pl.multiple_of(k * LANES + start, CHUNK), CHUNK)
 
 
-def copy_weights(first, mine, other, held, sems):
-    def go(low, high):
-        one = pltpu.make_async_copy(low, held.at[0], sems.at[0])
-        two = pltpu.make_async_copy(high, held.at[1], sems.at[1])
-        one.start()
-        two.start()
-        one.wait()
-        two.wait()
+def start_weights(places, first, mine, other, held, sems):
+    def go(halves):
+        for i, (half, at, rows, tiles) in enumerate(places):
+            span = pl.ds(at, tiles * rows)
+            pltpu.make_async_copy(
+                halves[half].at[:, span, :], held.at[half, :, span, :], sems.at[i]
+            ).start()
 
     @pl.when(first == 0)
     def _():
-        go(mine, other)
+        go((mine, other))
 
     @pl.when(first != 0)
     def _():
-        go(other, mine)
+        go((other, mine))
+
+
+def wait_weights(places, which, mine, held, sems):
+    for i in which:
+        half, at, rows, tiles = places[i]
+        span = pl.ds(at, tiles * rows)
+        pltpu.make_async_copy(mine.at[:, span, :], held.at[half, :, span, :], sems.at[i]).wait()
 
 
 def map_tiles(held, place, tiles):
-    half, at, rows = place
+    half, at, rows, _ = place
     parts = []
     for t in tiles:
         part = held[half, :, at + t * rows : at + (t + 1) * rows, :]
@@ -126,7 +132,7 @@
             out[to : to + size, :] = blocks[at : at + size, :]
 
 
-def by_owner(target, turned, out, group):
+def by_owner(target, turned, out, group, scale=None):
     channels = turned.shape[1]
     own = target.shape[0] // group
     per = 16 // own
@@ -135,6 +141,7 @@
         for j in range(first, first + per):
             if j < COEF:
                 part = nt_dot(target, turned[j])
+                part = part if scale is None else part * scale
             else:
                 part = jnp.zeros((target.shape[0], channels), f32)
             parts.append(part.reshape(group, 1, own, channels))
@@ -146,41 +153,78 @@
     shards, out, acc = refs[:-2], refs[-2], refs[-1]
     acc[...] = jnp.zeros_like(acc)
     for shard, at in zip(shards, places):
-        rows, columns = shard.shape
+        columns, rows = shard.shape
         lane = lax.broadcasted_iota(jnp.int32, (rows, acc.shape[1]), 1)
         row = lax.broadcasted_iota(jnp.int32, (rows, acc.shape[1]), 0)
-        place = (lane == row + at).astype(bf16)
-        acc[:columns, :] += lax.dot_general(
-            shard[...], place, (((0,), (0,)), ((), ())), preferred_element_type=f32
-        )
+        acc[:columns, :] += half_dot(shard[...], (lane == row + at).astype(bf16))
     out[...] = acc[...].astype(bf16)
 
 
-def share_kernel(stats, every, message, out):
-    group = message.shape[0]
+def slab_kernel(sets, first, slabs, out):
+    group, most, lanes = slabs.shape[0] // 2, slabs.shape[1] // 2, slabs.shape[2]
+    blocks = [jnp.concatenate([slabs[g], slabs[group + g]], axis=0) for g in range(group)]
+
+    def lay(which):
+        to = 0
+        for rows, columns, at in which:
+            size = 4 * columns
+            row = lax.broadcasted_iota(jnp.int32, (size, 4 * most), 0)
+            lane = lax.broadcasted_iota(jnp.int32, (size, 4 * most), 1)
+            kept = row // columns * most + row % columns
+            chosen = (lane == kept).astype(bf16)
+            source = lax.broadcasted_iota(jnp.int32, (lanes, LANES), 0)
+            place = lax.broadcasted_iota(jnp.int32, (lanes, LANES), 1)
+            for t in range(group * rows // LANES):
+                acc = None
+                for g in range(group):
+                    if g * rows >= (t + 1) * LANES or (g + 1) * rows <= t * LANES:
+                        continue
+                    shift = g * rows - t * LANES - at
+                    hit = (place == source + shift) & (source >= at) & (source < at + rows)
+                    term = half_dot(blocks[g], hit.astype(bf16))
+                    acc = term if acc is None else acc + term
+                tile = half_dot(chosen, acc.astype(bf16))
+                out[to : to + size, :] = tile.astype(bf16)
+                to += size
+        if to < out.shape[0]:
+            out[to:, :] = jnp.zeros((out.shape[0] - to, LANES), bf16)
+
+    @pl.when(first[0, 0] == 0)
+    def _():
+        lay(sets[0])
+
+    @pl.when(first[0, 0] != 0)
+    def _():
+        lay(sets[1])
+
+
+def message_kernel(ids, stats, every, msg, out):
+    group = out.shape[0]
     count = stats.shape[1] // 2
     total = jnp.sum(every[:, :, :count], axis=0)
     share = stats[:, :count] / jnp.where(total > 0.0, total, 1.0)
-    scale = widen(share, LANES).T.reshape(group, 1, count // group, LANES)
-    per = 16 * group // count
-    scale = jnp.broadcast_to(scale, (group, per, count // group, LANES)).reshape(group, 16, LANES)
-    for at in range(0, message.shape[1], 16):
-        part = message[:, at : at + 16, :].astype(f32) * scale
-        out[:, at : at + 16, :] = part.astype(bf16)
-
-
-def rotate_kernel(ids, nodes, wigner, z, grad_edge, paired, wide):
-    count, edges = nodes.shape[0], wigner.shape[2]
+    scale = widen(share, LANES).T
+    by_owner(hot_rows(ids[1:2, :], count).astype(bf16), msg, out, group, scale)
+
+
+def rotate_kernel(own, ids, nodes, wigner, z, grad_edge, paired, wide):
+    group, edges = nodes.shape[0], wigner.shape[2]
     channels = LANES
+    per = 16 // (2 * own)
+    count = own * group
     target = hot_rows(ids[1:2, :], count)
     both = (target + hot_rows(ids[0:1, :], count)).astype(bf16)
     target = target.astype(bf16)
     wide[...] = wigner[...].astype(f32)
-    for j in range(COEF):
-        at = slice(j * channels, (j + 1) * channels)
-        paired[j] = half_dot(nodes[:, at].T, both).astype(bf16).astype(f32)
-        at = slice((COEF + j) * channels, (COEF + j + 1) * channels)
-        grad_edge[j] = half_dot(nodes[:, at].T, target).astype(bf16)
+    for first in range(0, COEF, per):
+        rows = nodes[:, first * 2 * own : first * 2 * own + 16, :].astype(f32)
+        rows = rows.reshape(group, 2 * per, own, channels)
+        for j in range(first, min(first + per, COEF)):
+            at = 2 * (j - first)
+            here = rows[:, at].reshape(count, channels).T.astype(bf16)
+            paired[j] = half_dot(here, both).astype(bf16).astype(f32)
+            here = rows[:, at + 1].reshape(count, channels).T.astype(bf16)
+            grad_edge[j] = half_dot(here, target).astype(bf16)
     for l in range(LMAX + 1):
         for k in ROWS_OF[l]:
             acc = None
@@ -201,8 +245,9 @@
     attention_t,
     mine,
     other,
-    message,
+    messages,
     stats,
+    sent,
     scalar,
     per_edge,
     held,
@@ -212,20 +257,23 @@
     msg,
     heads_acc,
     sems,
+    out_sem,
 ):
     channels, edges = LANES, wigner.shape[2]
     heads = attention_t.shape[0]
     count = stats.shape[1] // 2
-    copy_weights(first[0, 0], mine, other, held, sems)
+    start_weights(places, first[0, 0], mine, other, held, sems)
     wide[...] = wigner[...].astype(f32)
     base, rows = ZERO
     acc = None
+    wait_weights(places, (0,), mine, held, sems)
     for tiles in pairs(rows):
         right = z[tiles[0] : tiles[-1] + 1].reshape(-1, edges)
         term = half_dot(map_tiles(held, places[0], tiles), right)
         acc = term if acc is None else acc + term
     spread(acc, held, places[0][2], base, y)
     for (base, rows), real, imag in ((ONE, places[1], places[2]), (TWO, places[3], places[4])):
+        wait_weights(places, (1, 2) if base == ONE[0] else (3, 4), mine, held, sems)
         acc = None
         for tiles in pairs(rows):
             lo, hi = base + tiles[0], base + tiles[-1] + 1
@@ -265,12 +313,17 @@
         heads_acc[at, :] = total
 
     chunks(channels, body)
+    copy = pltpu.make_async_copy(msg, messages, out_sem.at[0])
+    copy.start()
     grad_norm = jnp.sum(heads_acc[...].reshape(heads, channels // heads, edges), axis=1)
     own_shared = nt_full(own_norm * grad_norm, target)
-    stats[...] = jnp.concatenate([own_sum, own_shared], axis=1)
+    sums = jnp.concatenate([own_sum, own_shared], axis=1)
+    stats[...] = sums
+    for owner in range(group):
+        sent[owner] = sums
     per_edge[:heads, :] = own_norm
     per_edge[heads:, :] = grad_norm
-    by_owner(target.astype(bf16), msg, message, group)
+    copy.wait()
 
 
 def backward_kernel(
@@ -285,13 +338,15 @@
     attention,
     attention_t,
     z,
-    grad_conv,
+    grad_out,
     mine,
     theirs,
     wide,
     norm,
     grad,
     turned,
+    grad_conv,
+    out_sem,
 ):
     channels, edges = LANES, wigner.shape[2]
     heads = attention_t.shape[0]
@@ -333,6 +388,8 @@
     depth = (LMAX + 1) * channels
     parts, share = mine.shape[0], depth // (2 * mine.shape[0])
     grad_conv[...] = grad[...].astype(bf16)
+    copy = pltpu.make_async_copy(grad_conv, grad_out, out_sem.at[0])
+    copy.start()
     turned[:depth, :] = nt_dot(grad_conv[:depth, :], z[: LMAX + 1].reshape(depth, edges))
     turned[depth:, :] = jnp.zeros((turned.shape[0] - depth, depth), f32)
     padded = mine.shape[1]
@@ -357,6 +414,8 @@
     @pl.when(first[0, 0] != 0)
     def _():
         store((theirs, mine))
+
+    copy.wait()
 
 
 def scatter_kernel(
@@ -380,7 +439,7 @@
 ):
     channels, edges = LANES, wigner.shape[2]
     count = own * group
-    copy_weights(first[0, 0], mine, other, held, sems)
+    start_weights(places, first[0, 0], mine, other, held, sems)
     wide[...] = wigner[...].astype(f32)
     grad[...] = grad_conv[...].astype(f32)
     zs = held.shape[1]
@@ -398,11 +457,13 @@
             grad_rows[:, to : to + channels] = ordered[at, :].T.astype(bf16)
     base, rows = ZERO
     left = grad_rows[:, : rows * channels]
+    wait_weights(places, (0,), mine, held, sems)
     for tiles in pairs(rows):
         out = half_dot(left, map_tiles(held, places[0], tiles)).astype(bf16).astype(f32)
         for i, t in enumerate(tiles):
             dz[t] = out[:, i * channels : (i + 1) * channels].T
     for (base, rows), real, imag in ((ONE, places[1], places[2]), (TWO, places[3], places[4])):
+        wait_weights(places, (1, 2) if base == ONE[0] else (3, 4), mine, held, sems)
         plus = grad_rows[:, base * channels : (base + rows) * channels]
         minus = grad_rows[:, (base + rows) * channels : (base + 2 * rows) * channels]
         left = jnp.concatenate([plus, minus], axis=0)
@@ -435,14 +496,15 @@
     return -(-COEF * own // 16) * 16
 
 
-def sum_kernel(parts, nodes, total):
-    group, own = parts.shape[0], nodes.shape[0]
+def sum_kernel(parts, nodes, tail, total):
+    group = parts.shape[0]
     acc = parts[0].astype(f32)
     for g in range(1, group):
         acc = acc + parts[g].astype(f32)
     total[...] = acc
-    for n in range(own):
-        nodes[n] = total[pl.ds(n, COEF, stride=own), :].astype(bf16)
+    used = nodes.shape[0] * nodes.shape[1]
+    nodes[...] = acc[:used].astype(bf16).reshape(nodes.shape)
+    tail[...] = total[used : used + tail.shape[0], :]
 
 
 def pad_to(block, rows, columns):
@@ -451,12 +513,6 @@
 
 def whole_lanes(count):
     return -(-count // LANES) * LANES
-
-
-def column_tiles(block):
-    rows, columns = block.shape
-    tiles = block.reshape(rows, columns // LANES, LANES)
-    return jnp.transpose(tiles, (1, 0, 2)).reshape(-1, LANES)
 
 
 def gather_weights(shards):
@@ -476,33 +532,30 @@
         out_specs=VMEM,
         scratch_shapes=[pltpu.VMEM((most, 2 * lanes), f32)],
         compiler_params=PARAMS,
-    )(*shards)
+    )(*[w.T for w in shards])
+    core = lax.axis_index("core")
     near = lax.all_gather(packed, "core")
-    core = lax.axis_index("core")
-    first = core == 0
     sent = lax.dynamic_slice_in_dim(near, core * lanes, lanes, axis=2)
     slabs = gather(sent.reshape(2 * most, lanes), ROW_GROUP)
-    pieces = slabs.reshape(2, -1, 2, most, lanes)
-    whole = [r * pieces.shape[1] for r in rows]
-    tiled = []
-    for s in sets:
-        at, parts = 0, []
-        for i in s:
-            piece = pieces[:, :, :, : columns[i], at : at + rows[i]]
-            at += rows[i]
-            piece = jnp.transpose(piece, (0, 2, 3, 1, 4)).reshape(4 * columns[i], whole[i])
-            parts.append(column_tiles(piece))
-        tiled.append(jnp.concatenate(parts, axis=0))
-    depth = max(t.shape[0] for t in tiled)
-    tiled = [pad_to(t, depth, LANES) for t in tiled]
-    half = lax.all_gather(jnp.where(first, tiled[0], tiled[1]), "z")
+    group = slabs.shape[0] // 2
     places = [None] * len(shards)
+    depth = 0
     for half_index, s in enumerate(sets):
         at = 0
         for i in s:
-            places[i] = (half_index, at, 4 * columns[i])
-            at += whole[i] // LANES * 4 * columns[i]
-    return half, places, slabs
+            tiles = group * rows[i] // LANES
+            places[i] = (half_index, at, 4 * columns[i], tiles)
+            at += tiles * 4 * columns[i]
+        depth = max(depth, at)
+    kinds = [[(rows[i], columns[i], starts[i] - n * lanes) for i in s] for n, s in enumerate(sets)]
+    tiled = pl.pallas_call(
+        functools.partial(slab_kernel, kinds),
+        out_shape=jax.ShapeDtypeStruct((depth, LANES), bf16),
+        in_specs=[pl.BlockSpec(memory_space=pltpu.SMEM), VMEM],
+        out_specs=VMEM,
+        compiler_params=PARAMS,
+    )(core.astype(jnp.int32).reshape(1, 1), slabs)
+    return lax.all_gather(tiled, "z"), places, tiled
 
 
 def on_device(
@@ -520,7 +573,7 @@
     w_two_imag,
     attention,
 ):
-    half, places, slabs = gather_weights((w_zero, w_one_real, w_one_imag, w_two_real, w_two_imag))
+    half, places, tiled = gather_weights((w_zero, w_one_real, w_one_imag, w_two_real, w_two_imag))
     row_count = embeddings.shape[1]
     harmonics = embeddings.shape[2]
     channels = embeddings.shape[3]
@@ -537,10 +590,12 @@
     first = core.astype(jnp.int32).reshape(1, 1)
     own_first = lax.axis_index(GRAPH) * row_count
     present = ((own_first + lax.iota(jnp.int32, row_count)) < atom_counts[0])[:, None]
-    cot_rows = jnp.where(present, cotangent[0].reshape(row_count, width), 0.0).astype(bf16)
-    own_rows = jnp.concatenate([embeddings[0].reshape(row_count, width), cot_rows], axis=1)
-    own_rows, slabs = lax.optimization_barrier((own_rows, slabs))
-    nodes = gather(own_rows, GRAPH).reshape(all_nodes, 2 * width)
+    cot_rows = jnp.where(present[:, :, None], cotangent[0], 0.0).astype(bf16)
+    own_rows = jnp.stack([embeddings[0], cot_rows])
+    own_rows = jnp.transpose(own_rows, (2, 0, 1, 3)).reshape(-1, channels)
+    own_rows = pad_to(own_rows, -(-own_rows.shape[0] // 16) * 16, channels)
+    own_rows, tiled = lax.optimization_barrier((own_rows, tiled))
+    nodes = gather(own_rows, GRAPH)
     half, nodes = lax.optimization_barrier((half, nodes))
     other = lax.ppermute(half, "core", [(0, 1), (1, 0)])
 
@@ -548,7 +603,7 @@
     field = (channels, edge_rows)
     wide = pltpu.VMEM(rotation.shape, f32)
     z, grad_edge = pl.pallas_call(
-        rotate_kernel,
+        functools.partial(rotate_kernel, row_count),
         out_shape=(
             jax.ShapeDtypeStruct((REDUCED,) + field, bf16),
             jax.ShapeDtypeStruct((COEF,) + field, bf16),
@@ -559,19 +614,22 @@
         compiler_params=PARAMS,
     )(ids, nodes, rotation)
     held = pltpu.VMEM((2,) + half.shape, bf16)
-    copies = pltpu.SemaphoreType.DMA((2,))
+    copies = pltpu.SemaphoreType.DMA((len(places),))
+    out_copy = pltpu.SemaphoreType.DMA((1,))
 
     span = node_rows(row_count)
-    message_sums, stats, scalar, per_edge = pl.pallas_call(
+    sums = (head_count, 2 * all_nodes)
+    messages, stats, sent, scalar, per_edge = pl.pallas_call(
         functools.partial(forward_kernel, places, group),
         out_shape=(
-            jax.ShapeDtypeStruct((group, span, channels), bf16),
-            jax.ShapeDtypeStruct((head_count, 2 * all_nodes), f32),
+            jax.ShapeDtypeStruct((COEF,) + field, bf16),
+            jax.ShapeDtypeStruct(sums, f32),
+            jax.ShapeDtypeStruct((group,) + sums, f32),
             jax.ShapeDtypeStruct(field, f32),
             jax.ShapeDtypeStruct((2 * head_count, edge_rows), f32),
         ),
         in_specs=[smem] + [VMEM] * 5 + [ANY] * 2,
-        out_specs=[VMEM] * 4,
+        out_specs=[ANY] + [VMEM] * 4,
         scratch_shapes=[
             held,
             pltpu.VMEM((REDUCED * channels, edge_rows), f32),
@@ -580,19 +638,11 @@
             pltpu.VMEM((COEF,) + field, bf16),
             pltpu.VMEM(field, f32),
             copies,
+            out_copy,
         ],
         compiler_params=PARAMS,
     )(first, ids, z, rotation, grad_edge, attention_t, half, other)
-    every = gather(stats, GRAPH)
-    shared_sums = pl.pallas_call(
-        share_kernel,
-        out_shape=jax.ShapeDtypeStruct(message_sums.shape, bf16),
-        in_specs=[VMEM] * 3,
-        out_specs=VMEM,
-        compiler_params=PARAMS,
-    )(stats, every, message_sums)
-    every, shared_sums = lax.optimization_barrier((every, shared_sums))
-    summed = lax.psum_scatter(shared_sums, GRAPH, scatter_dimension=0, tiled=True)
+    every = exchange(sent, GRAPH)
 
     columns = lax.axis_size(COLUMN_GROUP)
     depth = channels * (LMAX + 1)
@@ -607,19 +657,37 @@
             partial,
         ),
         in_specs=[smem] + [VMEM] * 10,
-        out_specs=[VMEM] * 3,
+        out_specs=[ANY] + [VMEM] * 2,
         scratch_shapes=[
             wide,
             pltpu.VMEM(field, f32),
             pltpu.VMEM((REDUCED * channels, edge_rows), f32),
             pltpu.VMEM((depth + padded, depth), f32),
+            pltpu.VMEM((REDUCED * channels, edge_rows), bf16),
+            out_copy,
         ],
         compiler_params=PARAMS,
     )(first, ids, stats, every, scalar, per_edge, rotation, grad_edge, attention, attention_t, z)
 
     theirs = lax.ppermute(theirs, "core", [(0, 1), (1, 0)])
     mine = (mine.astype(f32) + theirs.astype(f32)).astype(bf16)
+    mine, messages = lax.optimization_barrier((mine, messages))
     zero_parts = exchange(mine, COLUMN_GROUP)
+    message_sums = pl.pallas_call(
+        message_kernel,
+        out_shape=jax.ShapeDtypeStruct((group, span, channels), bf16),
+        in_specs=[VMEM] * 4,
+        out_specs=VMEM,
+        compiler_params=PARAMS,
+    )(ids, stats, every, messages)
+    message_sums = message_sums.reshape(group // 2, 2 * span, channels)
+    near_sums = lax.psum_scatter(message_sums, "y", scatter_dimension=0, tiled=True)
+    near_sums = near_sums.reshape(2, span, channels)
+    side = lax.axis_index("xl")
+    kept = lax.dynamic_index_in_dim(near_sums, side, keepdims=False)
+    passed = lax.dynamic_index_in_dim(near_sums, 1 - side, keepdims=False)
+    passed = lax.ppermute(passed, "xl", [(0, 1), (1, 0)])
+    summed = kept.astype(f32) + passed.astype(f32)
     zero_sum = jnp.sum(zero_parts.astype(f32), axis=0)
     att_flat = zero_sum[share : share + 2].reshape(-1)[: head_count * channels]
     zero_send = jnp.transpose(zero_sum[:share].reshape(share, group, -1), (1, 0, 2))
@@ -628,17 +696,18 @@
     zero_send = jnp.pad(zero_send, ((0, 0), (0, 0), (0, lanes - inner)))
     zero_send = zero_send.reshape(group, share * lanes // LANES, LANES)
     att = att_flat.reshape(head_count, channels)
+    used = harmonics * row_count
     spare = lanes - channels // 2
     beside = spare >= max(inner, channels // 2) and share >= 2 * head_count
     if beside:
-        att = jnp.pad(att.reshape(2 * head_count, -1), ((0, share - 2 * head_count), (spare, 0)))
+        att = jnp.concatenate([att[:, :spare], att[:, spare:]], axis=0)
+        att = jnp.pad(att, ((0, share - 2 * head_count), (spare, 0)))
         last_rows = zero_send + att[None]
     else:
         att = jnp.broadcast_to(att[None], (group, head_count, channels))
         last_rows = jnp.concatenate([zero_send, att], axis=1)
     last_rows = last_rows.astype(bf16)
 
-    used = harmonics * row_count
     zero_rows = share * lanes // LANES
     grad_sums = pl.pallas_call(
         functools.partial(scatter_kernel, places, group, row_count),
@@ -661,25 +730,28 @@
     grad_sums = lax.dynamic_update_slice(grad_sums, last_rows, (0, used, 0))
     last = exchange(grad_sums, GRAPH)
 
-    grad_nodes, total = pl.pallas_call(
+    grad_nodes, tail = pl.pallas_call(
         sum_kernel,
         out_shape=(
-            jax.ShapeDtypeStruct((row_count, harmonics, channels), bf16),
-            jax.ShapeDtypeStruct(last.shape[1:], f32),
+            jax.ShapeDtypeStruct((harmonics, row_count, channels), bf16),
+            jax.ShapeDtypeStruct(last_rows.shape[1:], f32),
         ),
         in_specs=[VMEM],
         out_specs=[VMEM] * 2,
+        scratch_shapes=[pltpu.VMEM(last.shape[1:], f32)],
         compiler_params=PARAMS,
     )(last)
-    tail = total[used : used + last_rows.shape[1]] * (1.0 / (2 * columns))
+    tail = tail * (1.0 / (2 * columns))
     grad_zero = tail[:zero_rows].reshape(share, lanes)[:, :inner].T
     if beside:
-        grad_att = tail[: 2 * head_count, spare:].reshape(head_count, channels).T
+        grad_att = jnp.concatenate(
+            [tail[:head_count, spare:], tail[head_count : 2 * head_count, spare:]], axis=1
+        ).T
     else:
         grad_att = tail[zero_rows:].T
-    update = summed[0, :used].reshape(harmonics, row_count, channels)
-    update = jnp.where(present[None], update, jnp.zeros_like(update))
-    update = jnp.transpose(update, (1, 0, 2))
+    update = summed[:used].reshape(harmonics, row_count, channels)
+    update = jnp.transpose(jnp.where(present[None], update, 0.0).astype(bf16), (1, 0, 2))
+    grad_nodes = jnp.transpose(grad_nodes, (1, 0, 2))
 
     shape = (1, row_count, harmonics, channels)
     return (update.reshape(shape), grad_nodes.reshape(shape), grad_zero, grad_att)

time: 236 us -> 215 us (0.911)
  the two profiles are of different devices: /device:TPU:68 before, /device:TPU:1 now
where the time goes in v3:
time: 215 us; the launch traced here: 211 us
  blocking collectives  73.6 us (34%)
  waiting for transfers between devices  49.4 us (23%)
  starting transfers between devices  28.7 us (13%)
  Pallas kernels  27.4 us (13%)
  between operations  15.7 us (7%)
  local copies, waits for them, and re-layouts  12.5 us (6%)
  other arithmetic  4.14 us (2%)
    all_to_all x2, blocking collectives, gather(): return lax.all_to_all(copies, axes, split_axis=0, concat_axis=0, tiled=True)  65.2 us
    all_to_all x3, waiting for transfers between devices, exchange(): return lax.all_to_all(blocks, axes, split_axis=0, concat_axis=0, tiled=True)  20.3 us
    reduce_scatter x1, waiting for transfers between devices, on_device(): lax.psum_scatter(message_sums, 'y', scatter_dimension=0, tiled=True)  19.6 us
    all_to_all x3, starting transfers between devices, exchange(): return lax.all_to_all(blocks, axes, split_axis=0, concat_axis=0, tiled=True)  18.6 us
    unnamed x38, local copies, waits for them, and re-layouts  8.54 us
    all_gather x1, blocking collectives, gather_weights(): near = lax.all_gather(packed, 'core')  8.37 us
    pallas_call x1, Pallas kernels, on_device(): pl.pallas_call(functools.partial(scatter_kernel, places, group, row_count...  7.39 us
    pallas_call x1, Pallas kernels, on_device(): pl.pallas_call(functools.partial(forward_kernel, places, group), out_shap...  7.33 us
  transfers between devices with their start and end apart: 8, of which 6 were waited for; matrix products, arithmetic and copies ran while one was open for 3% of the time, Pallas kernels for 6%

profile of v3, /device:TPU:1, one launch (start us, length us, event | category | flops | bytes accessed | tf_op | source)
XLA Modules:
  0.0 211.5 jit_solution(9786842097149920902)
XLA Ops:
  7.9 0.7 copy-done.9
  10.8 8.4 %all-gather = bf16[64,256]{1,0:T(8,128)(2,1)S(1)} all-gather(bf16[32,256]{1,0:T(8,128)(2,1)S(1)} %shard_map.156), channel_id=2, replica_groups=mesh['xh'=2,'z'=8,'core'=2,'y'=8,'xl'=2] {'core'}, dimensions={0}, use_global_device_ids=true | all-gather | bytes 49152 | tf_op jit(solution)/shard_map/all_gather | solution.py:537
  19.3 21.5 %all_to_all.25.slabs = bf16[32,64,128]{2,1,0:T(8,128)(2,1)S(1)} all-to-all(bf16[32,64,128]{2,1,0:T(8,128)(2,1)S(1)} %broadcast_in_dim.40), channel_id=1, replica_groups=mesh['xh'=2,'z'=8,'core'=2,'y'=8,'xl'=2] {'xh','y','xl'}, dimensions={0} | all-to-all | bytes 1048576 | tf_op jit(solution)/shard_map/all_to_all | solution.py:32
  40.8 4.1 %shard_map.157 = bf16[1376,128]{1,0:T(8,128)(2,1)} custom-call(s32[1,1]{1,0:T(1,128)} %bitcast.2.first, bf16[32,64,128]{2,1,0:T(8,128)(2,1)S(1)} %all_to_all.25.slabs), custom_call_target="tpu_custom_call" | custom-call | tf_op jit(solution)/shard_map/pallas_call | solution.py:551
  46.1 43.8 %all_to_all.26.nodes = bf16[16,400,128]{2,1,0:T(8,128)(2,1)S(1)} all-to-all(bf16[16,400,128]{2,1,0:T(8,128)(2,1)S(1)} %broadcast_in_dim.43), channel_id=1, replica_groups=mesh['xh'=2,'z'=8,'core'=2,'y'=8,'xl'=2] {'y','xl'}, dimensions={0} | all-to-all | bytes 3276800 | tf_op jit(solution)/shard_map/all_to_all | solution.py:32
  89.9 4.5 %collective-permute-start = (bf16[8,1376,128]{2,1,0:T(8,128)(2,1)}, bf16[8,1376,128]{2,1,0:T(8,128)(2,1)}, u32[]{:S(2)}, u32[]{:S(2)}) collective-permute-start(bf16[8,1376,128]{2,1,0:T(8,128)(2,1)} %bitcast.42), channel_id=1, source_target_pairs={{0,16},{16,0},{1,17},{17,1},{2,18},{18,2},{3,19},{19,3},{4,20},{20... | collective-permute-start | bytes 8454152 | tf_op jit(solution)/shard_map/ppermute | solution.py:600
  95.2 2.3 %shard_map.158 = (bf16[29,128,128]{2,1,0:T(8,128)(2,1)S(1)}, bf16[49,128,128]{2,1,0:T(8,128)(2,1)S(1)}) custom-call(s32[8,128]{1,0:T(8,128)S(1)} %stack.12.ids, bf16[16,400,128]{2,1,0:T(8,128)(2,1)S(1)} %all_to_all.26.nodes, bf16[29,49,128]{2,1,0:T(8,128)(2,1)S(1)} %bitcast.45), custom_call_target="tpu_custom_call" | custom-call | tf_op jit(solution)/shard_map/pallas_call | solution.py:605
  97.6 1.9 collective-permute-done.other
  99.5 7.3 %shard_map.159 = (bf16[49,128,128]{2,1,0:T(8,128)(2,1)S(1)}, f32[8,128]{1,0:T(8,128)S(1)}, f32[16,8,128]{2,1,0:T(8,128)}, f32[128,128]{1,0:T(8,128)S(1)}, f32[16,128]{1,0:T(8,128)S(1)}) custom-call(s32[1,1]{1,0:T(1,128)} %bitcast.2.first, s32[8,128]{1,0:T(8,128)S(1)} %stack.12.ids, bf16[29,128,128]{2,1,0:T(8,128)(2,1)S(1)} %get-tuple-element.23.z, ...), custom_call_target="tpu_custom_call" | custom-call | tf_op jit(solution)/shard_map/pallas_call | solution.py:622
  106.8 1.2 copy-done.3
  108.0 6.5 %all-to-all-start.2 = ((f32[16,8,128]{2,1,0:T(8,128)}), f32[16,8,128]{2,1,0:T(8,128)S(1)}, u32[]{:S(2)}, u32[]{:S(2)}) async-start(f32[16,8,128]{2,1,0:T(8,128)} %get-tuple-element.27), calls=%async_computation.2 | async-start | bytes 131072 | tf_op jit(solution)/shard_map/all_to_all | solution.py:36
  114.6 7.8 %all-to-all-done.2.every = f32[16,8,128]{2,1,0:T(8,128)S(1)} async-done(((f32[16,8,128]{2,1,0:T(8,128)}), f32[16,8,128]{2,1,0:T(8,128)S(1)}, u32[]{:S(2)}, u32[]{:S(2)}) %all-to-all-start.2) | async-done | bytes 65568 | tf_op jit(solution)/shard_map/all_to_all | solution.py:36
  122.3 1.4 copy-done.2
  123.8 3.2 %shard_map.160 = (bf16[3712,128]{1,0:T(8,128)(2,1)S(1)}, bf16[16,32,896]{2,1,0:T(8,128)(2,1)S(1)}, bf16[16,32,896]{2,1,0:T(8,128)(2,1)S(1)}) custom-call(s32[1,1]{1,0:T(1,128)} %bitcast.2.first, s32[8,128]{1,0:T(8,128)S(1)} %stack.12.ids, f32[8,128]{1,0:T(8,128)S(1)} %get-tuple-element.26.stats, f32[16,8,128]{2,1,0:T(8,128)S(1)} %all-to-all-done.2.every, ...), custom_call_target="tpu_custom_call" | custom-call | tf_op jit(solution)/shard_map/pallas_call | solution.py:652
  127.0 1.0 copy-done.5
  128.0 3.7 %collective-permute-start.1 = (bf16[16,32,896]{2,1,0:T(8,128)(2,1)S(1)}, bf16[16,32,896]{2,1,0:T(8,128)(2,1)S(1)}, u32[]{:S(2)}, u32[]{:S(2)}) collective-permute-start(bf16[16,32,896]{2,1,0:T(8,128)(2,1)S(1)} %get-tuple-element.31), channel_id=1, source_target_pairs={{0,16},{16,0},{1,17},{17,1},{2,18},{18,2},{3,19},{19,3},{4,20},{20... | collective-permute-start | bytes 2752520 | tf_op jit(solution)/shard_map/ppermute | solution.py:672
  131.7 2.1 collective-permute-done.1
  133.8 1.1 add_convert_fusion
  134.9 8.5 %all-to-all-start.3 = ((bf16[16,32,896]{2,1,0:T(8,128)(2,1)}), bf16[16,32,896]{2,1,0:T(8,128)(2,1)}, u32[]{:S(2)}, u32[]{:S(2)}) async-start(bf16[16,32,896]{2,1,0:T(8,128)(2,1)} %add_convert_fusion), calls=%async_computation.4 | async-start | bytes 1835008 | tf_op jit(solution)/shard_map/all_to_all | solution.py:36
  143.5 1.2 copy-done.6
  144.6 7.4 %shard_map.162 = bf16[16,224,128]{2,1,0:T(8,128)(2,1)} custom-call(s32[1,1]{1,0:T(1,128)} %bitcast.2.first, s32[8,128]{1,0:T(8,128)S(1)} %stack.12.ids, bf16[3712,128]{1,0:T(8,128)(2,1)S(1)} %copy-done.6, bf16[29,49,128]{2,1,0:T(8,128)(2,1)S(1)} %bitcast.48, bf16[8,1376,128]{2,1,0:T(8,128)(2,1)S(1)} %bitcast.44, bf16[8,1376,128]{2,1,0:T(8,128)(2,1)} %collective-permute-done.other), custom_call_target="tpu_custom_call" | custom-call | tf_op jit(solution)/shard_map/pallas_call | solution.py:712
  152.1 2.1 %shard_map.161 = bf16[16,208,128]{2,1,0:T(8,128)(2,1)} custom-call(s32[8,128]{1,0:T(8,128)S(1)} %stack.12.ids, f32[8,128]{1,0:T(8,128)S(1)} %get-tuple-element.26.stats, f32[16,8,128]{2,1,0:T(8,128)S(1)} %all-to-all-done.2.every, bf16[49,128,128]{2,1,0:T(8,128)(2,1)S(1)} %copy-done.4), custom_call_target="tpu_custom_call" | custom-call | tf_op jit(solution)/shard_map/pallas_call | solution.py:676
  154.2 12.5 %all-to-all-done.3 = bf16[16,32,896]{2,1,0:T(8,128)(2,1)} async-done(((bf16[16,32,896]{2,1,0:T(8,128)(2,1)}), bf16[16,32,896]{2,1,0:T(8,128)(2,1)}, u32[]{:S(2)}, u32[]{:S(2)}) %all-to-all-start.3) | async-done | bytes 917536 | tf_op jit(solution)/shard_map/all_to_all | solution.py:36
  166.7 1.3 convert_reduce_fusion
  168.6 1.7 dynamic_update_slice.3
  170.2 3.6 %all-to-all-start.4 = ((bf16[16,224,128]{2,1,0:T(8,128)(2,1)}), bf16[16,224,128]{2,1,0:T(8,128)(2,1)S(1)}, u32[]{:S(2)}, u32[]{:S(2)}) async-start(bf16[16,224,128]{2,1,0:T(8,128)(2,1)} %dynamic_update_slice.3), calls=%async_computation.5 | async-start | bytes 1835008 | tf_op jit(solution)/shard_map/all_to_all | solution.py:36
  173.9 19.6 %reduce-scatter.2.cloned.1.call-done = bf16[1,416,128]{2,1,0:T(8,128)(2,1)} async-done(((bf16[8,416,128]{2,1,0:T(8,128)(2,1)}), bf16[1,416,128]{2,1,0:T(8,128)(2,1)}) %reduce-scatter.2.cloned.1.call-update) | async-done | bytes 106512 | tf_op jit(solution)/shard_map/reduce_scatter | solution.py:684
  193.5 0.8 dynamic-slice_bitcast_fusion
  194.3 1.9 collective-permute-start.2
  196.3 5.5 %collective-permute-done.2 = bf16[208,128]{1,0:T(8,128)(2,1)S(1)} collective-permute-done((bf16[208,128]{1,0:T(8,128)(2,1)S(1)}, bf16[208,128]{1,0:T(8,128)(2,1)S(1)}, u32[]{:S(2)}, u32[]{:S(2)}) %collective-permute-start.2) | collective-permute-done | bytes 53280 | tf_op jit(solution)/shard_map/ppermute | solution.py:689
  201.8 0.7 fusion
  202.5 0.8 shard_map.163
  (65 shorter events, 5.8 us)
Async XLA Ops:
  7.2 82.7 %all-gather.4.cloned.1.call-start = ((), (), s32[]{:S(2)}) async-start(), calls=%async_computation.7 | async-start | bytes 3170304 | tf_op jit(solution)/shard_map/all_gather | solution.py:558
  7.2 0.7 copy-start.8
  7.9 0.7 copy-start.9
  8.6 0.7 copy-start.10
  9.3 0.7 copy-start.11
  10.0 0.7 copy-start.12
  10.7 34.9 %copy-start.14 = (f32[1,4,49,128]{3,1,2,0:T(4,128)S(1)}, f32[1,4,49,128]{3,1,2,0:T(4,128)}, u32[]{:S(2)}) copy-start(f32[1,4,49,128]{3,1,2,0:T(4,128)} %param.19) | copy-start | bytes 301060
  10.7 35.0 %copy-start.15 = (bf16[1,4,49,128]{3,1,2,0:T(4,128)(2,1)S(1)}, bf16[1,4,49,128]{3,1,2,0:T(4,128)(2,1)}, u32[]{:S(2)}) copy-start(bf16[1,4,49,128]{3,1,2,0:T(4,128)(2,1)} %param.13) | copy-start | bytes 150532
  46.0 48.9 %copy-start.13 = (bf16[1,29,49,128]{3,1,2,0:T(8,128)(2,1)S(1)}, bf16[1,29,49,128]{3,1,2,0:T(8,128)(2,1)}, u32[]{:S(2)}) copy-start(bf16[1,29,49,128]{3,1,2,0:T(8,128)(2,1)} %param.18) | copy-start | bytes 1091332
  46.1 49.1 %copy-start.16 = (s32[1,128]{1,0:T(1,128)S(1)}, s32[1,128]{1,0:T(1,128)}, u32[]{:S(2)}) copy-start(s32[1,128]{1,0:T(1,128)} %param.16) | copy-start | bytes 1540
  46.1 49.1 %copy-start.17 = (s32[1,128]{1,0:T(1,128)S(1)}, s32[1,128]{1,0:T(1,128)}, u32[]{:S(2)}) copy-start(s32[1,128]{1,0:T(1,128)} %param.17) | copy-start | bytes 1540
  89.8 9.6 %copy-start.7 = (bf16[128,8]{0,1:T(8,128)(2,1)S(1)}, bf16[128,8]{0,1:T(8,128)(2,1)}, u32[]{:S(2)}) copy-start(bf16[128,8]{0,1:T(8,128)(2,1)} %param.25) | copy-start | bytes 6148
  89.9 9.6 %collective-permute-start = (bf16[8,1376,128]{2,1,0:T(8,128)(2,1)}, bf16[8,1376,128]{2,1,0:T(8,128)(2,1)}, u32[]{:S(2)}, u32[]{:S(2)}) collective-permute-start(bf16[8,1376,128]{2,1,0:T(8,128)(2,1)} %bitcast.42), channel_id=1, source_target_pairs={{0,16},{16,0},{1,17},{17,1},{2,18},{18,2},{3,19},{19,3},{4,20},{20... | collective-permute-start | bytes 8454152 | tf_op jit(solution)/shard_map/ppermute | solution.py:600
  97.6 9.2 %copy-start.1 = (bf16[49,128,128]{2,1,0:T(8,128)(2,1)}, bf16[49,128,128]{2,1,0:T(8,128)(2,1)S(1)}, u32[]{:S(2)}) copy-start(bf16[49,128,128]{2,1,0:T(8,128)(2,1)S(1)} %get-tuple-element.24.grad_edge) | copy-start | bytes 4816900
  106.8 1.2 copy-start.3
  108.0 14.4 %all-to-all-start.2 = ((f32[16,8,128]{2,1,0:T(8,128)}), f32[16,8,128]{2,1,0:T(8,128)S(1)}, u32[]{:S(2)}, u32[]{:S(2)}) async-start(f32[16,8,128]{2,1,0:T(8,128)} %get-tuple-element.27), calls=%async_computation.2 | async-start | bytes 131072 | tf_op jit(solution)/shard_map/all_to_all | solution.py:36
  122.3 1.4 copy-start.2
  127.0 1.0 copy-start.5
  128.0 5.8 %collective-permute-start.1 = (bf16[16,32,896]{2,1,0:T(8,128)(2,1)S(1)}, bf16[16,32,896]{2,1,0:T(8,128)(2,1)S(1)}, u32[]{:S(2)}, u32[]{:S(2)}) collective-permute-start(bf16[16,32,896]{2,1,0:T(8,128)(2,1)S(1)} %get-tuple-element.31), channel_id=1, source_target_pairs={{0,16},{16,0},{1,17},{17,1},{2,18},{18,2},{3,19},{19,3},{4,20},{20... | collective-permute-start | bytes 2752520 | tf_op jit(solution)/shard_map/ppermute | solution.py:672
  133.8 9.7 %copy-start = (bf16[11008,128]{1,0:T(8,128)(2,1)S(1)}, bf16[11008,128]{1,0:T(8,128)(2,1)}, u32[]{:S(2)}) copy-start(bf16[11008,128]{1,0:T(8,128)(2,1)} %all-gather.4.cloned.1.call-done) | copy-start | bytes 8454148
  134.9 31.8 %all-to-all-start.3 = ((bf16[16,32,896]{2,1,0:T(8,128)(2,1)}), bf16[16,32,896]{2,1,0:T(8,128)(2,1)}, u32[]{:S(2)}, u32[]{:S(2)}) async-start(bf16[16,32,896]{2,1,0:T(8,128)(2,1)} %add_convert_fusion), calls=%async_computation.4 | async-start | bytes 1835008 | tf_op jit(solution)/shard_map/all_to_all | solution.py:36
  143.4 50.1 %reduce-scatter.2.cloned.1.call-start = ((), (), s32[]{:S(2)}) async-start(), calls=%async_computation.6 | async-start | bytes 958464 | tf_op jit(solution)/shard_map/reduce_scatter | solution.py:684
  143.5 1.2 copy-start.6
  144.6 7.4 %copy-start.4 = (bf16[49,128,128]{2,1,0:T(8,128)(2,1)S(1)}, bf16[49,128,128]{2,1,0:T(8,128)(2,1)}, u32[]{:S(2)}) copy-start(bf16[49,128,128]{2,1,0:T(8,128)(2,1)} %copy-done.3) | copy-start | bytes 4816900
  170.2 32.3 %all-to-all-start.4 = ((bf16[16,224,128]{2,1,0:T(8,128)(2,1)}), bf16[16,224,128]{2,1,0:T(8,128)(2,1)S(1)}, u32[]{:S(2)}, u32[]{:S(2)}) async-start(bf16[16,224,128]{2,1,0:T(8,128)(2,1)} %dynamic_update_slice.3), calls=%async_computation.5 | async-start | bytes 1835008 | tf_op jit(solution)/shard_map/all_to_all | solution.py:36
  194.3 7.4 %collective-permute-start.2 = (bf16[208,128]{1,0:T(8,128)(2,1)S(1)}, bf16[208,128]{1,0:T(8,128)(2,1)S(1)}, u32[]{:S(2)}, u32[]{:S(2)}) collective-permute-start(bf16[208,128]{1,0:T(8,128)(2,1)S(1)} %get-tuple-element.38), channel_id=1, source_target_pairs={{0,1},{1,0},{2,3},{3,2},{4,5},{5,4},{6,7},{7,6},{8,9},{9,8},{10,11... | collective-permute-start | bytes 159752 | tf_op jit(solution)/shard_map/ppermute | solution.py:689
Sparse Core Ops, SparseCore 0:
  45.0 43.5 all-gather.3
  154.3 39.0 reduce-scatter.1

commit v4 on v3

--- a/solution.py
+++ b/solution.py
@@ -48,8 +48,8 @@
 TWO = (3 * LMAX + 1, LMAX - 1)
 CHUNK = 32
 VMEM = pl.BlockSpec(memory_space=pltpu.VMEM)
-ANY = pl.BlockSpec(memory_space=pl.ANY)
-PARAMS = pltpu.CompilerParams(vmem_limit_bytes=48 * 1024 * 1024)
+HBM = pl.BlockSpec(memory_space=pltpu.HBM)
+PARAMS = pltpu.CompilerParams(vmem_limit_bytes=28 * 1024 * 1024)
 
 
 def nt_dot(left, right):
@@ -150,13 +150,20 @@
 
 
 def pack_kernel(places, *refs):
-    shards, out, acc = refs[:-2], refs[-2], refs[-1]
+    count = len(places)
+    shards, out = refs[:count], refs[count]
+    held, acc, sems = refs[count + 1 : -2], refs[-2], refs[-1]
+    copies = [pltpu.make_async_copy(shards[i], held[i], sems.at[i]) for i in range(count)]
+    for copy in copies:
+        copy.start()
     acc[...] = jnp.zeros_like(acc)
-    for shard, at in zip(shards, places):
+    for copy, shard, at in zip(copies, held, places):
         columns, rows = shard.shape
         lane = lax.broadcasted_iota(jnp.int32, (rows, acc.shape[1]), 1)
         row = lax.broadcasted_iota(jnp.int32, (rows, acc.shape[1]), 0)
-        acc[:columns, :] += half_dot(shard[...], (lane == row + at).astype(bf16))
+        place = (lane == row + at).astype(bf16)
+        copy.wait()
+        acc[:columns, :] += half_dot(shard[...], place)
     out[...] = acc[...].astype(bf16)
 
 
@@ -207,7 +214,7 @@
     by_owner(hot_rows(ids[1:2, :], count).astype(bf16), msg, out, group, scale)
 
 
-def rotate_kernel(own, ids, nodes, wigner, z, grad_edge, paired, wide):
+def rotate_kernel(own, ids, nodes, wigner, z, edge_out, paired, wide, grad_edge, out_sem):
     group, edges = nodes.shape[0], wigner.shape[2]
     channels = LANES
     per = 16 // (2 * own)
@@ -225,13 +232,16 @@
             paired[j] = half_dot(here, both).astype(bf16).astype(f32)
             here = rows[:, at + 1].reshape(count, channels).T.astype(bf16)
             grad_edge[j] = half_dot(here, target).astype(bf16)
+    copy = pltpu.make_async_copy(grad_edge, edge_out, out_sem.at[0])
+    copy.start()
     for l in range(LMAX + 1):
         for k in ROWS_OF[l]:
             acc = None
             for j in COEFS_OF[l]:
-                term = wide[k, j : j + 1, :] * paired[j]
+                term = wide[j, k : k + 1, :] * paired[j]
                 acc = term if acc is None else acc + term
             z[k] = acc.astype(bf16)
+    copy.wait()
 
 
 def forward_kernel(
@@ -241,7 +251,7 @@
     ids,
     z,
     wigner,
-    grad_edge,
+    edge_in,
     attention_t,
     mine,
     other,
@@ -256,6 +266,7 @@
     norm,
     msg,
     heads_acc,
+    grad_edge,
     sems,
     out_sem,
 ):
@@ -263,6 +274,8 @@
     heads = attention_t.shape[0]
     count = stats.shape[1] // 2
     start_weights(places, first[0, 0], mine, other, held, sems)
+    edge_copy = pltpu.make_async_copy(edge_in, grad_edge, out_sem.at[1])
+    edge_copy.start()
     wide[...] = wigner[...].astype(f32)
     base, rows = ZERO
     acc = None
@@ -306,12 +319,13 @@
             for j in COEFS_OF[l]:
                 acc = None
                 for k in ROWS_OF[l]:
-                    term = wide[k, j : j + 1, :] * y[rows_at(k, start), :]
+                    term = wide[j, k : k + 1, :] * y[rows_at(k, start), :]
                     acc = term if acc is None else acc + term
                 total = total + acc * grad_edge[j, at, :].astype(f32)
                 msg[j, at, :] = (acc * own).astype(bf16)
         heads_acc[at, :] = total
 
+    edge_copy.wait()
     chunks(channels, body)
     copy = pltpu.make_async_copy(msg, messages, out_sem.at[0])
     copy.start()
@@ -334,7 +348,7 @@
     scalar,
     per_edge,
     wigner,
-    grad_edge,
+    edge_in,
     attention,
     attention_t,
     z,
@@ -346,11 +360,14 @@
     grad,
     turned,
     grad_conv,
+    grad_edge,
     out_sem,
 ):
     channels, edges = LANES, wigner.shape[2]
     heads = attention_t.shape[0]
     count = stats.shape[1] // 2
+    edge_copy = pltpu.make_async_copy(edge_in, grad_edge, out_sem.at[1])
+    edge_copy.start()
     wide[...] = wigner[...].astype(f32)
     total = jnp.sum(every[:, :, :count], axis=0)
     total = jnp.where(total > 0.0, total, 1.0)
@@ -379,10 +396,11 @@
             for k in ROWS_OF[l]:
                 acc = None
                 for j, field in zip(COEFS_OF[l], fields):
-                    term = wide[k, j : j + 1, :] * field
+                    term = wide[j, k : k + 1, :] * field
                     acc = term if acc is None else acc + term
                 grad[rows_at(k, start), :] = acc
 
+    edge_copy.wait()
     chunks(channels, body)
     grad[:channels, :] = grad[:channels, :] + grad_scalar
     depth = (LMAX + 1) * channels
@@ -428,14 +446,16 @@
     wigner,
     mine,
     other,
-    grads,
+    grads_out,
     held,
     wide,
     dz,
     gp,
     grad,
     grad_rows,
+    grads,
     sems,
+    out_sem,
 ):
     channels, edges = LANES, wigner.shape[2]
     count = own * group
@@ -483,23 +503,92 @@
             for j in COEFS_OF[l]:
                 acc = None
                 for k in ROWS_OF[l]:
-                    term = wide[k, j : j + 1, :] * dz[k, at, :]
+                    term = wide[j, k : k + 1, :] * dz[k, at, :]
                     acc = term if acc is None else acc + term
                 gp[j, at, :] = acc.astype(bf16)
 
     chunks(channels, body)
     both = (hot_rows(ids[1:2, :], count) + hot_rows(ids[0:1, :], count)).astype(bf16)
     by_owner(both, gp, grads, group)
+    whole = pl.ds(0, grads.shape[1])
+    copy = pltpu.make_async_copy(grads, grads_out.at[:, whole, :], out_sem.at[0])
+    copy.start()
+    copy.wait()
 
 
 def node_rows(own):
     return -(-COEF * own // 16) * 16
 
 
+def one_hot(rows, columns, shift, low, high):
+    row = lax.broadcasted_iota(jnp.int32, (rows, columns), 0)
+    column = lax.broadcasted_iota(jnp.int32, (rows, columns), 1)
+    return ((column == row + shift) & (row >= low) & (row < high)).astype(bf16)
+
+
+def tail_kernel(used, share, heads, parts, grads_in, grads, total, att, window, sems):
+    count, depth = parts.shape[0], parts.shape[2]
+    group, rows = window.shape[0], window.shape[1]
+    inner, skip = depth // group, used % 16
+    base = used - skip
+    old = pltpu.make_async_copy(
+        grads_in.at[:, pl.ds(base, 16), :], window.at[:, pl.ds(0, 16), :], sems.at[0]
+    )
+    old.start()
+    acc = parts[0].astype(f32)
+    for p in range(1, count):
+        acc = acc + parts[p].astype(f32)
+    total[...] = acc
+    for h in range(heads):
+        row, at = share + h // (depth // LANES), h % (depth // LANES) * LANES
+        att[h : h + 1, :] = total[row : row + 1, at : at + LANES]
+    low = att[...].astype(bf16)
+    half = LANES // 2
+    left = half_dot(low, one_hot(LANES, LANES, half, 0, half)).astype(bf16)
+    right = half_dot(low, one_hot(LANES, LANES, 0, half, LANES)).astype(bf16)
+    row = lax.broadcasted_iota(jnp.int32, (rows, heads), 0)
+    head = lax.broadcasted_iota(jnp.int32, (rows, heads), 1)
+    tail = half_dot((row == head + skip).astype(bf16), left)
+    tail = tail + half_dot((row == head + skip + heads).astype(bf16), right)
+    moved = half_dot(one_hot(rows, total.shape[0], -skip, skip, skip + share), acc.astype(bf16))
+    moved = moved.astype(bf16)
+    kept = lax.broadcasted_iota(jnp.int32, (rows, LANES), 0) < skip
+    old.wait()
+    for g in range(group):
+        first = g * inner // LANES * LANES
+        last = -(-(g + 1) * inner // LANES) * LANES
+        shift = g * inner - first
+        place = one_hot(last - first, LANES, -shift, shift, shift + inner)
+        piece = half_dot(moved[:, first:last], place) + tail
+        before = window[g, :16, :].astype(f32)
+        if rows > 16:
+            before = jnp.concatenate([before, jnp.zeros((rows - 16, LANES), f32)], axis=0)
+        window[g] = jnp.where(kept, before, piece).astype(bf16)
+    new = pltpu.make_async_copy(window, grads.at[:, pl.ds(base, rows), :], sems.at[1])
+    new.start()
+    new.wait()
+
+
+def last_kernel(scale, parts, nodes, zero, att, total):
+    acc = parts[0].astype(f32)
+    for g in range(1, parts.shape[0]):
+        acc = acc + parts[g].astype(f32)
+    total[...] = acc
+    used = nodes.shape[0] * nodes.shape[1]
+    heads, half = att.shape[0], LANES // 2
+    nodes[...] = acc[:used].astype(bf16).reshape(nodes.shape)
+    zero[...] = total[used : used + zero.shape[0], :][:, : zero.shape[1]] * scale
+    left = full_dot(
+        total[used : used + heads, :], one_hot(LANES, LANES, -half, half, LANES).astype(f32)
+    )
+    lane = lax.broadcasted_iota(jnp.int32, (heads, LANES), 1)
+    right = jnp.where(lane >= half, total[used + heads : used + 2 * heads, :], 0.0)
+    att[...] = (left + right) * scale
+
+
 def sum_kernel(parts, nodes, tail, total):
-    group = parts.shape[0]
     acc = parts[0].astype(f32)
-    for g in range(1, group):
+    for g in range(1, parts.shape[0]):
         acc = acc + parts[g].astype(f32)
     total[...] = acc
     used = nodes.shape[0] * nodes.shape[1]
@@ -528,9 +617,10 @@
     packed = pl.pallas_call(
         functools.partial(pack_kernel, starts),
         out_shape=jax.ShapeDtypeStruct((most, 2 * lanes), bf16),
-        in_specs=[VMEM] * len(shards),
+        in_specs=[HBM] * len(shards),
         out_specs=VMEM,
-        scratch_shapes=[pltpu.VMEM((most, 2 * lanes), f32)],
+        scratch_shapes=[pltpu.VMEM(w.shape[::-1], bf16) for w in shards]
+        + [pltpu.VMEM((most, 2 * lanes), f32), pltpu.SemaphoreType.DMA((len(shards),))],
         compiler_params=PARAMS,
     )(*[w.T for w in shards])
     core = lax.axis_index("core")
@@ -582,7 +672,7 @@
     head_count = attention.shape[1]
     group = lax.axis_size(GRAPH)
     all_nodes = row_count * group
-    rotation = wigner[0]
+    rotation = jnp.transpose(wigner[0], (1, 0, 2))
     in_use = (lax.iota(jnp.int32, edge_rows) < edge_counts[0, 0]).astype(jnp.int32)
     ids = jnp.stack([source[0], target[0], in_use] + [jnp.zeros_like(in_use)] * 5)
     attention_t = attention.T
@@ -602,6 +692,9 @@
     smem = pl.BlockSpec(memory_space=pltpu.SMEM)
     field = (channels, edge_rows)
     wide = pltpu.VMEM(rotation.shape, f32)
+    out_copy = pltpu.SemaphoreType.DMA((1,))
+    two_copies = pltpu.SemaphoreType.DMA((2,))
+    edge_field = pltpu.VMEM((COEF,) + field, bf16)
     z, grad_edge = pl.pallas_call(
         functools.partial(rotate_kernel, row_count),
         out_shape=(
@@ -609,13 +702,17 @@
             jax.ShapeDtypeStruct((COEF,) + field, bf16),
         ),
         in_specs=[VMEM] * 3,
-        out_specs=[VMEM] * 2,
-        scratch_shapes=[pltpu.VMEM((COEF,) + field, f32), wide],
+        out_specs=[VMEM, HBM],
+        scratch_shapes=[
+            pltpu.VMEM((COEF,) + field, f32),
+            wide,
+            pltpu.VMEM((COEF,) + field, bf16),
+            out_copy,
+        ],
         compiler_params=PARAMS,
     )(ids, nodes, rotation)
     held = pltpu.VMEM((2,) + half.shape, bf16)
     copies = pltpu.SemaphoreType.DMA((len(places),))
-    out_copy = pltpu.SemaphoreType.DMA((1,))
 
     span = node_rows(row_count)
     sums = (head_count, 2 * all_nodes)
@@ -628,8 +725,8 @@
             jax.ShapeDtypeStruct(field, f32),
             jax.ShapeDtypeStruct((2 * head_count, edge_rows), f32),
         ),
-        in_specs=[smem] + [VMEM] * 5 + [ANY] * 2,
-        out_specs=[ANY] + [VMEM] * 4,
+        in_specs=[smem] + [VMEM] * 3 + [HBM, VMEM] + [HBM] * 2,
+        out_specs=[HBM] + [VMEM] * 4,
         scratch_shapes=[
             held,
             pltpu.VMEM((REDUCED * channels, edge_rows), f32),
@@ -637,8 +734,9 @@
             pltpu.VMEM(field, f32),
             pltpu.VMEM((COEF,) + field, bf16),
             pltpu.VMEM(field, f32),
+            edge_field,
             copies,
-            out_copy,
+            two_copies,
         ],
         compiler_params=PARAMS,
     )(first, ids, z, rotation, grad_edge, attention_t, half, other)
@@ -656,15 +754,16 @@
             partial,
             partial,
         ),
-        in_specs=[smem] + [VMEM] * 10,
-        out_specs=[ANY] + [VMEM] * 2,
+        in_specs=[smem] + [VMEM] * 6 + [HBM] + [VMEM] * 3,
+        out_specs=[HBM] + [VMEM] * 2,
         scratch_shapes=[
             wide,
             pltpu.VMEM(field, f32),
             pltpu.VMEM((REDUCED * channels, edge_rows), f32),
             pltpu.VMEM((depth + padded, depth), f32),
             pltpu.VMEM((REDUCED * channels, edge_rows), bf16),
-            out_copy,
+            edge_field,
+            two_copies,
         ],
         compiler_params=PARAMS,
     )(first, ids, stats, every, scalar, per_edge, rotation, grad_edge, attention, attention_t, z)
@@ -680,6 +779,7 @@
         out_specs=VMEM,
         compiler_params=PARAMS,
     )(ids, stats, every, messages)
+    message_sums, grad_conv = lax.optimization_barrier((message_sums, grad_conv))
     message_sums = message_sums.reshape(group // 2, 2 * span, channels)
     near_sums = lax.psum_scatter(message_sums, "y", scatter_dimension=0, tiled=True)
     near_sums = near_sums.reshape(2, span, channels)
@@ -688,34 +788,18 @@
     passed = lax.dynamic_index_in_dim(near_sums, 1 - side, keepdims=False)
     passed = lax.ppermute(passed, "xl", [(0, 1), (1, 0)])
     summed = kept.astype(f32) + passed.astype(f32)
-    zero_sum = jnp.sum(zero_parts.astype(f32), axis=0)
-    att_flat = zero_sum[share : share + 2].reshape(-1)[: head_count * channels]
-    zero_send = jnp.transpose(zero_sum[:share].reshape(share, group, -1), (1, 0, 2))
-    inner = zero_send.shape[2]
+    used = harmonics * row_count
+    inner = depth // group
     lanes = whole_lanes(inner)
-    zero_send = jnp.pad(zero_send, ((0, 0), (0, 0), (0, lanes - inner)))
-    zero_send = zero_send.reshape(group, share * lanes // LANES, LANES)
-    att = att_flat.reshape(head_count, channels)
-    used = harmonics * row_count
-    spare = lanes - channels // 2
-    beside = spare >= max(inner, channels // 2) and share >= 2 * head_count
-    if beside:
-        att = jnp.concatenate([att[:, :spare], att[:, spare:]], axis=0)
-        att = jnp.pad(att, ((0, share - 2 * head_count), (spare, 0)))
-        last_rows = zero_send + att[None]
-    else:
-        att = jnp.broadcast_to(att[None], (group, head_count, channels))
-        last_rows = jnp.concatenate([zero_send, att], axis=1)
-    last_rows = last_rows.astype(bf16)
-
-    zero_rows = share * lanes // LANES
+    beside = lanes - inner >= channels // 2 and lanes == channels and share >= 2 * head_count
+    tail_rows = share if beside else share * lanes // LANES + head_count
     grad_sums = pl.pallas_call(
         functools.partial(scatter_kernel, places, group, row_count),
         out_shape=jax.ShapeDtypeStruct(
-            (group, -(-(used + last_rows.shape[1]) // 16) * 16, channels), bf16
+            (group, -(-(used + tail_rows) // 16) * 16, channels), bf16
         ),
-        in_specs=[smem] + [VMEM] * 3 + [ANY] * 2,
-        out_specs=VMEM,
+        in_specs=[smem] + [VMEM] * 3 + [HBM] * 2,
+        out_specs=HBM,
         scratch_shapes=[
             held,
             wide,
@@ -723,31 +807,67 @@
             pltpu.VMEM((COEF,) + field, bf16),
             pltpu.VMEM((REDUCED * channels, edge_rows), f32),
             pltpu.VMEM((edge_rows, REDUCED * channels), bf16),
+            pltpu.VMEM((group, span, channels), bf16),
             copies,
+            out_copy,
         ],
         compiler_params=PARAMS,
     )(first, ids, grad_conv, rotation, half, other)
-    grad_sums = lax.dynamic_update_slice(grad_sums, last_rows, (0, used, 0))
-    last = exchange(grad_sums, GRAPH)
-
-    grad_nodes, tail = pl.pallas_call(
-        sum_kernel,
-        out_shape=(
-            jax.ShapeDtypeStruct((harmonics, row_count, channels), bf16),
-            jax.ShapeDtypeStruct(last_rows.shape[1:], f32),
-        ),
-        in_specs=[VMEM],
-        out_specs=[VMEM] * 2,
-        scratch_shapes=[pltpu.VMEM(last.shape[1:], f32)],
-        compiler_params=PARAMS,
-    )(last)
-    tail = tail * (1.0 / (2 * columns))
-    grad_zero = tail[:zero_rows].reshape(share, lanes)[:, :inner].T
+    nodes_shape = jax.ShapeDtypeStruct((harmonics, row_count, channels), bf16)
+    batch_scale = 1.0 / (2 * columns)
     if beside:
-        grad_att = jnp.concatenate(
-            [tail[:head_count, spare:], tail[head_count : 2 * head_count, spare:]], axis=1
-        ).T
+        window = -(-(used % 16 + share) // 16) * 16
+        grad_sums = pl.pallas_call(
+            functools.partial(tail_kernel, used, share, head_count),
+            out_shape=jax.ShapeDtypeStruct(grad_sums.shape, bf16),
+            in_specs=[VMEM, HBM],
+            out_specs=HBM,
+            input_output_aliases={1: 0},
+            scratch_shapes=[
+                pltpu.VMEM((padded, depth), f32),
+                pltpu.VMEM((head_count, channels), f32),
+                pltpu.VMEM((group, window, channels), bf16),
+                two_copies,
+            ],
+            compiler_params=PARAMS,
+        )(zero_parts, grad_sums)
+        last = exchange(grad_sums, GRAPH)
+        grad_nodes, grad_zero, grad_att = pl.pallas_call(
+            functools.partial(last_kernel, batch_scale),
+            out_shape=(
+                nodes_shape,
+                jax.ShapeDtypeStruct((share, inner), f32),
+                jax.ShapeDtypeStruct((head_count, channels), f32),
+            ),
+            in_specs=[VMEM],
+            out_specs=[VMEM] * 3,
+            scratch_shapes=[pltpu.VMEM(last.shape[1:], f32)],
+            compiler_params=PARAMS,
+        )(last)
+        grad_zero, grad_att = grad_zero.T, grad_att.T
     else:
+        zero_sum = jnp.sum(zero_parts.astype(f32), axis=0)
+        att = zero_sum[share : share + 2].reshape(-1)[: head_count * channels]
+        zero_send = jnp.transpose(zero_sum[:share].reshape(share, group, inner), (1, 0, 2))
+        zero_send = jnp.pad(zero_send, ((0, 0), (0, 0), (0, lanes - inner)))
+        zero_send = zero_send.reshape(group, share * lanes // LANES, LANES)
+        att = jnp.broadcast_to(
+            att.reshape(1, head_count, channels), (group, head_count, channels)
+        )
+        last_rows = jnp.concatenate([zero_send, att], axis=1).astype(bf16)
+        grad_sums = lax.dynamic_update_slice(grad_sums, last_rows, (0, used, 0))
+        last = exchange(grad_sums, GRAPH)
+        grad_nodes, tail = pl.pallas_call(
+            sum_kernel,
+            out_shape=(nodes_shape, jax.ShapeDtypeStruct((tail_rows, channels), f32)),
+            in_specs=[VMEM],
+            out_specs=[VMEM] * 2,
+            scratch_shapes=[pltpu.VMEM(last.shape[1:], f32)],
+            compiler_params=PARAMS,
+        )(last)
+        tail = tail * batch_scale
+        zero_rows = share * lanes // LANES
+        grad_zero = tail[:zero_rows].reshape(share, lanes)[:, :inner].T
         grad_att = tail[zero_rows:].T
     update = summed[:used].reshape(harmonics, row_count, channels)
     update = jnp.transpose(jnp.where(present[None], update, 0.0).astype(bf16), (1, 0, 2))

time: 215 us -> 212 us (0.986)
  waiting for transfers between devices: 49.4 us -> 37.6 us
  local copies, waits for them, and re-layouts: 12.5 us -> 22.8 us
    reduce_scatter x1, waiting for transfers between devices: 19.6 us -> 6.01 us  [on_device(): lax.psum_scatter(message_sums, 'y', scatter_dimension=0, tiled=True)]
    unnamed x38 -> x57, local copies, waits for them, and re-layouts: 8.54 us -> 21.6 us
    all_to_all x3, waiting for transfers between devices: 20.3 us -> 26.4 us  [exchange(): return lax.all_to_all(blocks, axes, split_axis=0, concat_axis=0, tiled=True)]
    ppermute x1, waiting for transfers between devices: 5.5 us -> 2.54 us  [on_device(): passed = lax.ppermute(passed, 'xl', [(0, 1), (1, 0)])]
  transfers between devices with their start and end apart: 8 -> 8, of which waited for: 6 -> 7; matrix products, arithmetic and copies ran while one was open for 3% -> 1% of each run, Pallas kernels for 6% -> 5%
where the time goes in v4:
time: 212 us; the launch traced here: 208 us
  blocking collectives  72.5 us (34%)
  waiting for transfers between devices  37.6 us (18%)
  starting transfers between devices  30.8 us (15%)
  Pallas kernels  26.9 us (13%)
  local copies, waits for them, and re-layouts  22.8 us (11%)
  between operations  15.7 us (7%)
    all_to_all x2, blocking collectives, gather(): return lax.all_to_all(copies, axes, split_axis=0, concat_axis=0, tiled=True)  64.2 us
    all_to_all x3, waiting for transfers between devices, exchange(): return lax.all_to_all(blocks, axes, split_axis=0, concat_axis=0, tiled=True)  26.4 us
    unnamed x57, local copies, waits for them, and re-layouts  21.6 us
    all_to_all x3, starting transfers between devices, exchange(): return lax.all_to_all(blocks, axes, split_axis=0, concat_axis=0, tiled=True)  18.5 us
    all_gather x1, blocking collectives, gather_weights(): near = lax.all_gather(packed, 'core')  8.37 us
    pallas_call x1, Pallas kernels, on_device(): pl.pallas_call(functools.partial(forward_kernel, places, group), out_shap...  6.52 us
    reduce_scatter x1, waiting for transfers between devices, on_device(): lax.psum_scatter(message_sums, 'y', scatter_dimension=0, tiled=True)  6.01 us
    ppermute x1, starting transfers between devices, on_device(): other = lax.ppermute(half, 'core', [(0, 1), (1, 0)])  5.82 us
  transfers between devices with their start and end apart: 8, of which 7 were waited for; matrix products, arithmetic and copies ran while one was open for 1% of the time, Pallas kernels for 5%

profile of v4, /device:TPU:1, one launch (start us, length us, event | category | flops | bytes accessed | tf_op | source)
XLA Modules:
  0.0 208.4 jit_solution(7842376514630103261)
XLA Ops:
  11.4 8.4 %all-gather = bf16[64,256]{1,0:T(8,128)(2,1)S(1)} all-gather(bf16[32,256]{1,0:T(8,128)(2,1)S(1)} %shard_map.156), channel_id=2, replica_groups=mesh['xh'=2,'z'=8,'core'=2,'y'=8,'xl'=2] {'core'}, dimensions={0}, use_global_device_ids=true | all-gather | bytes 49152 | tf_op jit(solution)/shard_map/all_gather | solution.py:627
  19.9 21.5 %all_to_all.25.slabs = bf16[32,64,128]{2,1,0:T(8,128)(2,1)S(1)} all-to-all(bf16[32,64,128]{2,1,0:T(8,128)(2,1)S(1)} %broadcast_in_dim.39), channel_id=1, replica_groups=mesh['xh'=2,'z'=8,'core'=2,'y'=8,'xl'=2] {'xh','y','xl'}, dimensions={0} | all-to-all | bytes 1048576 | tf_op jit(solution)/shard_map/all_to_all | solution.py:32
  41.4 4.1 %shard_map.157 = bf16[1376,128]{1,0:T(8,128)(2,1)} custom-call(s32[1,1]{1,0:T(1,128)} %bitcast.2.first, bf16[32,64,128]{2,1,0:T(8,128)(2,1)S(1)} %all_to_all.25.slabs), custom_call_target="tpu_custom_call" | custom-call | tf_op jit(solution)/shard_map/pallas_call | solution.py:641
  46.6 42.7 %all_to_all.26.nodes = bf16[16,400,128]{2,1,0:T(8,128)(2,1)} all-to-all(bf16[16,400,128]{2,1,0:T(8,128)(2,1)S(1)} %broadcast_in_dim.42), channel_id=1, replica_groups=mesh['xh'=2,'z'=8,'core'=2,'y'=8,'xl'=2] {'y','xl'}, dimensions={0} | all-to-all | bytes 3276800 | tf_op jit(solution)/shard_map/all_to_all | solution.py:32
  89.4 5.8 %collective-permute-start = (bf16[8,1376,128]{2,1,0:T(8,128)(2,1)}, bf16[8,1376,128]{2,1,0:T(8,128)(2,1)S(1)}, u32[]{:S(2)}, u32[]{:S(2)}) collective-permute-start(bf16[8,1376,128]{2,1,0:T(8,128)(2,1)} %bitcast.36), channel_id=1, source_target_pairs={{0,16},{16,0},{1,17},{17,1},{2,18},{18,2},{3,19},{19,3},{4,20},{20... | collective-permute-start | bytes 8454152 | tf_op jit(solution)/shard_map/ppermute | solution.py:690
  95.9 1.4 copy-done.7
  97.3 2.4 %shard_map.158 = (bf16[29,128,128]{2,1,0:T(8,128)(2,1)S(1)}, bf16[49,128,128]{2,1,0:T(8,128)(2,1)S(1)}) custom-call(s32[8,128]{1,0:T(8,128)S(1)} %stack.12.ids, bf16[16,400,128]{2,1,0:T(8,128)(2,1)S(1)} %copy-done.7, bf16[49,29,128]{2,1,0:T(8,128)(2,1)S(1)} %bitcast.39), custom_call_target="tpu_custom_call" | custom-call | tf_op jit(solution)/shard_map/pallas_call | solution.py:698
  100.2 3.2 %copy-done = bf16[11008,128]{1,0:T(8,128)(2,1)S(1)} copy-done((bf16[11008,128]{1,0:T(8,128)(2,1)S(1)}, bf16[11008,128]{1,0:T(8,128)(2,1)}, u32[]{:S(2)}) %copy-start) | copy-done | bytes 2818072
  103.4 6.5 %shard_map.159 = (bf16[49,128,128]{2,1,0:T(8,128)(2,1)S(1)}, f32[8,128]{1,0:T(8,128)S(1)}, f32[16,8,128]{2,1,0:T(8,128)}, f32[128,128]{1,0:T(8,128)S(1)}, f32[16,128]{1,0:T(8,128)S(1)}) custom-call(s32[1,1]{1,0:T(1,128)} %bitcast.2.first, s32[8,128]{1,0:T(8,128)S(1)} %stack.12.ids, bf16[29,128,128]{2,1,0:T(8,128)(2,1)S(1)} %get-tuple-element.26.z, ...), custom_call_target="tpu_custom_call" | custom-call | tf_op jit(solution)/shard_map/pallas_call | solution.py:719
  110.0 1.1 copy-done.14
  111.1 6.2 %all-to-all-start.2 = ((f32[16,8,128]{2,1,0:T(8,128)}), f32[16,8,128]{2,1,0:T(8,128)S(1)}, u32[]{:S(2)}, u32[]{:S(2)}) async-start(f32[16,8,128]{2,1,0:T(8,128)} %get-tuple-element.30), calls=%async_computation.2 | async-start | bytes 131072 | tf_op jit(solution)/shard_map/all_to_all | solution.py:36
  117.4 7.8 %all-to-all-done.2.every = f32[16,8,128]{2,1,0:T(8,128)S(1)} async-done(((f32[16,8,128]{2,1,0:T(8,128)}), f32[16,8,128]{2,1,0:T(8,128)S(1)}, u32[]{:S(2)}, u32[]{:S(2)}) %all-to-all-start.2) | async-done | bytes 65568 | tf_op jit(solution)/shard_map/all_to_all | solution.py:36
  125.2 1.4 copy-done.9
  126.6 1.2 copy-done.12
  127.8 3.7 %shard_map.160 = (bf16[3712,128]{1,0:T(8,128)(2,1)S(1)}, bf16[16,32,896]{2,1,0:T(8,128)(2,1)S(1)}, bf16[16,32,896]{2,1,0:T(8,128)(2,1)S(1)}) custom-call(s32[1,1]{1,0:T(1,128)} %bitcast.2.first, s32[8,128]{1,0:T(8,128)S(1)} %stack.12.ids, f32[8,128]{1,0:T(8,128)S(1)} %get-tuple-element.29.stats, f32[16,8,128]{2,1,0:T(8,128)S(1)} %all-to-all-done.2.every, ...), custom_call_target="tpu_custom_call" | custom-call | tf_op jit(solution)/shard_map/pallas_call | solution.py:750
  132.5 3.3 %collective-permute-start.1 = (bf16[16,32,896]{2,1,0:T(8,128)(2,1)S(1)}, bf16[16,32,896]{2,1,0:T(8,128)(2,1)S(1)}, u32[]{:S(2)}, u32[]{:S(2)}) collective-permute-start(bf16[16,32,896]{2,1,0:T(8,128)(2,1)S(1)} %get-tuple-element.34), channel_id=1, source_target_pairs={{0,16},{16,0},{1,17},{17,1},{2,18},{18,2},{3,19},{19,3},{4,20},{20... | collective-permute-start | bytes 2752520 | tf_op jit(solution)/shard_map/ppermute | solution.py:771
  135.8 2.1 collective-permute-done.1
  137.9 1.2 add_convert_fusion
  139.1 8.7 %all-to-all-start.3 = ((bf16[16,32,896]{2,1,0:T(8,128)(2,1)}), bf16[16,32,896]{2,1,0:T(8,128)(2,1)}, u32[]{:S(2)}, u32[]{:S(2)}) async-start(bf16[16,32,896]{2,1,0:T(8,128)(2,1)} %add_convert_fusion), calls=%async_computation.4 | async-start | bytes 1835008 | tf_op jit(solution)/shard_map/all_to_all | solution.py:36
  147.8 1.6 copy-done.15
  149.4 1.2 shard_map.161
  151.6 1.8 copy-done.3
  153.4 1.2 copy-done.17
  154.6 5.7 %shard_map.162.grads_in = bf16[16,224,128]{2,1,0:T(8,128)(2,1)S(1)} custom-call(s32[1,1]{1,0:T(1,128)} %bitcast.2.first, s32[8,128]{1,0:T(8,128)S(1)} %stack.12.ids, bf16[3712,128]{1,0:T(8,128)(2,1)S(1)} %copy-done.17, bf16[49,29,128]{2,1,0:T(8,128)(2,1)S(1)} %bitcast.42, bf16[8,1376,128]{2,1,0:T(8,128)(2,1)S(1)} %bitcast.38, bf16[8,1376,128]{2,1,0:T(8,128)(2,1)S(1)} %copy-done.3), custom_call_target="tpu_custom_call" | custom-call | tf_op jit(solution)/shard_map/pallas_call | solution.py:796
  161.2 9.9 %all-to-all-done.3.parts = bf16[16,32,896]{2,1,0:T(8,128)(2,1)} async-done(((bf16[16,32,896]{2,1,0:T(8,128)(2,1)}), bf16[16,32,896]{2,1,0:T(8,128)(2,1)}, u32[]{:S(2)}, u32[]{:S(2)}) %all-to-all-start.3) | async-done | bytes 917536 | tf_op jit(solution)/shard_map/all_to_all | solution.py:36
  171.1 1.2 copy-done.5
  172.3 1.8 shard_map.163
  175.0 3.6 %all-to-all-start.4 = ((bf16[16,224,128]{2,1,0:T(8,128)(2,1)}), bf16[16,224,128]{2,1,0:T(8,128)(2,1)S(1)}, u32[]{:S(2)}, u32[]{:S(2)}) async-start(bf16[16,224,128]{2,1,0:T(8,128)(2,1)} %copy-done.6), calls=%async_computation.5 | async-start | bytes 1835008 | tf_op jit(solution)/shard_map/all_to_all | solution.py:36
  178.7 6.0 %reduce-scatter.2.cloned.1.call-done = bf16[1,416,128]{2,1,0:T(8,128)(2,1)} async-done(((bf16[8,416,128]{2,1,0:T(8,128)(2,1)}), bf16[1,416,128]{2,1,0:T(8,128)(2,1)}) %reduce-scatter.2.cloned.1.call-update) | async-done | bytes 106512 | tf_op jit(solution)/shard_map/reduce_scatter | solution.py:784
  185.5 3.1 %collective-permute-start.2 = (bf16[208,128]{1,0:T(8,128)(2,1)S(1)}, bf16[208,128]{1,0:T(8,128)(2,1)S(1)}, u32[]{:S(2)}, u32[]{:S(2)}) collective-permute-start(bf16[208,128]{1,0:T(8,128)(2,1)S(1)} %get-tuple-element.44), channel_id=1, source_target_pairs={{0,1},{1,0},{2,3},{3,2},{4,5},{5,4},{6,7},{7,6},{8,9},{9,8},{10,11... | collective-permute-start | bytes 159752 | tf_op jit(solution)/shard_map/ppermute | solution.py:789
  188.7 2.5 %collective-permute-done.2 = bf16[208,128]{1,0:T(8,128)(2,1)S(1)} collective-permute-done((bf16[208,128]{1,0:T(8,128)(2,1)S(1)}, bf16[208,128]{1,0:T(8,128)(2,1)S(1)}, u32[]{:S(2)}, u32[]{:S(2)}) %collective-permute-start.2) | collective-permute-done | bytes 53280 | tf_op jit(solution)/shard_map/ppermute | solution.py:789
  192.0 8.7 %all-to-all-done.4.parts = bf16[16,224,128]{2,1,0:T(8,128)(2,1)S(1)} async-done(((bf16[16,224,128]{2,1,0:T(8,128)(2,1)}), bf16[16,224,128]{2,1,0:T(8,128)(2,1)S(1)}, u32[]{:S(2)}, u32[]{:S(2)}) %all-to-all-start.4) | async-done | bytes 917536 | tf_op jit(solution)/shard_map/all_to_all | solution.py:36
  (72 shorter events, 11.8 us)
Async XLA Ops:
  7.2 82.2 %all-gather.4.cloned.1.call-start = ((), (), s32[]{:S(2)}) async-start(), calls=%async_computation.7 | async-start | bytes 3170304 | tf_op jit(solution)/shard_map/all_gather | solution.py:648
  7.2 0.7 copy-start.19
  10.7 35.5 %copy-start.24 = (f32[1,4,49,128]{3,1,2,0:T(4,128)S(1)}, f32[1,4,49,128]{3,1,2,0:T(4,128)}, u32[]{:S(2)}) copy-start(f32[1,4,49,128]{3,1,2,0:T(4,128)} %param.19) | copy-start | bytes 301060
  10.7 35.6 %copy-start.25 = (bf16[1,4,49,128]{3,1,2,0:T(4,128)(2,1)S(1)}, bf16[1,4,49,128]{3,1,2,0:T(4,128)(2,1)}, u32[]{:S(2)}) copy-start(bf16[1,4,49,128]{3,1,2,0:T(4,128)(2,1)} %param.13) | copy-start | bytes 150532
  46.6 49.3 %copy-start.26 = (s32[1,128]{1,0:T(1,128)S(1)}, s32[1,128]{1,0:T(1,128)}, u32[]{:S(2)}) copy-start(s32[1,128]{1,0:T(1,128)} %param.16) | copy-start | bytes 1540
  46.6 49.2 %copy-start.27 = (s32[1,128]{1,0:T(1,128)S(1)}, s32[1,128]{1,0:T(1,128)}, u32[]{:S(2)}) copy-start(s32[1,128]{1,0:T(1,128)} %param.17) | copy-start | bytes 1540
  46.6 49.3 %copy-start.10 = (bf16[1,29,49,128]{3,1,2,0:T(8,128)(2,1)S(1)}, bf16[1,29,49,128]{3,1,2,0:T(8,128)(2,1)}, u32[]{:S(2)}) copy-start(bf16[1,29,49,128]{3,1,2,0:T(8,128)(2,1)} %param.18) | copy-start | bytes 1091332
  89.4 10.8 %copy-start.18 = (bf16[128,8]{0,1:T(8,128)(2,1)S(1)}, bf16[128,8]{0,1:T(8,128)(2,1)}, u32[]{:S(2)}) copy-start(bf16[128,8]{0,1:T(8,128)(2,1)} %param.25) | copy-start | bytes 6148
  89.4 10.8 %collective-permute-start = (bf16[8,1376,128]{2,1,0:T(8,128)(2,1)}, bf16[8,1376,128]{2,1,0:T(8,128)(2,1)S(1)}, u32[]{:S(2)}, u32[]{:S(2)}) collective-permute-start(bf16[8,1376,128]{2,1,0:T(8,128)(2,1)} %bitcast.36), channel_id=1, source_target_pairs={{0,16},{16,0},{1,17},{17,1},{2,18},{18,2},{3,19},{19,3},{4,20},{20... | collective-permute-start | bytes 8454152 | tf_op jit(solution)/shard_map/ppermute | solution.py:690
  95.9 1.4 copy-start.7
  99.7 10.2 %copy-start.8 = (bf16[49,128,128]{2,1,0:T(8,128)(2,1)}, bf16[49,128,128]{2,1,0:T(8,128)(2,1)S(1)}, u32[]{:S(2)}) copy-start(bf16[49,128,128]{2,1,0:T(8,128)(2,1)S(1)} %get-tuple-element.27.edge_in) | copy-start | bytes 4816900
  99.7 10.2 %copy-start.11 = (bf16[29,128,128]{2,1,0:T(8,128)(2,1)}, bf16[29,128,128]{2,1,0:T(8,128)(2,1)S(1)}, u32[]{:S(2)}) copy-start(bf16[29,128,128]{2,1,0:T(8,128)(2,1)S(1)} %get-tuple-element.26.z) | copy-start | bytes 2850820
  100.2 9.8 %copy-start.2 = (bf16[8,1376,128]{2,1,0:T(8,128)(2,1)}, bf16[8,1376,128]{2,1,0:T(8,128)(2,1)S(1)}, u32[]{:S(2)}) copy-start(bf16[8,1376,128]{2,1,0:T(8,128)(2,1)S(1)} %collective-permute-done.other) | copy-start | bytes 8454148
  100.2 3.2 %copy-start = (bf16[11008,128]{1,0:T(8,128)(2,1)S(1)}, bf16[11008,128]{1,0:T(8,128)(2,1)}, u32[]{:S(2)}) copy-start(bf16[11008,128]{1,0:T(8,128)(2,1)} %all-gather.4.cloned.1.call-done) | copy-start | bytes 8454148
  110.0 1.2 copy-start.14
  111.1 14.1 %all-to-all-start.2 = ((f32[16,8,128]{2,1,0:T(8,128)}), f32[16,8,128]{2,1,0:T(8,128)S(1)}, u32[]{:S(2)}, u32[]{:S(2)}) async-start(f32[16,8,128]{2,1,0:T(8,128)} %get-tuple-element.30), calls=%async_computation.2 | async-start | bytes 131072 | tf_op jit(solution)/shard_map/all_to_all | solution.py:36
  125.2 1.4 copy-start.9
  126.6 1.2 copy-start.12
  131.5 1.0 copy-start.16
  132.5 5.4 %collective-permute-start.1 = (bf16[16,32,896]{2,1,0:T(8,128)(2,1)S(1)}, bf16[16,32,896]{2,1,0:T(8,128)(2,1)S(1)}, u32[]{:S(2)}, u32[]{:S(2)}) collective-permute-start(bf16[16,32,896]{2,1,0:T(8,128)(2,1)S(1)} %get-tuple-element.34), channel_id=1, source_target_pairs={{0,16},{16,0},{1,17},{17,1},{2,18},{18,2},{3,19},{19,3},{4,20},{20... | collective-permute-start | bytes 2752520 | tf_op jit(solution)/shard_map/ppermute | solution.py:771
  139.1 32.1 %all-to-all-start.3 = ((bf16[16,32,896]{2,1,0:T(8,128)(2,1)}), bf16[16,32,896]{2,1,0:T(8,128)(2,1)}, u32[]{:S(2)}, u32[]{:S(2)}) async-start(bf16[16,32,896]{2,1,0:T(8,128)(2,1)} %add_convert_fusion), calls=%async_computation.4 | async-start | bytes 1835008 | tf_op jit(solution)/shard_map/all_to_all | solution.py:36
  147.8 3.8 %copy-start.1 = (bf16[11008,128]{1,0:T(8,128)(2,1)S(1)}, bf16[11008,128]{1,0:T(8,128)(2,1)}, u32[]{:S(2)}) copy-start(bf16[11008,128]{1,0:T(8,128)(2,1)} %all-gather.4.cloned.1.call-done) | copy-start | bytes 8454148
  147.8 36.9 %reduce-scatter.2.cloned.1.call-start = ((), (), s32[]{:S(2)}) async-start(), calls=%async_computation.6 | async-start | bytes 958464 | tf_op jit(solution)/shard_map/reduce_scatter | solution.py:784
  147.8 1.6 copy-start.15
  150.6 0.9 copy-start.13
  151.6 1.8 copy-start.3
  153.4 1.2 copy-start.17
  160.3 0.9 copy-start.4
  171.1 1.2 copy-start.5
  174.1 0.9 copy-start.6
  175.0 25.7 %all-to-all-start.4 = ((bf16[16,224,128]{2,1,0:T(8,128)(2,1)}), bf16[16,224,128]{2,1,0:T(8,128)(2,1)S(1)}, u32[]{:S(2)}, u32[]{:S(2)}) async-start(bf16[16,224,128]{2,1,0:T(8,128)(2,1)} %copy-done.6), calls=%async_computation.5 | async-start | bytes 1835008 | tf_op jit(solution)/shard_map/all_to_all | solution.py:36
  185.5 5.7 %collective-permute-start.2 = (bf16[208,128]{1,0:T(8,128)(2,1)S(1)}, bf16[208,128]{1,0:T(8,128)(2,1)S(1)}, u32[]{:S(2)}, u32[]{:S(2)}) collective-permute-start(bf16[208,128]{1,0:T(8,128)(2,1)S(1)} %get-tuple-element.44), channel_id=1, source_target_pairs={{0,1},{1,0},{2,3},{3,2},{4,5},{5,4},{6,7},{7,6},{8,9},{9,8},{10,11... | collective-permute-start | bytes 159752 | tf_op jit(solution)/shard_map/ppermute | solution.py:789
  (4 other events, 2.8 us)
Sparse Core Ops, SparseCore 0:
  45.6 43.6 all-gather.3
  151.7 32.9 reduce-scatter.1

commit v5 on v4

--- a/solution.py
+++ b/solution.py
@@ -49,7 +49,14 @@
 CHUNK = 32
 VMEM = pl.BlockSpec(memory_space=pltpu.VMEM)
 HBM = pl.BlockSpec(memory_space=pltpu.HBM)
-PARAMS = pltpu.CompilerParams(vmem_limit_bytes=28 * 1024 * 1024)
+SMALL = pltpu.CompilerParams(vmem_limit_bytes=28 * 1024 * 1024)
+LARGE = pltpu.CompilerParams(vmem_limit_bytes=48 * 1024 * 1024)
+WHOLE = pltpu.CompilerParams(vmem_limit_bytes=60 * 1024 * 1024)
+EDGE_PART = (0, COEF)
+MESSAGE_PART = (COEF, COEF)
+CONV_PART = (2 * COEF, REDUCED)
+ZERO_PART = (2 * COEF + REDUCED, LMAX + 1)
+SPILL = 1200
 
 
 def nt_dot(left, right):
@@ -71,6 +78,10 @@
     heads, edges = values.shape
     wide = jnp.broadcast_to(values[:, None, :], (heads, channels // heads, edges))
     return wide.reshape(channels, edges)
+
+
+def part_of(spill, part):
+    return spill.at[pl.ds(part[0], part[1])]
 
 
 def chunks(channels, body):
@@ -205,16 +216,19 @@
         lay(sets[1])
 
 
-def message_kernel(ids, stats, every, msg, out):
+def message_kernel(ids, stats, every, spill, out, msg, sem):
+    copy = pltpu.make_async_copy(part_of(spill, MESSAGE_PART), msg, sem.at[0])
+    copy.start()
     group = out.shape[0]
     count = stats.shape[1] // 2
     total = jnp.sum(every[:, :, :count], axis=0)
     share = stats[:, :count] / jnp.where(total > 0.0, total, 1.0)
     scale = widen(share, LANES).T
+    copy.wait()
     by_owner(hot_rows(ids[1:2, :], count).astype(bf16), msg, out, group, scale)
 
 
-def rotate_kernel(own, ids, nodes, wigner, z, edge_out, paired, wide, grad_edge, out_sem):
+def rotate_kernel(own, ids, nodes, wigner, z, spill, paired, wide, grad_edge, out_sem):
     group, edges = nodes.shape[0], wigner.shape[2]
     channels = LANES
     per = 16 // (2 * own)
@@ -232,7 +246,7 @@
             paired[j] = half_dot(here, both).astype(bf16).astype(f32)
             here = rows[:, at + 1].reshape(count, channels).T.astype(bf16)
             grad_edge[j] = half_dot(here, target).astype(bf16)
-    copy = pltpu.make_async_copy(grad_edge, edge_out, out_sem.at[0])
+    copy = pltpu.make_async_copy(grad_edge, part_of(spill, EDGE_PART), out_sem.at[0])
     copy.start()
     for l in range(LMAX + 1):
         for k in ROWS_OF[l]:
@@ -241,7 +255,12 @@
                 term = wide[j, k : k + 1, :] * paired[j]
                 acc = term if acc is None else acc + term
             z[k] = acc.astype(bf16)
+    zero_copy = pltpu.make_async_copy(
+        z.at[pl.ds(0, LMAX + 1)], part_of(spill, ZERO_PART), out_sem.at[1]
+    )
+    zero_copy.start()
     copy.wait()
+    zero_copy.wait()
 
 
 def forward_kernel(
@@ -251,11 +270,11 @@
     ids,
     z,
     wigner,
-    edge_in,
+    spill_in,
     attention_t,
     mine,
     other,
-    messages,
+    spill,
     stats,
     sent,
     scalar,
@@ -274,7 +293,7 @@
     heads = attention_t.shape[0]
     count = stats.shape[1] // 2
     start_weights(places, first[0, 0], mine, other, held, sems)
-    edge_copy = pltpu.make_async_copy(edge_in, grad_edge, out_sem.at[1])
+    edge_copy = pltpu.make_async_copy(part_of(spill_in, EDGE_PART), grad_edge, out_sem.at[1])
     edge_copy.start()
     wide[...] = wigner[...].astype(f32)
     base, rows = ZERO
@@ -327,7 +346,7 @@
 
     edge_copy.wait()
     chunks(channels, body)
-    copy = pltpu.make_async_copy(msg, messages, out_sem.at[0])
+    copy = pltpu.make_async_copy(msg, part_of(spill, MESSAGE_PART), out_sem.at[0])
     copy.start()
     grad_norm = jnp.sum(heads_acc[...].reshape(heads, channels // heads, edges), axis=1)
     own_shared = nt_full(own_norm * grad_norm, target)
@@ -348,11 +367,10 @@
     scalar,
     per_edge,
     wigner,
-    edge_in,
+    spill_in,
     attention,
     attention_t,
-    z,
-    grad_out,
+    spill,
     mine,
     theirs,
     wide,
@@ -361,13 +379,16 @@
     turned,
     grad_conv,
     grad_edge,
+    z,
     out_sem,
 ):
     channels, edges = LANES, wigner.shape[2]
     heads = attention_t.shape[0]
     count = stats.shape[1] // 2
-    edge_copy = pltpu.make_async_copy(edge_in, grad_edge, out_sem.at[1])
+    edge_copy = pltpu.make_async_copy(part_of(spill_in, EDGE_PART), grad_edge, out_sem.at[1])
     edge_copy.start()
+    zero_copy = pltpu.make_async_copy(part_of(spill_in, ZERO_PART), z, out_sem.at[2])
+    zero_copy.start()
     wide[...] = wigner[...].astype(f32)
     total = jnp.sum(every[:, :, :count], axis=0)
     total = jnp.where(total > 0.0, total, 1.0)
@@ -405,10 +426,13 @@
     grad[:channels, :] = grad[:channels, :] + grad_scalar
     depth = (LMAX + 1) * channels
     parts, share = mine.shape[0], depth // (2 * mine.shape[0])
-    grad_conv[...] = grad[...].astype(bf16)
-    copy = pltpu.make_async_copy(grad_conv, grad_out, out_sem.at[0])
+    grad_conv[...] = grad[...].astype(bf16).reshape(grad_conv.shape)
+    copy = pltpu.make_async_copy(grad_conv, part_of(spill, CONV_PART), out_sem.at[0])
     copy.start()
-    turned[:depth, :] = nt_dot(grad_conv[:depth, :], z[: LMAX + 1].reshape(depth, edges))
+    zero_copy.wait()
+    turned[:depth, :] = nt_dot(
+        grad_conv[: LMAX + 1].reshape(depth, edges), z[...].reshape(depth, edges)
+    )
     turned[depth:, :] = jnp.zeros((turned.shape[0] - depth, depth), f32)
     padded = mine.shape[1]
     tail_row = lax.broadcasted_iota(jnp.int32, (padded, depth), 0)
@@ -442,7 +466,7 @@
     own,
     first,
     ids,
-    grad_conv,
+    spill,
     wigner,
     mine,
     other,
@@ -454,14 +478,18 @@
     grad,
     grad_rows,
     grads,
+    grad_conv,
     sems,
     out_sem,
 ):
     channels, edges = LANES, wigner.shape[2]
     count = own * group
+    conv_copy = pltpu.make_async_copy(part_of(spill, CONV_PART), grad_conv, out_sem.at[1])
+    conv_copy.start()
     start_weights(places, first[0, 0], mine, other, held, sems)
     wide[...] = wigner[...].astype(f32)
-    grad[...] = grad_conv[...].astype(f32)
+    conv_copy.wait()
+    grad[...] = grad_conv[...].astype(f32).reshape(grad.shape)
     zs = held.shape[1]
     for base, rows in (ZERO, ONE, (ONE[0] + ONE[1], ONE[1]), TWO, (TWO[0] + TWO[1], TWO[1])):
         size = rows * channels // (2 * zs)
@@ -621,7 +649,7 @@
         out_specs=VMEM,
         scratch_shapes=[pltpu.VMEM(w.shape[::-1], bf16) for w in shards]
         + [pltpu.VMEM((most, 2 * lanes), f32), pltpu.SemaphoreType.DMA((len(shards),))],
-        compiler_params=PARAMS,
+        compiler_params=WHOLE,
     )(*[w.T for w in shards])
     core = lax.axis_index("core")
     near = lax.all_gather(packed, "core")
@@ -643,7 +671,7 @@
         out_shape=jax.ShapeDtypeStruct((depth, LANES), bf16),
         in_specs=[pl.BlockSpec(memory_space=pltpu.SMEM), VMEM],
         out_specs=VMEM,
-        compiler_params=PARAMS,
+        compiler_params=SMALL,
     )(core.astype(jnp.int32).reshape(1, 1), slabs)
     return lax.all_gather(tiled, "z"), places, tiled
 
@@ -692,34 +720,35 @@
     smem = pl.BlockSpec(memory_space=pltpu.SMEM)
     field = (channels, edge_rows)
     wide = pltpu.VMEM(rotation.shape, f32)
+    spill_shape = jax.ShapeDtypeStruct((SPILL,) + field, bf16)
     out_copy = pltpu.SemaphoreType.DMA((1,))
     two_copies = pltpu.SemaphoreType.DMA((2,))
     edge_field = pltpu.VMEM((COEF,) + field, bf16)
-    z, grad_edge = pl.pallas_call(
+    z, spill = pl.pallas_call(
         functools.partial(rotate_kernel, row_count),
         out_shape=(
             jax.ShapeDtypeStruct((REDUCED,) + field, bf16),
-            jax.ShapeDtypeStruct((COEF,) + field, bf16),
+            spill_shape,
         ),
         in_specs=[VMEM] * 3,
         out_specs=[VMEM, HBM],
         scratch_shapes=[
             pltpu.VMEM((COEF,) + field, f32),
             wide,
-            pltpu.VMEM((COEF,) + field, bf16),
-            out_copy,
+            edge_field,
+            two_copies,
         ],
-        compiler_params=PARAMS,
+        compiler_params=LARGE,
     )(ids, nodes, rotation)
     held = pltpu.VMEM((2,) + half.shape, bf16)
     copies = pltpu.SemaphoreType.DMA((len(places),))
 
     span = node_rows(row_count)
     sums = (head_count, 2 * all_nodes)
-    messages, stats, sent, scalar, per_edge = pl.pallas_call(
+    spill, stats, sent, scalar, per_edge = pl.pallas_call(
         functools.partial(forward_kernel, places, group),
         out_shape=(
-            jax.ShapeDtypeStruct((COEF,) + field, bf16),
+            spill_shape,
             jax.ShapeDtypeStruct(sums, f32),
             jax.ShapeDtypeStruct((group,) + sums, f32),
             jax.ShapeDtypeStruct(field, f32),
@@ -738,8 +767,9 @@
             copies,
             two_copies,
         ],
-        compiler_params=PARAMS,
-    )(first, ids, z, rotation, grad_edge, attention_t, half, other)
+        input_output_aliases={4: 0},
+        compiler_params=LARGE,
+    )(first, ids, z, rotation, spill, attention_t, half, other)
     every = exchange(sent, GRAPH)
 
     columns = lax.axis_size(COLUMN_GROUP)
@@ -747,39 +777,42 @@
     share = depth // (2 * columns)
     padded = -(-(share + 2) // 16) * 16
     partial = jax.ShapeDtypeStruct((columns, padded, depth), bf16)
-    grad_conv, mine, theirs = pl.pallas_call(
+    spill, mine, theirs = pl.pallas_call(
         backward_kernel,
         out_shape=(
-            jax.ShapeDtypeStruct((REDUCED * channels, edge_rows), bf16),
+            spill_shape,
             partial,
             partial,
         ),
-        in_specs=[smem] + [VMEM] * 6 + [HBM] + [VMEM] * 3,
+        in_specs=[smem] + [VMEM] * 6 + [HBM] + [VMEM] * 2,
         out_specs=[HBM] + [VMEM] * 2,
         scratch_shapes=[
             wide,
             pltpu.VMEM(field, f32),
             pltpu.VMEM((REDUCED * channels, edge_rows), f32),
             pltpu.VMEM((depth + padded, depth), f32),
-            pltpu.VMEM((REDUCED * channels, edge_rows), bf16),
+            pltpu.VMEM((REDUCED,) + field, bf16),
             edge_field,
-            two_copies,
+            pltpu.VMEM((LMAX + 1,) + field, bf16),
+            pltpu.SemaphoreType.DMA((3,)),
         ],
-        compiler_params=PARAMS,
-    )(first, ids, stats, every, scalar, per_edge, rotation, grad_edge, attention, attention_t, z)
+        input_output_aliases={7: 0},
+        compiler_params=LARGE,
+    )(first, ids, stats, every, scalar, per_edge, rotation, spill, attention, attention_t)
 
     theirs = lax.ppermute(theirs, "core", [(0, 1), (1, 0)])
     mine = (mine.astype(f32) + theirs.astype(f32)).astype(bf16)
-    mine, messages = lax.optimization_barrier((mine, messages))
+    mine, spill = lax.optimization_barrier((mine, spill))
     zero_parts = exchange(mine, COLUMN_GROUP)
     message_sums = pl.pallas_call(
         message_kernel,
         out_shape=jax.ShapeDtypeStruct((group, span, channels), bf16),
-        in_specs=[VMEM] * 4,
+        in_specs=[VMEM] * 3 + [HBM],
         out_specs=VMEM,
-        compiler_params=PARAMS,
-    )(ids, stats, every, messages)
-    message_sums, grad_conv = lax.optimization_barrier((message_sums, grad_conv))
+        scratch_shapes=[edge_field, out_copy],
+        compiler_params=LARGE,
+    )(ids, stats, every, spill)
+    message_sums, spill = lax.optimization_barrier((message_sums, spill))
     message_sums = message_sums.reshape(group // 2, 2 * span, channels)
     near_sums = lax.psum_scatter(message_sums, "y", scatter_dimension=0, tiled=True)
     near_sums = near_sums.reshape(2, span, channels)
@@ -798,7 +831,7 @@
         out_shape=jax.ShapeDtypeStruct(
             (group, -(-(used + tail_rows) // 16) * 16, channels), bf16
         ),
-        in_specs=[smem] + [VMEM] * 3 + [HBM] * 2,
+        in_specs=[smem, VMEM, HBM, VMEM] + [HBM] * 2,
         out_specs=HBM,
         scratch_shapes=[
             held,
@@ -808,11 +841,12 @@
             pltpu.VMEM((REDUCED * channels, edge_rows), f32),
             pltpu.VMEM((edge_rows, REDUCED * channels), bf16),
             pltpu.VMEM((group, span, channels), bf16),
+            pltpu.VMEM((REDUCED,) + field, bf16),
             copies,
-            out_copy,
+            two_copies,
         ],
-        compiler_params=PARAMS,
-    )(first, ids, grad_conv, rotation, half, other)
+        compiler_params=LARGE,
+    )(first, ids, spill, rotation, half, other)
     nodes_shape = jax.ShapeDtypeStruct((harmonics, row_count, channels), bf16)
     batch_scale = 1.0 / (2 * columns)
     if beside:
@@ -829,7 +863,7 @@
                 pltpu.VMEM((group, window, channels), bf16),
                 two_copies,
             ],
-            compiler_params=PARAMS,
+            compiler_params=SMALL,
         )(zero_parts, grad_sums)
         last = exchange(grad_sums, GRAPH)
         grad_nodes, grad_zero, grad_att = pl.pallas_call(
@@ -842,7 +876,7 @@
             in_specs=[VMEM],
             out_specs=[VMEM] * 3,
             scratch_shapes=[pltpu.VMEM(last.shape[1:], f32)],
-            compiler_params=PARAMS,
+            compiler_params=SMALL,
         )(last)
         grad_zero, grad_att = grad_zero.T, grad_att.T
     else:
@@ -863,7 +897,7 @@
             in_specs=[VMEM],
             out_specs=[VMEM] * 2,
             scratch_shapes=[pltpu.VMEM(last.shape[1:], f32)],
-            compiler_params=PARAMS,
+            compiler_params=SMALL,
         )(last)
         tail = tail * batch_scale
         zero_rows = share * lanes // LANES

time: 212 us -> 206 us (0.972)
  local copies, waits for them, and re-layouts: 22.8 us -> 7.2 us
  Pallas kernels: 26.9 us -> 34.1 us
  waiting for transfers between devices: 37.6 us -> 41.4 us
    unnamed x57 -> x25, local copies, waits for them, and re-layouts: 21.6 us -> 5.92 us
    all_to_all x3, waiting for transfers between devices: 26.4 us -> 29.3 us  [exchange(): return lax.all_to_all(blocks, axes, split_axis=0, concat_axis=0, tiled=True)]
  transfers between devices with their start and end apart: 8 -> 8, of which waited for: 7 -> 7; matrix products, arithmetic and copies ran while one was open for 1% -> 1% of each run, Pallas kernels for 5% -> 7%
where the time goes in v5:
time: 206 us; the launch traced here: 203 us
  blocking collectives  73.7 us (36%)
  waiting for transfers between devices  41.4 us (20%)
  Pallas kernels  34.1 us (17%)
  starting transfers between devices  29 us (14%)
  between operations  15.7 us (8%)
  local copies, waits for them, and re-layouts  7.2 us (3%)
    all_to_all x2, blocking collectives, gather(): return lax.all_to_all(copies, axes, split_axis=0, concat_axis=0, tiled=True)  65.1 us
    all_to_all x3, waiting for transfers between devices, exchange(): return lax.all_to_all(blocks, axes, split_axis=0, concat_axis=0, tiled=True)  29.3 us
    all_to_all x3, starting transfers between devices, exchange(): return lax.all_to_all(blocks, axes, split_axis=0, concat_axis=0, tiled=True)  18.7 us
    all_gather x1, blocking collectives, gather_weights(): near = lax.all_gather(packed, 'core')  8.58 us
    pallas_call x1, Pallas kernels, on_device(): pl.pallas_call(functools.partial(forward_kernel, places, group), out_shap...  8.06 us
    pallas_call x1, Pallas kernels, on_device(): pl.pallas_call(functools.partial(scatter_kernel, places, group, row_count...  6.61 us
    reduce_scatter x1, waiting for transfers between devices, on_device(): lax.psum_scatter(message_sums, 'y', scatter_dimension=0, tiled=True)  6.61 us
    unnamed x25, local copies, waits for them, and re-layouts  5.92 us
  transfers between devices with their start and end apart: 8, of which 7 were waited for; matrix products, arithmetic and copies ran while one was open for 1% of the time, Pallas kernels for 7%

profile of v5, /device:TPU:1, one launch (start us, length us, event | category | flops | bytes accessed | tf_op | source)
XLA Modules:
  0.0 203.0 jit_solution(2634036562784842413)
XLA Ops:
  7.2 2.0 shard_map.156
  9.2 8.6 %all-gather = bf16[64,256]{1,0:T(8,128)(2,1)S(1)} all-gather(bf16[32,256]{1,0:T(8,128)(2,1)} %shard_map.156), channel_id=2, replica_groups=mesh['xh'=2,'z'=8,'core'=2,'y'=8,'xl'=2] {'core'}, dimensions={0}, use_global_device_ids=true | all-gather | bytes 49152 | tf_op jit(solution)/shard_map/all_gather | solution.py:655
  17.9 21.5 %all_to_all.25.slabs = bf16[32,64,128]{2,1,0:T(8,128)(2,1)S(1)} all-to-all(bf16[32,64,128]{2,1,0:T(8,128)(2,1)S(1)} %broadcast_in_dim.39), channel_id=1, replica_groups=mesh['xh'=2,'z'=8,'core'=2,'y'=8,'xl'=2] {'xh','y','xl'}, dimensions={0} | all-to-all | bytes 1048576 | tf_op jit(solution)/shard_map/all_to_all | solution.py:32
  39.4 4.1 %shard_map.157 = bf16[1376,128]{1,0:T(8,128)(2,1)} custom-call(s32[1,1]{1,0:T(1,128)} %bitcast.2.first, bf16[32,64,128]{2,1,0:T(8,128)(2,1)S(1)} %all_to_all.25.slabs), custom_call_target="tpu_custom_call" | custom-call | tf_op jit(solution)/shard_map/pallas_call | solution.py:669
  44.7 43.6 %all_to_all.26.nodes = bf16[16,400,128]{2,1,0:T(8,128)(2,1)S(1)} all-to-all(bf16[16,400,128]{2,1,0:T(8,128)(2,1)S(1)} %broadcast_in_dim.42), channel_id=1, replica_groups=mesh['xh'=2,'z'=8,'core'=2,'y'=8,'xl'=2] {'y','xl'}, dimensions={0} | all-to-all | bytes 3276800 | tf_op jit(solution)/shard_map/all_to_all | solution.py:32
  88.3 4.3 %collective-permute-start = (bf16[8,1376,128]{2,1,0:T(8,128)(2,1)}, bf16[8,1376,128]{2,1,0:T(8,128)(2,1)}, u32[]{:S(2)}, u32[]{:S(2)}) collective-permute-start(bf16[8,1376,128]{2,1,0:T(8,128)(2,1)} %bitcast.36), channel_id=1, source_target_pairs={{0,16},{16,0},{1,17},{17,1},{2,18},{18,2},{3,19},{19,3},{4,20},{20... | collective-permute-start | bytes 8454152 | tf_op jit(solution)/shard_map/ppermute | solution.py:718
  93.4 3.8 %shard_map.158 = (bf16[29,128,128]{2,1,0:T(8,128)(2,1)S(1)}, bf16[1200,128,128]{2,1,0:T(8,128)(2,1)}) custom-call(s32[8,128]{1,0:T(8,128)S(1)} %stack.12.ids, bf16[16,400,128]{2,1,0:T(8,128)(2,1)S(1)} %all_to_all.26.nodes, bf16[49,29,128]{2,1,0:T(8,128)(2,1)S(1)} %bitcast.39), custom_call_target="tpu_custom_call" | custom-call | tf_op jit(solution)/shard_map/pallas_call | solution.py:727
  97.8 1.8 copy-done
  99.6 8.1 %shard_map.159 = (bf16[1200,128,128]{2,1,0:T(8,128)(2,1)}, f32[8,128]{1,0:T(8,128)S(1)}, f32[16,8,128]{2,1,0:T(8,128)}, f32[128,128]{1,0:T(8,128)S(1)}, f32[16,128]{1,0:T(8,128)S(1)}) custom-call(s32[1,1]{1,0:T(1,128)} %bitcast.2.first, s32[8,128]{1,0:T(8,128)S(1)} %stack.12.ids, ...), custom_call_target="tpu_custom_call", output_to_operand_aliasing={{0}: (4, {})} | custom-call | tf_op jit(solution)/shard_map/pallas_call | solution.py:748
  107.7 6.7 %all-to-all-start.2 = ((f32[16,8,128]{2,1,0:T(8,128)}), f32[16,8,128]{2,1,0:T(8,128)S(1)}, u32[]{:S(2)}, u32[]{:S(2)}) async-start(f32[16,8,128]{2,1,0:T(8,128)} %get-tuple-element.30), calls=%async_computation.2 | async-start | bytes 131072 | tf_op jit(solution)/shard_map/all_to_all | solution.py:36
  114.5 8.0 %all-to-all-done.2.every = f32[16,8,128]{2,1,0:T(8,128)S(1)} async-done(((f32[16,8,128]{2,1,0:T(8,128)}), f32[16,8,128]{2,1,0:T(8,128)S(1)}, u32[]{:S(2)}, u32[]{:S(2)}) %all-to-all-start.2) | async-done | bytes 65568 | tf_op jit(solution)/shard_map/all_to_all | solution.py:36
  122.6 4.1 %shard_map.160 = (bf16[1200,128,128]{2,1,0:T(8,128)(2,1)}, bf16[16,32,896]{2,1,0:T(8,128)(2,1)S(1)}, bf16[16,32,896]{2,1,0:T(8,128)(2,1)S(1)}) custom-call(s32[1,1]{1,0:T(1,128)} %bitcast.2.first, s32[8,128]{1,0:T(8,128)S(1)} %stack.12.ids, f32[8,128]{1,0:T(8,128)S(1)} %get-tuple-element.29.stats, ...), custom_call_target="tpu_custom_call", output_to_operand_aliasing={{0}: (7, {})} | custom-call | tf_op jit(solution)/shard_map/pallas_call | solution.py:780
  126.7 3.0 %collective-permute-start.1 = (bf16[16,32,896]{2,1,0:T(8,128)(2,1)S(1)}, bf16[16,32,896]{2,1,0:T(8,128)(2,1)S(1)}, u32[]{:S(2)}, u32[]{:S(2)}) collective-permute-start(bf16[16,32,896]{2,1,0:T(8,128)(2,1)S(1)} %get-tuple-element.35), channel_id=1, source_target_pairs={{0,16},{16,0},{1,17},{17,1},{2,18},{18,2},{3,19},{19,3},{4,20},{20... | collective-permute-start | bytes 2752520 | tf_op jit(solution)/shard_map/ppermute | solution.py:803
  129.7 2.1 %collective-permute-done.1 = bf16[16,32,896]{2,1,0:T(8,128)(2,1)S(1)} collective-permute-done((bf16[16,32,896]{2,1,0:T(8,128)(2,1)S(1)}, bf16[16,32,896]{2,1,0:T(8,128)(2,1)S(1)}, u32[]{:S(2)}, u32[]{:S(2)}) %collective-permute-start.1) | collective-permute-done | bytes 917536 | tf_op jit(solution)/shard_map/ppermute | solution.py:803
  131.8 1.1 add_convert_fusion
  132.9 8.4 %all-to-all-start.3 = ((bf16[16,32,896]{2,1,0:T(8,128)(2,1)}), bf16[16,32,896]{2,1,0:T(8,128)(2,1)}, u32[]{:S(2)}, u32[]{:S(2)}) async-start(bf16[16,32,896]{2,1,0:T(8,128)(2,1)} %add_convert_fusion), calls=%async_computation.4 | async-start | bytes 1835008 | tf_op jit(solution)/shard_map/all_to_all | solution.py:36
  141.5 2.8 %shard_map.161 = bf16[16,208,128]{2,1,0:T(8,128)(2,1)S(1)} custom-call(s32[8,128]{1,0:T(8,128)S(1)} %stack.12.ids, f32[8,128]{1,0:T(8,128)S(1)} %get-tuple-element.29.stats, f32[16,8,128]{2,1,0:T(8,128)S(1)} %all-to-all-done.2.every, bf16[1200,128,128]{2,1,0:T(8,128)(2,1)} %get-tuple-element.40.spill), custom_call_target="tpu_custom_call" | custom-call | tf_op jit(solution)/shard_map/pallas_call | solution.py:807
  144.4 0.9 copy-done.6
  145.3 6.6 %shard_map.162.grads_in = bf16[16,224,128]{2,1,0:T(8,128)(2,1)S(1)} custom-call(s32[1,1]{1,0:T(1,128)} %bitcast.2.first, s32[8,128]{1,0:T(8,128)S(1)} %stack.12.ids, bf16[1200,128,128]{2,1,0:T(8,128)(2,1)} %get-tuple-element.40.spill, bf16[49,29,128]{2,1,0:T(8,128)(2,1)S(1)} %bitcast.42, bf16[8,1376,128]{2,1,0:T(8,128)(2,1)S(1)} %bitcast.38, ...), custom_call_target="tpu_custom_call" | custom-call | tf_op jit(solution)/shard_map/pallas_call | solution.py:829
  152.0 0.9 copy-done.2
  152.9 11.8 %all-to-all-done.3.parts = bf16[16,32,896]{2,1,0:T(8,128)(2,1)} async-done(((bf16[16,32,896]{2,1,0:T(8,128)(2,1)}), bf16[16,32,896]{2,1,0:T(8,128)(2,1)}, u32[]{:S(2)}, u32[]{:S(2)}) %all-to-all-start.3) | async-done | bytes 917536 | tf_op jit(solution)/shard_map/all_to_all | solution.py:36
  164.7 1.2 copy-done.3
  165.8 1.8 shard_map.163
  167.6 0.9 copy-done.4
  168.6 3.6 %all-to-all-start.4 = ((bf16[16,224,128]{2,1,0:T(8,128)(2,1)}), bf16[16,224,128]{2,1,0:T(8,128)(2,1)S(1)}, u32[]{:S(2)}, u32[]{:S(2)}) async-start(bf16[16,224,128]{2,1,0:T(8,128)(2,1)} %copy-done.4), calls=%async_computation.5 | async-start | bytes 1835008 | tf_op jit(solution)/shard_map/all_to_all | solution.py:36
  172.2 6.6 %reduce-scatter.2.cloned.1.call-done = bf16[1,416,128]{2,1,0:T(8,128)(2,1)} async-done(((bf16[8,416,128]{2,1,0:T(8,128)(2,1)}), bf16[1,416,128]{2,1,0:T(8,128)(2,1)}) %reduce-scatter.2.cloned.1.call-update) | async-done | bytes 106512 | tf_op jit(solution)/shard_map/reduce_scatter | solution.py:817
  178.8 0.8 dynamic-slice_bitcast_fusion
  179.6 2.7 %collective-permute-start.2 = (bf16[208,128]{1,0:T(8,128)(2,1)S(1)}, bf16[208,128]{1,0:T(8,128)(2,1)S(1)}, u32[]{:S(2)}, u32[]{:S(2)}) collective-permute-start(bf16[208,128]{1,0:T(8,128)(2,1)S(1)} %get-tuple-element.44), channel_id=1, source_target_pairs={{0,1},{1,0},{2,3},{3,2},{4,5},{5,4},{6,7},{7,6},{8,9},{9,8},{10,11... | collective-permute-start | bytes 159752 | tf_op jit(solution)/shard_map/ppermute | solution.py:822
  182.4 2.8 %collective-permute-done.2 = bf16[208,128]{1,0:T(8,128)(2,1)S(1)} collective-permute-done((bf16[208,128]{1,0:T(8,128)(2,1)S(1)}, bf16[208,128]{1,0:T(8,128)(2,1)S(1)}, u32[]{:S(2)}, u32[]{:S(2)}) %collective-permute-start.2) | collective-permute-done | bytes 53280 | tf_op jit(solution)/shard_map/ppermute | solution.py:822
  185.2 0.7 fusion
  185.9 9.5 %all-to-all-done.4.parts = bf16[16,224,128]{2,1,0:T(8,128)(2,1)S(1)} async-done(((bf16[16,224,128]{2,1,0:T(8,128)(2,1)}), bf16[16,224,128]{2,1,0:T(8,128)(2,1)S(1)}, u32[]{:S(2)}, u32[]{:S(2)}) %all-to-all-start.4) | async-done | bytes 917536 | tf_op jit(solution)/shard_map/all_to_all | solution.py:36
  195.3 0.9 shard_map.164
  (40 shorter events, 1.7 us)
Async XLA Ops:
  7.2 37.0 %copy-start.8 = (f32[1,4,49,128]{3,1,2,0:T(4,128)S(1)}, f32[1,4,49,128]{3,1,2,0:T(4,128)}, u32[]{:S(2)}) copy-start(f32[1,4,49,128]{3,1,2,0:T(4,128)} %param.19) | copy-start | bytes 301060
  7.2 37.1 %copy-start.9 = (bf16[1,4,49,128]{3,1,2,0:T(4,128)(2,1)S(1)}, bf16[1,4,49,128]{3,1,2,0:T(4,128)(2,1)}, u32[]{:S(2)}) copy-start(bf16[1,4,49,128]{3,1,2,0:T(4,128)(2,1)} %param.13) | copy-start | bytes 150532
  7.2 81.2 %all-gather.4.cloned.1.call-start = ((), (), s32[]{:S(2)}) async-start(), calls=%async_computation.7 | async-start | bytes 3170304 | tf_op jit(solution)/shard_map/all_gather | solution.py:676
  44.3 49.1 %copy-start.10 = (s32[1,128]{1,0:T(1,128)S(1)}, s32[1,128]{1,0:T(1,128)}, u32[]{:S(2)}) copy-start(s32[1,128]{1,0:T(1,128)} %param.16) | copy-start | bytes 1540
  44.3 49.1 %copy-start.11 = (s32[1,128]{1,0:T(1,128)S(1)}, s32[1,128]{1,0:T(1,128)}, u32[]{:S(2)}) copy-start(s32[1,128]{1,0:T(1,128)} %param.17) | copy-start | bytes 1540
  44.3 49.1 %copy-start.5 = (bf16[1,29,49,128]{3,1,2,0:T(8,128)(2,1)S(1)}, bf16[1,29,49,128]{3,1,2,0:T(8,128)(2,1)}, u32[]{:S(2)}) copy-start(bf16[1,29,49,128]{3,1,2,0:T(8,128)(2,1)} %param.18) | copy-start | bytes 1091332
  44.7 53.1 %copy-start.7 = (bf16[128,8]{0,1:T(8,128)(2,1)S(1)}, bf16[128,8]{0,1:T(8,128)(2,1)}, u32[]{:S(2)}) copy-start(bf16[128,8]{0,1:T(8,128)(2,1)} %param.25) | copy-start | bytes 6148
  88.3 9.5 %collective-permute-start = (bf16[8,1376,128]{2,1,0:T(8,128)(2,1)}, bf16[8,1376,128]{2,1,0:T(8,128)(2,1)}, u32[]{:S(2)}, u32[]{:S(2)}) collective-permute-start(bf16[8,1376,128]{2,1,0:T(8,128)(2,1)} %bitcast.36), channel_id=1, source_target_pairs={{0,16},{16,0},{1,17},{17,1},{2,18},{18,2},{3,19},{19,3},{4,20},{20... | collective-permute-start | bytes 8454152 | tf_op jit(solution)/shard_map/ppermute | solution.py:718
  97.8 1.8 copy-start
  107.7 14.9 %all-to-all-start.2 = ((f32[16,8,128]{2,1,0:T(8,128)}), f32[16,8,128]{2,1,0:T(8,128)S(1)}, u32[]{:S(2)}, u32[]{:S(2)}) async-start(f32[16,8,128]{2,1,0:T(8,128)} %get-tuple-element.30), calls=%async_computation.2 | async-start | bytes 131072 | tf_op jit(solution)/shard_map/all_to_all | solution.py:36
  126.7 5.1 %collective-permute-start.1 = (bf16[16,32,896]{2,1,0:T(8,128)(2,1)S(1)}, bf16[16,32,896]{2,1,0:T(8,128)(2,1)S(1)}, u32[]{:S(2)}, u32[]{:S(2)}) collective-permute-start(bf16[16,32,896]{2,1,0:T(8,128)(2,1)S(1)} %get-tuple-element.35), channel_id=1, source_target_pairs={{0,16},{16,0},{1,17},{17,1},{2,18},{18,2},{3,19},{19,3},{4,20},{20... | collective-permute-start | bytes 2752520 | tf_op jit(solution)/shard_map/ppermute | solution.py:803
  132.9 31.7 %all-to-all-start.3 = ((bf16[16,32,896]{2,1,0:T(8,128)(2,1)}), bf16[16,32,896]{2,1,0:T(8,128)(2,1)}, u32[]{:S(2)}, u32[]{:S(2)}) async-start(bf16[16,32,896]{2,1,0:T(8,128)(2,1)} %add_convert_fusion), calls=%async_computation.4 | async-start | bytes 1835008 | tf_op jit(solution)/shard_map/all_to_all | solution.py:36
  141.3 4.0 %copy-start.1 = (bf16[11008,128]{1,0:T(8,128)(2,1)S(1)}, bf16[11008,128]{1,0:T(8,128)(2,1)}, u32[]{:S(2)}) copy-start(bf16[11008,128]{1,0:T(8,128)(2,1)} %all-gather.4.cloned.1.call-done) | copy-start | bytes 8454148
  141.3 37.5 %reduce-scatter.2.cloned.1.call-start = ((), (), s32[]{:S(2)}) async-start(), calls=%async_computation.6 | async-start | bytes 958464 | tf_op jit(solution)/shard_map/reduce_scatter | solution.py:817
  144.4 0.9 copy-start.6
  151.9 0.9 copy-start.2
  164.7 1.2 copy-start.3
  167.6 0.9 copy-start.4
  168.6 26.8 %all-to-all-start.4 = ((bf16[16,224,128]{2,1,0:T(8,128)(2,1)}), bf16[16,224,128]{2,1,0:T(8,128)(2,1)S(1)}, u32[]{:S(2)}, u32[]{:S(2)}) async-start(bf16[16,224,128]{2,1,0:T(8,128)(2,1)} %copy-done.4), calls=%async_computation.5 | async-start | bytes 1835008 | tf_op jit(solution)/shard_map/all_to_all | solution.py:36
  179.6 5.5 %collective-permute-start.2 = (bf16[208,128]{1,0:T(8,128)(2,1)S(1)}, bf16[208,128]{1,0:T(8,128)(2,1)S(1)}, u32[]{:S(2)}, u32[]{:S(2)}) collective-permute-start(bf16[208,128]{1,0:T(8,128)(2,1)S(1)} %get-tuple-element.44), channel_id=1, source_target_pairs={{0,1},{1,0},{2,3},{3,2},{4,5},{5,4},{6,7},{7,6},{8,9},{9,8},{10,11... | collective-permute-start | bytes 159752 | tf_op jit(solution)/shard_map/ppermute | solution.py:822
Sparse Core Ops, SparseCore 0:
  43.6 43.5 all-gather.3
  145.4 33.3 reduce-scatter.1

commit v6 on v5

--- a/solution.py
+++ b/solution.py
@@ -56,6 +56,7 @@
 MESSAGE_PART = (COEF, COEF)
 CONV_PART = (2 * COEF, REDUCED)
 ZERO_PART = (2 * COEF + REDUCED, LMAX + 1)
+SUM_START = 2 * COEF + REDUCED + LMAX + 1
 SPILL = 1200
 
 
@@ -143,7 +144,7 @@
             out[to : to + size, :] = blocks[at : at + size, :]
 
 
-def by_owner(target, turned, out, group, scale=None):
+def by_owner(target, turned, out, group, scale=None, split=False):
     channels = turned.shape[1]
     own = target.shape[0] // group
     per = 16 // own
@@ -157,7 +158,12 @@
                 part = jnp.zeros((target.shape[0], channels), f32)
             parts.append(part.reshape(group, 1, own, channels))
         block = jnp.concatenate(parts, axis=1).reshape(group, 16, channels)
-        out[:, first * own : first * own + 16, :] = block.astype(bf16)
+        at = first * own
+        if split:
+            half, at = at // LANES * group, at % LANES
+            out[half : half + group, at : at + 16, :] = block.astype(bf16)
+        else:
+            out[:, at : at + 16, :] = block.astype(bf16)
 
 
 def pack_kernel(places, *refs):
@@ -182,7 +188,35 @@
     group, most, lanes = slabs.shape[0] // 2, slabs.shape[1] // 2, slabs.shape[2]
     blocks = [jnp.concatenate([slabs[g], slabs[group + g]], axis=0) for g in range(group)]
 
+    def rolled(which):
+        wide = [block.astype(f32) for block in blocks]
+        lane = lax.broadcasted_iota(jnp.int32, wide[0].shape, 1)
+        to = 0
+        for rows, columns, at in which:
+            size = 4 * columns
+            row = lax.broadcasted_iota(jnp.int32, (size, 4 * most), 0)
+            column = lax.broadcasted_iota(jnp.int32, (size, 4 * most), 1)
+            chosen = (column == row // columns * most + row % columns).astype(bf16)
+            tiles = [None] * (group * rows // LANES)
+            for g in range(group):
+                t, off = divmod(g * rows, LANES)
+                shift = (off - at) % LANES
+                moved = pltpu.roll(wide[g], shift, 1) if shift else wide[g]
+                tiles[t] = moved if tiles[t] is None else jnp.where(lane >= off, moved, tiles[t])
+                if off + rows > LANES:
+                    tiles[t + 1] = moved
+            for t in range(0, len(tiles), 2):
+                pair = jnp.concatenate([tile.astype(bf16) for tile in tiles[t : t + 2]], axis=1)
+                pair = half_dot(chosen, pair).astype(bf16)
+                for i in range(len(tiles[t : t + 2])):
+                    out[to : to + size, :] = pair[:, i * LANES : (i + 1) * LANES]
+                    to += size
+        if to < out.shape[0]:
+            out[to:, :] = jnp.zeros((out.shape[0] - to, LANES), bf16)
+
     def lay(which):
+        if lanes == LANES:
+            return rolled(which)
         to = 0
         for rows, columns, at in which:
             size = 4 * columns
@@ -470,7 +504,7 @@
     wigner,
     mine,
     other,
-    grads_out,
+    spill_out,
     held,
     wide,
     dz,
@@ -537,9 +571,10 @@
 
     chunks(channels, body)
     both = (hot_rows(ids[1:2, :], count) + hot_rows(ids[0:1, :], count)).astype(bf16)
-    by_owner(both, gp, grads, group)
-    whole = pl.ds(0, grads.shape[1])
-    copy = pltpu.make_async_copy(grads, grads_out.at[:, whole, :], out_sem.at[0])
+    by_owner(both, gp, grads, group, split=True)
+    copy = pltpu.make_async_copy(
+        grads, part_of(spill_out, (SUM_START, grads.shape[0])), out_sem.at[0]
+    )
     copy.start()
     copy.wait()
 
@@ -554,15 +589,21 @@
     return ((column == row + shift) & (row >= low) & (row < high)).astype(bf16)
 
 
-def tail_kernel(used, share, heads, parts, grads_in, grads, total, att, window, sems):
+def tail_kernel(used, share, heads, parts, spill, grads, total, att, sems):
     count, depth = parts.shape[0], parts.shape[2]
-    group, rows = window.shape[0], window.shape[1]
+    group = grads.shape[0]
     inner, skip = depth // group, used % 16
-    base = used - skip
-    old = pltpu.make_async_copy(
-        grads_in.at[:, pl.ds(base, 16), :], window.at[:, pl.ds(0, 16), :], sems.at[0]
+    base, rows = used - skip, grads.shape[1] - (used - skip)
+    low_copy = pltpu.make_async_copy(
+        spill.at[pl.ds(SUM_START, group)], grads.at[:, pl.ds(0, LANES), :], sems.at[0]
     )
-    old.start()
+    high_copy = pltpu.make_async_copy(
+        spill.at[pl.ds(SUM_START + group, group), pl.ds(0, base + 16 - LANES), :],
+        grads.at[:, pl.ds(LANES, base + 16 - LANES), :],
+        sems.at[1],
+    )
+    low_copy.start()
+    high_copy.start()
     acc = parts[0].astype(f32)
     for p in range(1, count):
         acc = acc + parts[p].astype(f32)
@@ -581,20 +622,18 @@
     moved = half_dot(one_hot(rows, total.shape[0], -skip, skip, skip + share), acc.astype(bf16))
     moved = moved.astype(bf16)
     kept = lax.broadcasted_iota(jnp.int32, (rows, LANES), 0) < skip
-    old.wait()
+    low_copy.wait()
+    high_copy.wait()
     for g in range(group):
         first = g * inner // LANES * LANES
         last = -(-(g + 1) * inner // LANES) * LANES
         shift = g * inner - first
         place = one_hot(last - first, LANES, -shift, shift, shift + inner)
         piece = half_dot(moved[:, first:last], place) + tail
-        before = window[g, :16, :].astype(f32)
+        before = grads[g, base : base + 16, :].astype(f32)
         if rows > 16:
             before = jnp.concatenate([before, jnp.zeros((rows - 16, LANES), f32)], axis=0)
-        window[g] = jnp.where(kept, before, piece).astype(bf16)
-    new = pltpu.make_async_copy(window, grads.at[:, pl.ds(base, rows), :], sems.at[1])
-    new.start()
-    new.wait()
+        grads[g, base:, :] = jnp.where(kept, before, piece).astype(bf16)
 
 
 def last_kernel(scale, parts, nodes, zero, att, total):
@@ -801,9 +840,6 @@
     )(first, ids, stats, every, scalar, per_edge, rotation, spill, attention, attention_t)
 
     theirs = lax.ppermute(theirs, "core", [(0, 1), (1, 0)])
-    mine = (mine.astype(f32) + theirs.astype(f32)).astype(bf16)
-    mine, spill = lax.optimization_barrier((mine, spill))
-    zero_parts = exchange(mine, COLUMN_GROUP)
     message_sums = pl.pallas_call(
         message_kernel,
         out_shape=jax.ShapeDtypeStruct((group, span, channels), bf16),
@@ -812,7 +848,9 @@
         scratch_shapes=[edge_field, out_copy],
         compiler_params=LARGE,
     )(ids, stats, every, spill)
-    message_sums, spill = lax.optimization_barrier((message_sums, spill))
+    theirs, message_sums, spill = lax.optimization_barrier((theirs, message_sums, spill))
+    mine = (mine.astype(f32) + theirs.astype(f32)).astype(bf16)
+    zero_parts = exchange(mine, COLUMN_GROUP)
     message_sums = message_sums.reshape(group // 2, 2 * span, channels)
     near_sums = lax.psum_scatter(message_sums, "y", scatter_dimension=0, tiled=True)
     near_sums = near_sums.reshape(2, span, channels)
@@ -826,11 +864,9 @@
     lanes = whole_lanes(inner)
     beside = lanes - inner >= channels // 2 and lanes == channels and share >= 2 * head_count
     tail_rows = share if beside else share * lanes // LANES + head_count
-    grad_sums = pl.pallas_call(
+    spill = pl.pallas_call(
         functools.partial(scatter_kernel, places, group, row_count),
-        out_shape=jax.ShapeDtypeStruct(
-            (group, -(-(used + tail_rows) // 16) * 16, channels), bf16
-        ),
+        out_shape=spill_shape,
         in_specs=[smem, VMEM, HBM, VMEM] + [HBM] * 2,
         out_specs=HBM,
         scratch_shapes=[
@@ -840,31 +876,30 @@
             pltpu.VMEM((COEF,) + field, bf16),
             pltpu.VMEM((REDUCED * channels, edge_rows), f32),
             pltpu.VMEM((edge_rows, REDUCED * channels), bf16),
-            pltpu.VMEM((group, span, channels), bf16),
+            pltpu.VMEM((2 * group, channels, channels), bf16),
             pltpu.VMEM((REDUCED,) + field, bf16),
             copies,
             two_copies,
         ],
+        input_output_aliases={2: 0},
         compiler_params=LARGE,
     )(first, ids, spill, rotation, half, other)
+    sums_shape = (group, -(-(used + tail_rows) // 16) * 16, channels)
     nodes_shape = jax.ShapeDtypeStruct((harmonics, row_count, channels), bf16)
     batch_scale = 1.0 / (2 * columns)
     if beside:
-        window = -(-(used % 16 + share) // 16) * 16
         grad_sums = pl.pallas_call(
             functools.partial(tail_kernel, used, share, head_count),
-            out_shape=jax.ShapeDtypeStruct(grad_sums.shape, bf16),
+            out_shape=jax.ShapeDtypeStruct(sums_shape, bf16),
             in_specs=[VMEM, HBM],
-            out_specs=HBM,
-            input_output_aliases={1: 0},
+            out_specs=VMEM,
             scratch_shapes=[
                 pltpu.VMEM((padded, depth), f32),
                 pltpu.VMEM((head_count, channels), f32),
-                pltpu.VMEM((group, window, channels), bf16),
                 two_copies,
             ],
             compiler_params=SMALL,
-        )(zero_parts, grad_sums)
+        )(zero_parts, spill)
         last = exchange(grad_sums, GRAPH)
         grad_nodes, grad_zero, grad_att = pl.pallas_call(
             functools.partial(last_kernel, batch_scale),
@@ -889,6 +924,10 @@
             att.reshape(1, head_count, channels), (group, head_count, channels)
         )
         last_rows = jnp.concatenate([zero_send, att], axis=1).astype(bf16)
+        grad_sums = spill[SUM_START : SUM_START + 2 * group].reshape(2, group, channels, channels)
+        grad_sums = jnp.transpose(grad_sums, (1, 0, 2, 3)).reshape(group, 2 * channels, channels)
+        rest = jnp.zeros(sums_shape, bf16)
+        grad_sums = lax.dynamic_update_slice(rest, grad_sums[:, :used], (0, 0, 0))
         grad_sums = lax.dynamic_update_slice(grad_sums, last_rows, (0, used, 0))
         last = exchange(grad_sums, GRAPH)
         grad_nodes, tail = pl.pallas_call(

time: 206 us -> 206 us (level)
    pallas_call x1, Pallas kernels: 4.07 us -> 1.38 us  [gather_weights(): pl.pallas_call(functools.partial(slab_kernel, kinds), out_shape=jax.Shape...]
    all_to_all x3, waiting for transfers between devices: 29.3 us -> 31.6 us  [exchange(): return lax.all_to_all(blocks, axes, split_axis=0, concat_axis=0, tiled=True)]
    ppermute x1, waiting for transfers between devices: 2.08 us -> 0.01 us  [on_device(): theirs = lax.ppermute(theirs, 'core', [(0, 1), (1, 0)])]
  transfers between devices with their start and end apart: 8 -> 8, of which waited for: 7 -> 6; matrix products, arithmetic and copies ran while one was open for 1% -> 1% of each run, Pallas kernels for 7% -> 9%
where the time goes in v6:
time: 206 us; the launch traced here: 203 us
  blocking collectives  72.3 us (35%)
  waiting for transfers between devices  41.8 us (20%)
  Pallas kernels  33.8 us (16%)
  starting transfers between devices  28.6 us (14%)
  between operations  15.7 us (8%)
  local copies, waits for them, and re-layouts  8.93 us (4%)
    all_to_all x2, blocking collectives, gather(): return lax.all_to_all(copies, axes, split_axis=0, concat_axis=0, tiled=True)  63.7 us
    all_to_all x3, waiting for transfers between devices, exchange(): return lax.all_to_all(blocks, axes, split_axis=0, concat_axis=0, tiled=True)  31.6 us
    all_to_all x3, starting transfers between devices, exchange(): return lax.all_to_all(blocks, axes, split_axis=0, concat_axis=0, tiled=True)  18 us
    all_gather x1, blocking collectives, gather_weights(): near = lax.all_gather(packed, 'core')  8.58 us
    pallas_call x1, Pallas kernels, on_device(): pl.pallas_call(functools.partial(forward_kernel, places, group), out_shap...  8.06 us
    unnamed x25, local copies, waits for them, and re-layouts  7.65 us
    pallas_call x1, Pallas kernels, on_device(): pl.pallas_call(functools.partial(scatter_kernel, places, group, row_count...  7.42 us
    reduce_scatter x1, waiting for transfers between devices, on_device(): lax.psum_scatter(message_sums, 'y', scatter_dimension=0, tiled=True)  6.12 us
  transfers between devices with their start and end apart: 8, of which 6 were waited for; matrix products, arithmetic and copies ran while one was open for 1% of the time, Pallas kernels for 9%

profile of v6, /device:TPU:1, one launch (start us, length us, event | category | flops | bytes accessed | tf_op | source)
XLA Modules:
  0.0 203.2 jit_solution(6567814537851059965)
XLA Ops:
  7.2 2.0 shard_map.156
  9.2 8.6 %all-gather = bf16[64,256]{1,0:T(8,128)(2,1)S(1)} all-gather(bf16[32,256]{1,0:T(8,128)(2,1)} %shard_map.156), channel_id=2, replica_groups=mesh['xh'=2,'z'=8,'core'=2,'y'=8,'xl'=2] {'core'}, dimensions={0}, use_global_device_ids=true | all-gather | bytes 49152 | tf_op jit(solution)/shard_map/all_gather | solution.py:694
  17.9 21.5 %all_to_all.25.slabs = bf16[32,64,128]{2,1,0:T(8,128)(2,1)S(1)} all-to-all(bf16[32,64,128]{2,1,0:T(8,128)(2,1)S(1)} %broadcast_in_dim.39), channel_id=1, replica_groups=mesh['xh'=2,'z'=8,'core'=2,'y'=8,'xl'=2] {'xh','y','xl'}, dimensions={0} | all-to-all | bytes 1048576 | tf_op jit(solution)/shard_map/all_to_all | solution.py:32
  39.4 1.4 shard_map.157
  42.0 42.2 %all_to_all.26.nodes = bf16[16,400,128]{2,1,0:T(8,128)(2,1)} all-to-all(bf16[16,400,128]{2,1,0:T(8,128)(2,1)S(1)} %broadcast_in_dim.42), channel_id=1, replica_groups=mesh['xh'=2,'z'=8,'core'=2,'y'=8,'xl'=2] {'y','xl'}, dimensions={0} | all-to-all | bytes 3276800 | tf_op jit(solution)/shard_map/all_to_all | solution.py:32
  84.2 1.1 all-gather.4.cloned.1.call-done
  85.3 5.0 %collective-permute-start = (bf16[8,1376,128]{2,1,0:T(8,128)(2,1)}, bf16[8,1376,128]{2,1,0:T(8,128)(2,1)S(1)}, u32[]{:S(2)}, u32[]{:S(2)}) collective-permute-start(bf16[8,1376,128]{2,1,0:T(8,128)(2,1)} %bitcast.36), channel_id=1, source_target_pairs={{0,16},{16,0},{1,17},{17,1},{2,18},{18,2},{3,19},{19,3},{4,20},{20... | collective-permute-start | bytes 8454152 | tf_op jit(solution)/shard_map/ppermute | solution.py:757
  91.0 1.4 copy-done.4
  92.4 3.8 %shard_map.158 = (bf16[29,128,128]{2,1,0:T(8,128)(2,1)S(1)}, bf16[1200,128,128]{2,1,0:T(8,128)(2,1)}) custom-call(s32[8,128]{1,0:T(8,128)S(1)} %stack.12.ids, bf16[16,400,128]{2,1,0:T(8,128)(2,1)S(1)} %copy-done.4, bf16[49,29,128]{2,1,0:T(8,128)(2,1)S(1)} %bitcast.39), custom_call_target="tpu_custom_call" | custom-call | tf_op jit(solution)/shard_map/pallas_call | solution.py:766
  96.2 1.6 copy-done.2
  97.8 1.8 copy-done
  99.6 8.1 %shard_map.159 = (bf16[1200,128,128]{2,1,0:T(8,128)(2,1)}, f32[8,128]{1,0:T(8,128)S(1)}, f32[16,8,128]{2,1,0:T(8,128)}, f32[128,128]{1,0:T(8,128)S(1)}, f32[16,128]{1,0:T(8,128)S(1)}) custom-call(s32[1,1]{1,0:T(1,128)} %bitcast.1.first, s32[8,128]{1,0:T(8,128)S(1)} %stack.12.ids, ...), custom_call_target="tpu_custom_call", output_to_operand_aliasing={{0}: (4, {})} | custom-call | tf_op jit(solution)/shard_map/pallas_call | solution.py:787
  107.7 7.1 %all-to-all-start.2 = ((f32[16,8,128]{2,1,0:T(8,128)}), f32[16,8,128]{2,1,0:T(8,128)S(1)}, u32[]{:S(2)}, u32[]{:S(2)}) async-start(f32[16,8,128]{2,1,0:T(8,128)} %get-tuple-element.29), calls=%async_computation.2 | async-start | bytes 131072 | tf_op jit(solution)/shard_map/all_to_all | solution.py:36
  114.9 8.5 %all-to-all-done.2.every = f32[16,8,128]{2,1,0:T(8,128)S(1)} async-done(((f32[16,8,128]{2,1,0:T(8,128)}), f32[16,8,128]{2,1,0:T(8,128)S(1)}, u32[]{:S(2)}, u32[]{:S(2)}) %all-to-all-start.2) | async-done | bytes 65568 | tf_op jit(solution)/shard_map/all_to_all | solution.py:36
  123.4 4.1 %shard_map.160 = (bf16[1200,128,128]{2,1,0:T(8,128)(2,1)}, bf16[16,32,896]{2,1,0:T(8,128)(2,1)S(1)}, bf16[16,32,896]{2,1,0:T(8,128)(2,1)S(1)}) custom-call(s32[1,1]{1,0:T(1,128)} %bitcast.1.first, s32[8,128]{1,0:T(8,128)S(1)} %stack.12.ids, f32[8,128]{1,0:T(8,128)S(1)} %get-tuple-element.28.stats, ...), custom_call_target="tpu_custom_call", output_to_operand_aliasing={{0}: (7, {})} | custom-call | tf_op jit(solution)/shard_map/pallas_call | solution.py:819
  127.5 2.3 %collective-permute-start.1 = (bf16[16,32,896]{2,1,0:T(8,128)(2,1)S(1)}, bf16[16,32,896]{2,1,0:T(8,128)(2,1)S(1)}, u32[]{:S(2)}, u32[]{:S(2)}) collective-permute-start(bf16[16,32,896]{2,1,0:T(8,128)(2,1)S(1)} %get-tuple-element.33), channel_id=1, source_target_pairs={{0,16},{16,0},{1,17},{17,1},{2,18},{18,2},{3,19},{19,3},{4,20},{20... | collective-permute-start | bytes 2752520 | tf_op jit(solution)/shard_map/ppermute | solution.py:842
  129.9 2.7 %shard_map.161 = bf16[16,208,128]{2,1,0:T(8,128)(2,1)S(1)} custom-call(s32[8,128]{1,0:T(8,128)S(1)} %stack.12.ids, f32[8,128]{1,0:T(8,128)S(1)} %get-tuple-element.28.stats, f32[16,8,128]{2,1,0:T(8,128)S(1)} %all-to-all-done.2.every, bf16[1200,128,128]{2,1,0:T(8,128)(2,1)} %get-tuple-element.38.spill), custom_call_target="tpu_custom_call" | custom-call | tf_op jit(solution)/shard_map/pallas_call | solution.py:843
  132.5 0.9 copy-done.6
  133.5 1.1 add_convert_fusion
  134.6 7.3 %all-to-all-start.3 = ((bf16[16,32,896]{2,1,0:T(8,128)(2,1)}), bf16[16,32,896]{2,1,0:T(8,128)(2,1)}, u32[]{:S(2)}, u32[]{:S(2)}) async-start(bf16[16,32,896]{2,1,0:T(8,128)(2,1)} %add_convert_fusion), calls=%async_computation.4 | async-start | bytes 1835008 | tf_op jit(solution)/shard_map/all_to_all | solution.py:36
  142.7 1.8 copy-done.3
  144.5 7.4 %shard_map.162.spill = bf16[1200,128,128]{2,1,0:T(8,128)(2,1)} custom-call(s32[1,1]{1,0:T(1,128)} %bitcast.1.first, s32[8,128]{1,0:T(8,128)S(1)} %stack.12.ids, bf16[1200,128,128]{2,1,0:T(8,128)(2,1)} %get-tuple-element.38.spill, bf16[49,29,128]{2,1,0:T(8,128)(2,1)S(1)} %bitcast.42, ...), custom_call_target="tpu_custom_call", output_to_operand_aliasing={{}: (2, {})} | custom-call | tf_op jit(solution)/shard_map/pallas_call | solution.py:867
  151.9 13.4 %all-to-all-done.3.parts = bf16[16,32,896]{2,1,0:T(8,128)(2,1)} async-done(((bf16[16,32,896]{2,1,0:T(8,128)(2,1)}), bf16[16,32,896]{2,1,0:T(8,128)(2,1)}, u32[]{:S(2)}, u32[]{:S(2)}) %all-to-all-start.3) | async-done | bytes 917536 | tf_op jit(solution)/shard_map/all_to_all | solution.py:36
  165.2 3.5 %shard_map.163 = bf16[16,224,128]{2,1,0:T(8,128)(2,1)} custom-call(bf16[16,32,896]{2,1,0:T(8,128)(2,1)} %all-to-all-done.3.parts, bf16[1200,128,128]{2,1,0:T(8,128)(2,1)} %shard_map.162.spill), custom_call_target="tpu_custom_call" | custom-call | tf_op jit(solution)/shard_map/pallas_call | solution.py:891
  168.8 3.6 %all-to-all-start.4 = ((bf16[16,224,128]{2,1,0:T(8,128)(2,1)}), bf16[16,224,128]{2,1,0:T(8,128)(2,1)S(1)}, u32[]{:S(2)}, u32[]{:S(2)}) async-start(bf16[16,224,128]{2,1,0:T(8,128)(2,1)} %shard_map.163), calls=%async_computation.5 | async-start | bytes 1835008 | tf_op jit(solution)/shard_map/all_to_all | solution.py:36
  172.5 6.1 %reduce-scatter.2.cloned.1.call-done = bf16[1,416,128]{2,1,0:T(8,128)(2,1)} async-done(((bf16[8,416,128]{2,1,0:T(8,128)(2,1)}), bf16[1,416,128]{2,1,0:T(8,128)(2,1)}) %reduce-scatter.2.cloned.1.call-update) | async-done | bytes 106512 | tf_op jit(solution)/shard_map/reduce_scatter | solution.py:855
  178.6 0.8 dynamic-slice_bitcast_fusion
  179.4 3.2 %collective-permute-start.2 = (bf16[208,128]{1,0:T(8,128)(2,1)S(1)}, bf16[208,128]{1,0:T(8,128)(2,1)S(1)}, u32[]{:S(2)}, u32[]{:S(2)}) collective-permute-start(bf16[208,128]{1,0:T(8,128)(2,1)S(1)} %get-tuple-element.42), channel_id=1, source_target_pairs={{0,1},{1,0},{2,3},{3,2},{4,5},{5,4},{6,7},{7,6},{8,9},{9,8},{10,11... | collective-permute-start | bytes 159752 | tf_op jit(solution)/shard_map/ppermute | solution.py:860
  182.6 2.3 %collective-permute-done.2 = bf16[208,128]{1,0:T(8,128)(2,1)S(1)} collective-permute-done((bf16[208,128]{1,0:T(8,128)(2,1)S(1)}, bf16[208,128]{1,0:T(8,128)(2,1)S(1)}, u32[]{:S(2)}, u32[]{:S(2)}) %collective-permute-start.2) | collective-permute-done | bytes 53280 | tf_op jit(solution)/shard_map/ppermute | solution.py:860
  185.0 0.7 fusion
  185.7 9.7 %all-to-all-done.4.parts = bf16[16,224,128]{2,1,0:T(8,128)(2,1)S(1)} async-done(((bf16[16,224,128]{2,1,0:T(8,128)(2,1)}), bf16[16,224,128]{2,1,0:T(8,128)(2,1)S(1)}, u32[]{:S(2)}, u32[]{:S(2)}) %all-to-all-start.4) | async-done | bytes 917536 | tf_op jit(solution)/shard_map/all_to_all | solution.py:36
  195.4 0.9 shard_map.164
  (40 shorter events, 1.6 us)
Async XLA Ops:
  7.2 34.3 %copy-start.8 = (f32[1,4,49,128]{3,1,2,0:T(4,128)S(1)}, f32[1,4,49,128]{3,1,2,0:T(4,128)}, u32[]{:S(2)}) copy-start(f32[1,4,49,128]{3,1,2,0:T(4,128)} %param.19) | copy-start | bytes 301060
  7.2 34.4 %copy-start.9 = (bf16[1,4,49,128]{3,1,2,0:T(4,128)(2,1)S(1)}, bf16[1,4,49,128]{3,1,2,0:T(4,128)(2,1)}, u32[]{:S(2)}) copy-start(bf16[1,4,49,128]{3,1,2,0:T(4,128)(2,1)} %param.13) | copy-start | bytes 150532
  7.2 78.1 %all-gather.4.cloned.1.call-start = ((), (), s32[]{:S(2)}) async-start(), calls=%async_computation.7 | async-start | bytes 3170304 | tf_op jit(solution)/shard_map/all_gather | solution.py:715
  41.6 49.4 %copy-start.10 = (s32[1,128]{1,0:T(1,128)S(1)}, s32[1,128]{1,0:T(1,128)}, u32[]{:S(2)}) copy-start(s32[1,128]{1,0:T(1,128)} %param.16) | copy-start | bytes 1540
  41.6 49.4 %copy-start.11 = (s32[1,128]{1,0:T(1,128)S(1)}, s32[1,128]{1,0:T(1,128)}, u32[]{:S(2)}) copy-start(s32[1,128]{1,0:T(1,128)} %param.17) | copy-start | bytes 1540
  41.6 49.4 %copy-start.5 = (bf16[1,29,49,128]{3,1,2,0:T(8,128)(2,1)S(1)}, bf16[1,29,49,128]{3,1,2,0:T(8,128)(2,1)}, u32[]{:S(2)}) copy-start(bf16[1,29,49,128]{3,1,2,0:T(8,128)(2,1)} %param.18) | copy-start | bytes 1091332
  42.0 55.8 %copy-start.7 = (bf16[128,8]{0,1:T(8,128)(2,1)S(1)}, bf16[128,8]{0,1:T(8,128)(2,1)}, u32[]{:S(2)}) copy-start(bf16[128,8]{0,1:T(8,128)(2,1)} %param.25) | copy-start | bytes 6148
  85.3 10.9 %collective-permute-start = (bf16[8,1376,128]{2,1,0:T(8,128)(2,1)}, bf16[8,1376,128]{2,1,0:T(8,128)(2,1)S(1)}, u32[]{:S(2)}, u32[]{:S(2)}) collective-permute-start(bf16[8,1376,128]{2,1,0:T(8,128)(2,1)} %bitcast.36), channel_id=1, source_target_pairs={{0,16},{16,0},{1,17},{17,1},{2,18},{18,2},{3,19},{19,3},{4,20},{20... | collective-permute-start | bytes 8454152 | tf_op jit(solution)/shard_map/ppermute | solution.py:757
  91.0 1.4 copy-start.4
  96.2 1.6 copy-start.2
  97.8 1.8 copy-start
  107.7 15.8 %all-to-all-start.2 = ((f32[16,8,128]{2,1,0:T(8,128)}), f32[16,8,128]{2,1,0:T(8,128)S(1)}, u32[]{:S(2)}, u32[]{:S(2)}) async-start(f32[16,8,128]{2,1,0:T(8,128)} %get-tuple-element.29), calls=%async_computation.2 | async-start | bytes 131072 | tf_op jit(solution)/shard_map/all_to_all | solution.py:36
  127.5 5.9 %collective-permute-start.1 = (bf16[16,32,896]{2,1,0:T(8,128)(2,1)S(1)}, bf16[16,32,896]{2,1,0:T(8,128)(2,1)S(1)}, u32[]{:S(2)}, u32[]{:S(2)}) collective-permute-start(bf16[16,32,896]{2,1,0:T(8,128)(2,1)S(1)} %get-tuple-element.33), channel_id=1, source_target_pairs={{0,16},{16,0},{1,17},{17,1},{2,18},{18,2},{3,19},{19,3},{4,20},{20... | collective-permute-start | bytes 2752520 | tf_op jit(solution)/shard_map/ppermute | solution.py:842
  132.5 0.9 copy-start.6
  133.5 9.2 %copy-start.1 = (bf16[11008,128]{1,0:T(8,128)(2,1)S(1)}, bf16[11008,128]{1,0:T(8,128)(2,1)}, u32[]{:S(2)}) copy-start(bf16[11008,128]{1,0:T(8,128)(2,1)} %all-gather.4.cloned.1.call-done) | copy-start | bytes 8454148
  134.6 30.7 %all-to-all-start.3 = ((bf16[16,32,896]{2,1,0:T(8,128)(2,1)}), bf16[16,32,896]{2,1,0:T(8,128)(2,1)}, u32[]{:S(2)}, u32[]{:S(2)}) async-start(bf16[16,32,896]{2,1,0:T(8,128)(2,1)} %add_convert_fusion), calls=%async_computation.4 | async-start | bytes 1835008 | tf_op jit(solution)/shard_map/all_to_all | solution.py:36
  141.9 36.7 %reduce-scatter.2.cloned.1.call-start = ((), (), s32[]{:S(2)}) async-start(), calls=%async_computation.6 | async-start | bytes 958464 | tf_op jit(solution)/shard_map/reduce_scatter | solution.py:855
  142.7 1.8 copy-start.3
  168.8 26.7 %all-to-all-start.4 = ((bf16[16,224,128]{2,1,0:T(8,128)(2,1)}), bf16[16,224,128]{2,1,0:T(8,128)(2,1)S(1)}, u32[]{:S(2)}, u32[]{:S(2)}) async-start(bf16[16,224,128]{2,1,0:T(8,128)(2,1)} %shard_map.163), calls=%async_computation.5 | async-start | bytes 1835008 | tf_op jit(solution)/shard_map/all_to_all | solution.py:36
  179.4 5.6 %collective-permute-start.2 = (bf16[208,128]{1,0:T(8,128)(2,1)S(1)}, bf16[208,128]{1,0:T(8,128)(2,1)S(1)}, u32[]{:S(2)}, u32[]{:S(2)}) collective-permute-start(bf16[208,128]{1,0:T(8,128)(2,1)S(1)} %get-tuple-element.42), channel_id=1, source_target_pairs={{0,1},{1,0},{2,3},{3,2},{4,5},{5,4},{6,7},{7,6},{8,9},{9,8},{10,11... | collective-permute-start | bytes 159752 | tf_op jit(solution)/shard_map/ppermute | solution.py:860
Sparse Core Ops, SparseCore 0:
  40.9 44.3 all-gather.3
  145.6 32.9 reduce-scatter.1

commit v7 on v6

--- a/solution.py
+++ b/solution.py
@@ -57,7 +57,8 @@
 CONV_PART = (2 * COEF, REDUCED)
 ZERO_PART = (2 * COEF + REDUCED, LMAX + 1)
 SUM_START = 2 * COEF + REDUCED + LMAX + 1
-SPILL = 1200
+SPILL = 600
+MAP_SLOTS = 7
 
 
 def nt_dot(left, right):
@@ -104,6 +105,9 @@
             pltpu.make_async_copy(
                 halves[half].at[:, span, :], held.at[half, :, span, :], sems.at[i]
             ).start()
+
+    if first is None:
+        return go((mine, other))
 
     @pl.when(first == 0)
     def _():
@@ -262,11 +266,15 @@
     by_owner(hot_rows(ids[1:2, :], count).astype(bf16), msg, out, group, scale)
 
 
-def rotate_kernel(own, ids, nodes, wigner, z, spill, paired, wide, grad_edge, out_sem):
+def rotate_kernel(
+    own, ids, nodes, wigner, half, z, spill, maps, paired, wide, grad_edge, out_sem
+):
     group, edges = nodes.shape[0], wigner.shape[2]
     channels = LANES
     per = 16 // (2 * own)
     count = own * group
+    half_copy = pltpu.make_async_copy(half, maps.at[2], out_sem.at[2])
+    half_copy.start()
     target = hot_rows(ids[1:2, :], count)
     both = (target + hot_rows(ids[0:1, :], count)).astype(bf16)
     target = target.astype(bf16)
@@ -295,6 +303,7 @@
     zero_copy.start()
     copy.wait()
     zero_copy.wait()
+    half_copy.wait()
 
 
 def forward_kernel(
@@ -306,9 +315,10 @@
     wigner,
     spill_in,
     attention_t,
-    mine,
+    maps_in,
     other,
     spill,
+    maps,
     stats,
     sent,
     scalar,
@@ -326,6 +336,7 @@
     channels, edges = LANES, wigner.shape[2]
     heads = attention_t.shape[0]
     count = stats.shape[1] // 2
+    mine = maps_in.at[2]
     start_weights(places, first[0, 0], mine, other, held, sems)
     edge_copy = pltpu.make_async_copy(part_of(spill_in, EDGE_PART), grad_edge, out_sem.at[1])
     edge_copy.start()
@@ -352,6 +363,8 @@
             acc = term if acc is None else acc + term
         spread(acc[:, :edges], held, real[2], base * channels, y)
         spread(acc[:, edges:], held, real[2], (base + rows) * channels, y)
+    maps_copy = pltpu.make_async_copy(held, maps.at[pl.ds(0, 2)], out_sem.at[2])
+    maps_copy.start()
     value = y[:channels, :]
     scalar[...] = value
     y[...] = y[...].astype(bf16).astype(f32)
@@ -391,6 +404,7 @@
     per_edge[:heads, :] = own_norm
     per_edge[heads:, :] = grad_norm
     copy.wait()
+    maps_copy.wait()
 
 
 def backward_kernel(
@@ -498,12 +512,10 @@
     places,
     group,
     own,
-    first,
     ids,
     spill,
     wigner,
-    mine,
-    other,
+    maps,
     spill_out,
     held,
     wide,
@@ -520,7 +532,8 @@
     count = own * group
     conv_copy = pltpu.make_async_copy(part_of(spill, CONV_PART), grad_conv, out_sem.at[1])
     conv_copy.start()
-    start_weights(places, first[0, 0], mine, other, held, sems)
+    mine = maps.at[0]
+    start_weights(places, None, mine, maps.at[1], held, sems)
     wide[...] = wigner[...].astype(f32)
     conv_copy.wait()
     grad[...] = grad_conv[...].astype(f32).reshape(grad.shape)
@@ -759,42 +772,45 @@
     smem = pl.BlockSpec(memory_space=pltpu.SMEM)
     field = (channels, edge_rows)
     wide = pltpu.VMEM(rotation.shape, f32)
+    maps_shape = jax.ShapeDtypeStruct((MAP_SLOTS,) + half.shape, bf16)
     spill_shape = jax.ShapeDtypeStruct((SPILL,) + field, bf16)
     out_copy = pltpu.SemaphoreType.DMA((1,))
     two_copies = pltpu.SemaphoreType.DMA((2,))
     edge_field = pltpu.VMEM((COEF,) + field, bf16)
-    z, spill = pl.pallas_call(
+    z, spill, maps = pl.pallas_call(
         functools.partial(rotate_kernel, row_count),
         out_shape=(
             jax.ShapeDtypeStruct((REDUCED,) + field, bf16),
             spill_shape,
+            maps_shape,
         ),
-        in_specs=[VMEM] * 3,
-        out_specs=[VMEM, HBM],
+        in_specs=[VMEM] * 3 + [HBM],
+        out_specs=[VMEM, HBM, HBM],
         scratch_shapes=[
             pltpu.VMEM((COEF,) + field, f32),
             wide,
             edge_field,
-            two_copies,
+            pltpu.SemaphoreType.DMA((3,)),
         ],
         compiler_params=LARGE,
-    )(ids, nodes, rotation)
+    )(ids, nodes, rotation, half)
     held = pltpu.VMEM((2,) + half.shape, bf16)
     copies = pltpu.SemaphoreType.DMA((len(places),))
 
     span = node_rows(row_count)
     sums = (head_count, 2 * all_nodes)
-    spill, stats, sent, scalar, per_edge = pl.pallas_call(
+    spill, maps, stats, sent, scalar, per_edge = pl.pallas_call(
         functools.partial(forward_kernel, places, group),
         out_shape=(
             spill_shape,
+            maps_shape,
             jax.ShapeDtypeStruct(sums, f32),
             jax.ShapeDtypeStruct((group,) + sums, f32),
             jax.ShapeDtypeStruct(field, f32),
             jax.ShapeDtypeStruct((2 * head_count, edge_rows), f32),
         ),
         in_specs=[smem] + [VMEM] * 3 + [HBM, VMEM] + [HBM] * 2,
-        out_specs=[HBM] + [VMEM] * 4,
+        out_specs=[HBM] * 2 + [VMEM] * 4,
         scratch_shapes=[
             held,
             pltpu.VMEM((REDUCED * channels, edge_rows), f32),
@@ -804,11 +820,11 @@
             pltpu.VMEM(field, f32),
             edge_field,
             copies,
-            two_copies,
+            pltpu.SemaphoreType.DMA((3,)),
         ],
-        input_output_aliases={4: 0},
+        input_output_aliases={4: 0, 6: 1},
         compiler_params=LARGE,
-    )(first, ids, z, rotation, spill, attention_t, half, other)
+    )(first, ids, z, rotation, spill, attention_t, maps, other)
     every = exchange(sent, GRAPH)
 
     columns = lax.axis_size(COLUMN_GROUP)
@@ -840,6 +856,9 @@
     )(first, ids, stats, every, scalar, per_edge, rotation, spill, attention, attention_t)
 
     theirs = lax.ppermute(theirs, "core", [(0, 1), (1, 0)])
+    mine = (mine.astype(f32) + theirs.astype(f32)).astype(bf16)
+    mine, spill = lax.optimization_barrier((mine, spill))
+    zero_parts = exchange(mine, COLUMN_GROUP)
     message_sums = pl.pallas_call(
         message_kernel,
         out_shape=jax.ShapeDtypeStruct((group, span, channels), bf16),
@@ -848,9 +867,7 @@
         scratch_shapes=[edge_field, out_copy],
         compiler_params=LARGE,
     )(ids, stats, every, spill)
-    theirs, message_sums, spill = lax.optimization_barrier((theirs, message_sums, spill))
-    mine = (mine.astype(f32) + theirs.astype(f32)).astype(bf16)
-    zero_parts = exchange(mine, COLUMN_GROUP)
+    message_sums, spill = lax.optimization_barrier((message_sums, spill))
     message_sums = message_sums.reshape(group // 2, 2 * span, channels)
     near_sums = lax.psum_scatter(message_sums, "y", scatter_dimension=0, tiled=True)
     near_sums = near_sums.reshape(2, span, channels)
@@ -867,7 +884,7 @@
     spill = pl.pallas_call(
         functools.partial(scatter_kernel, places, group, row_count),
         out_shape=spill_shape,
-        in_specs=[smem, VMEM, HBM, VMEM] + [HBM] * 2,
+        in_specs=[VMEM, HBM, VMEM, HBM],
         out_specs=HBM,
         scratch_shapes=[
             held,
@@ -881,9 +898,9 @@
             copies,
             two_copies,
         ],
-        input_output_aliases={2: 0},
+        input_output_aliases={1: 0},
         compiler_params=LARGE,
-    )(first, ids, spill, rotation, half, other)
+    )(ids, spill, rotation, maps)
     sums_shape = (group, -(-(used + tail_rows) // 16) * 16, channels)
     nodes_shape = jax.ShapeDtypeStruct((harmonics, row_count, channels), bf16)
     batch_scale = 1.0 / (2 * columns)
@@ -898,7 +915,7 @@
                 pltpu.VMEM((head_count, channels), f32),
                 two_copies,
             ],
-            compiler_params=SMALL,
+            compiler_params=LARGE,
         )(zero_parts, spill)
         last = exchange(grad_sums, GRAPH)
         grad_nodes, grad_zero, grad_att = pl.pallas_call(

time: 206 us -> 202 us (0.981)
  local copies, waits for them, and re-layouts: 8.93 us -> 3.22 us
    all_to_all x3, waiting for transfers between devices: 31.6 us -> 25.5 us  [exchange(): return lax.all_to_all(blocks, axes, split_axis=0, concat_axis=0, tiled=True)]
    unnamed x25 -> x15, local copies, waits for them, and re-layouts: 7.65 us -> 1.94 us
    reduce_scatter x1, waiting for transfers between devices: 6.12 us -> 8.73 us  [on_device(): lax.psum_scatter(message_sums, 'y', scatter_dimension=0, tiled=True)]
    ppermute x1, waiting for transfers between devices: 0.01 us -> 2.08 us  [on_device(): theirs = lax.ppermute(theirs, 'core', [(0, 1), (1, 0)])]
  transfers between devices with their start and end apart: 8 -> 8, of which waited for: 6 -> 7; matrix products, arithmetic and copies ran while one was open for 1% -> 1% of each run, Pallas kernels for 9% -> 9%
where the time goes in v7:
time: 202 us; the launch traced here: 198 us
  blocking collectives  72.2 us (36%)
  waiting for transfers between devices  40.5 us (20%)
  Pallas kernels  35.1 us (17%)
  starting transfers between devices  29.6 us (15%)
  between operations  15.6 us (8%)
  local copies, waits for them, and re-layouts  3.22 us (2%)
  other arithmetic  2.09 us (1%)
    all_to_all x2, blocking collectives, gather(): return lax.all_to_all(copies, axes, split_axis=0, concat_axis=0, tiled=True)  63.6 us
    all_to_all x3, waiting for transfers between devices, exchange(): return lax.all_to_all(blocks, axes, split_axis=0, concat_axis=0, tiled=True)  25.5 us
    all_to_all x3, starting transfers between devices, exchange(): return lax.all_to_all(blocks, axes, split_axis=0, concat_axis=0, tiled=True)  18.7 us
    pallas_call x1, Pallas kernels, on_device(): pl.pallas_call(functools.partial(scatter_kernel, places, group, row_count...  8.89 us
    reduce_scatter x1, waiting for transfers between devices, on_device(): lax.psum_scatter(message_sums, 'y', scatter_dimension=0, tiled=True)  8.73 us
    all_gather x1, blocking collectives, gather_weights(): near = lax.all_gather(packed, 'core')  8.58 us
    pallas_call x1, Pallas kernels, on_device(): pl.pallas_call(functools.partial(forward_kernel, places, group), out_shap...  8.14 us
    ppermute x1, starting transfers between devices, on_device(): other = lax.ppermute(half, 'core', [(0, 1), (1, 0)])  4.8 us
  transfers between devices with their start and end apart: 8, of which 7 were waited for; matrix products, arithmetic and copies ran while one was open for 1% of the time, Pallas kernels for 9%

profile of v7, /device:TPU:1, one launch (start us, length us, event | category | flops | bytes accessed | tf_op | source)
XLA Modules:
  0.0 198.4 jit_solution(8609996318209951442)
XLA Ops:
  7.2 2.0 shard_map.156
  9.2 8.6 %all-gather = bf16[64,256]{1,0:T(8,128)(2,1)S(1)} all-gather(bf16[32,256]{1,0:T(8,128)(2,1)} %shard_map.156), channel_id=2, replica_groups=mesh['xh'=2,'z'=8,'core'=2,'y'=8,'xl'=2] {'core'}, dimensions={0}, use_global_device_ids=true | all-gather | bytes 49152 | tf_op jit(solution)/shard_map/all_gather | solution.py:707
  17.9 21.5 %all_to_all.25.slabs = bf16[32,64,128]{2,1,0:T(8,128)(2,1)S(1)} all-to-all(bf16[32,64,128]{2,1,0:T(8,128)(2,1)S(1)} %broadcast_in_dim.39), channel_id=1, replica_groups=mesh['xh'=2,'z'=8,'core'=2,'y'=8,'xl'=2] {'xh','y','xl'}, dimensions={0} | all-to-all | bytes 1048576 | tf_op jit(solution)/shard_map/all_to_all | solution.py:32
  39.4 1.4 shard_map.157
  41.7 0.2 broadcast_in_dim.42
  42.0 42.1 %all_to_all.26.nodes = bf16[16,400,128]{2,1,0:T(8,128)(2,1)S(1)} all-to-all(bf16[16,400,128]{2,1,0:T(8,128)(2,1)S(1)} %broadcast_in_dim.42), channel_id=1, replica_groups=mesh['xh'=2,'z'=8,'core'=2,'y'=8,'xl'=2] {'y','xl'}, dimensions={0} | all-to-all | bytes 3276800 | tf_op jit(solution)/shard_map/all_to_all | solution.py:32
  84.1 1.2 all-gather.4.cloned.1.call-done
  85.3 4.8 %collective-permute-start = (bf16[8,1376,128]{2,1,0:T(8,128)(2,1)}, bf16[8,1376,128]{2,1,0:T(8,128)(2,1)}, u32[]{:S(2)}, u32[]{:S(2)}) collective-permute-start(bf16[8,1376,128]{2,1,0:T(8,128)(2,1)} %bitcast.40), channel_id=1, source_target_pairs={{0,16},{16,0},{1,17},{17,1},{2,18},{18,2},{3,19},{19,3},{4,20},{20... | collective-permute-start | bytes 8454152 | tf_op jit(solution)/shard_map/ppermute | solution.py:770
  90.8 1.8 copy-done.1
  92.6 3.7 %shard_map.158 = (bf16[29,128,128]{2,1,0:T(8,128)(2,1)S(1)}, bf16[600,128,128]{2,1,0:T(8,128)(2,1)}, bf16[7,8,1376,128]{3,2,1,0:T(8,128)(2,1)}) custom-call(s32[8,128]{1,0:T(8,128)S(1)} %stack.12.ids, bf16[16,400,128]{2,1,0:T(8,128)(2,1)S(1)} %all_to_all.26.nodes, bf16[49,29,128]{2,1,0:T(8,128)(2,1)S(1)} %bitcast.36, bf16[8,1376,128]{2,1,0:T(8,128)(2,1)S(1)} %bitcast.41), custom_call_target="tpu_custom_call" | custom-call | tf_op jit(solution)/shard_map/pallas_call | solution.py:780
  96.3 8.1 %shard_map.159 = (bf16[600,128,128]{2,1,0:T(8,128)(2,1)}, bf16[7,8,1376,128]{3,2,1,0:T(8,128)(2,1)}, f32[8,128]{1,0:T(8,128)S(1)}, f32[16,8,128]{2,1,0:T(8,128)}...) custom-call(s32[1,1]{1,0:T(1,128)} %bitcast.2.first, ...), custom_call_target="tpu_custom_call", output_to_operand_aliasing={{0}: (4, {}), {1}: (6, {})} | custom-call | tf_op jit(solution)/shard_map/pallas_call | solution.py:802
  104.5 7.5 %all-to-all-start.2 = ((f32[16,8,128]{2,1,0:T(8,128)}), f32[16,8,128]{2,1,0:T(8,128)S(1)}, u32[]{:S(2)}, u32[]{:S(2)}) async-start(f32[16,8,128]{2,1,0:T(8,128)} %get-tuple-element.33), calls=%async_computation.2 | async-start | bytes 131072 | tf_op jit(solution)/shard_map/all_to_all | solution.py:36
  111.9 0.1 copy.23.attention
  112.1 7.8 %all-to-all-done.2.every = f32[16,8,128]{2,1,0:T(8,128)S(1)} async-done(((f32[16,8,128]{2,1,0:T(8,128)}), f32[16,8,128]{2,1,0:T(8,128)S(1)}, u32[]{:S(2)}, u32[]{:S(2)}) %all-to-all-start.2) | async-done | bytes 65568 | tf_op jit(solution)/shard_map/all_to_all | solution.py:36
  119.8 4.1 %shard_map.160 = (bf16[600,128,128]{2,1,0:T(8,128)(2,1)}, bf16[16,32,896]{2,1,0:T(8,128)(2,1)S(1)}, bf16[16,32,896]{2,1,0:T(8,128)(2,1)S(1)}) custom-call(s32[1,1]{1,0:T(1,128)} %bitcast.2.first, s32[8,128]{1,0:T(8,128)S(1)} %stack.12.ids, f32[8,128]{1,0:T(8,128)S(1)} %get-tuple-element.32.stats, ...), custom_call_target="tpu_custom_call", output_to_operand_aliasing={{0}: (7, {})} | custom-call | tf_op jit(solution)/shard_map/pallas_call | solution.py:835
  124.0 3.3 %collective-permute-start.1 = (bf16[16,32,896]{2,1,0:T(8,128)(2,1)S(1)}, bf16[16,32,896]{2,1,0:T(8,128)(2,1)S(1)}, u32[]{:S(2)}, u32[]{:S(2)}) collective-permute-start(bf16[16,32,896]{2,1,0:T(8,128)(2,1)S(1)} %get-tuple-element.38), channel_id=1, source_target_pairs={{0,16},{16,0},{1,17},{17,1},{2,18},{18,2},{3,19},{19,3},{4,20},{20... | collective-permute-start | bytes 2752520 | tf_op jit(solution)/shard_map/ppermute | solution.py:858
  127.3 2.1 %collective-permute-done.1 = bf16[16,32,896]{2,1,0:T(8,128)(2,1)S(1)} collective-permute-done((bf16[16,32,896]{2,1,0:T(8,128)(2,1)S(1)}, bf16[16,32,896]{2,1,0:T(8,128)(2,1)S(1)}, u32[]{:S(2)}, u32[]{:S(2)}) %collective-permute-start.1) | collective-permute-done | bytes 917536 | tf_op jit(solution)/shard_map/ppermute | solution.py:858
  129.4 1.2 add_convert_fusion
  130.6 7.6 %all-to-all-start.3 = ((bf16[16,32,896]{2,1,0:T(8,128)(2,1)}), bf16[16,32,896]{2,1,0:T(8,128)(2,1)S(1)}, u32[]{:S(2)}, u32[]{:S(2)}) async-start(bf16[16,32,896]{2,1,0:T(8,128)(2,1)} %add_convert_fusion), calls=%async_computation.4 | async-start | bytes 1835008 | tf_op jit(solution)/shard_map/all_to_all | solution.py:36
  138.2 0.2 reduce-scatter.2.cloned.1.call-start
  138.4 3.6 %shard_map.161 = bf16[16,208,128]{2,1,0:T(8,128)(2,1)} custom-call(s32[8,128]{1,0:T(8,128)S(1)} %stack.12.ids, f32[8,128]{1,0:T(8,128)S(1)} %get-tuple-element.32.stats, f32[16,8,128]{2,1,0:T(8,128)S(1)} %all-to-all-done.2.every, bf16[600,128,128]{2,1,0:T(8,128)(2,1)} %get-tuple-element.43.spill), custom_call_target="tpu_custom_call" | custom-call | tf_op jit(solution)/shard_map/pallas_call | solution.py:862
  142.0 8.9 %shard_map.162.spill = bf16[600,128,128]{2,1,0:T(8,128)(2,1)} custom-call(s32[8,128]{1,0:T(8,128)S(1)} %stack.12.ids, bf16[600,128,128]{2,1,0:T(8,128)(2,1)} %get-tuple-element.43.spill, bf16[49,29,128]{2,1,0:T(8,128)(2,1)S(1)} %bitcast.39, bf16[7,8,1376,128]{3,2,1,0:T(8,128)(2,1)} %get-tuple-element.44.maps), custom_call_target="tpu_custom_call", output_to_operand_aliasing={{}: (1, {})} | custom-call | tf_op jit(solution)/shard_map/pallas_call | solution.py:884
  150.9 10.6 %all-to-all-done.3.parts = bf16[16,32,896]{2,1,0:T(8,128)(2,1)S(1)} async-done(((bf16[16,32,896]{2,1,0:T(8,128)(2,1)}), bf16[16,32,896]{2,1,0:T(8,128)(2,1)S(1)}, u32[]{:S(2)}, u32[]{:S(2)}) %all-to-all-start.3) | async-done | bytes 917536 | tf_op jit(solution)/shard_map/all_to_all | solution.py:36
  161.5 2.5 %shard_map.163 = bf16[16,224,128]{2,1,0:T(8,128)(2,1)} custom-call(bf16[16,32,896]{2,1,0:T(8,128)(2,1)S(1)} %all-to-all-done.3.parts, bf16[600,128,128]{2,1,0:T(8,128)(2,1)} %shard_map.162.spill), custom_call_target="tpu_custom_call" | custom-call | tf_op jit(solution)/shard_map/pallas_call | solution.py:908
  164.0 3.6 %all-to-all-start.4 = ((bf16[16,224,128]{2,1,0:T(8,128)(2,1)}), bf16[16,224,128]{2,1,0:T(8,128)(2,1)S(1)}, u32[]{:S(2)}, u32[]{:S(2)}) async-start(bf16[16,224,128]{2,1,0:T(8,128)(2,1)} %shard_map.163), calls=%async_computation.5 | async-start | bytes 1835008 | tf_op jit(solution)/shard_map/all_to_all | solution.py:36
  167.6 8.7 %reduce-scatter.2.cloned.1.call-done = bf16[1,416,128]{2,1,0:T(8,128)(2,1)} async-done(((bf16[8,416,128]{2,1,0:T(8,128)(2,1)}), bf16[1,416,128]{2,1,0:T(8,128)(2,1)}) %reduce-scatter.2.cloned.1.call-update) | async-done | bytes 106512 | tf_op jit(solution)/shard_map/reduce_scatter | solution.py:872
  176.3 0.8 dynamic-slice_bitcast_fusion
  177.2 2.6 %collective-permute-start.2 = (bf16[208,128]{1,0:T(8,128)(2,1)S(1)}, bf16[208,128]{1,0:T(8,128)(2,1)S(1)}, u32[]{:S(2)}, u32[]{:S(2)}) collective-permute-start(bf16[208,128]{1,0:T(8,128)(2,1)S(1)} %get-tuple-element.48), channel_id=1, source_target_pairs={{0,1},{1,0},{2,3},{3,2},{4,5},{5,4},{6,7},{7,6},{8,9},{9,8},{10,11... | collective-permute-start | bytes 159752 | tf_op jit(solution)/shard_map/ppermute | solution.py:877
  179.8 2.9 %collective-permute-done.2 = bf16[208,128]{1,0:T(8,128)(2,1)S(1)} collective-permute-done((bf16[208,128]{1,0:T(8,128)(2,1)S(1)}, bf16[208,128]{1,0:T(8,128)(2,1)S(1)}, u32[]{:S(2)}, u32[]{:S(2)}) %collective-permute-start.2) | collective-permute-done | bytes 53280 | tf_op jit(solution)/shard_map/ppermute | solution.py:877
  182.7 0.7 fusion
  183.4 7.2 %all-to-all-done.4.parts = bf16[16,224,128]{2,1,0:T(8,128)(2,1)S(1)} async-done(((bf16[16,224,128]{2,1,0:T(8,128)(2,1)}), bf16[16,224,128]{2,1,0:T(8,128)(2,1)S(1)}, u32[]{:S(2)}, u32[]{:S(2)}) %all-to-all-start.4) | async-done | bytes 917536 | tf_op jit(solution)/shard_map/all_to_all | solution.py:36
  190.6 0.9 shard_map.164
  (30 shorter events, 0.5 us)
Async XLA Ops:
  7.2 34.3 %copy-start.3 = (f32[1,4,49,128]{3,1,2,0:T(4,128)S(1)}, f32[1,4,49,128]{3,1,2,0:T(4,128)}, u32[]{:S(2)}) copy-start(f32[1,4,49,128]{3,1,2,0:T(4,128)} %param.19) | copy-start | bytes 301060
  7.2 34.4 %copy-start.4 = (bf16[1,4,49,128]{3,1,2,0:T(4,128)(2,1)S(1)}, bf16[1,4,49,128]{3,1,2,0:T(4,128)(2,1)}, u32[]{:S(2)}) copy-start(bf16[1,4,49,128]{3,1,2,0:T(4,128)(2,1)} %param.13) | copy-start | bytes 150532
  7.2 78.1 %all-gather.4.cloned.1.call-start = ((), (), s32[]{:S(2)}) async-start(), calls=%async_computation.7 | async-start | bytes 3170304 | tf_op jit(solution)/shard_map/all_gather | solution.py:728
  41.6 49.2 %copy-start.5 = (s32[1,128]{1,0:T(1,128)S(1)}, s32[1,128]{1,0:T(1,128)}, u32[]{:S(2)}) copy-start(s32[1,128]{1,0:T(1,128)} %param.16) | copy-start | bytes 1540
  41.6 49.2 %copy-start.6 = (s32[1,128]{1,0:T(1,128)S(1)}, s32[1,128]{1,0:T(1,128)}, u32[]{:S(2)}) copy-start(s32[1,128]{1,0:T(1,128)} %param.17) | copy-start | bytes 1540
  41.6 49.2 %copy-start = (bf16[1,29,49,128]{3,1,2,0:T(8,128)(2,1)S(1)}, bf16[1,29,49,128]{3,1,2,0:T(8,128)(2,1)}, u32[]{:S(2)}) copy-start(bf16[1,29,49,128]{3,1,2,0:T(8,128)(2,1)} %param.18) | copy-start | bytes 1091332
  84.1 12.2 %copy-start.2 = (bf16[128,8]{0,1:T(8,128)(2,1)S(1)}, bf16[128,8]{0,1:T(8,128)(2,1)}, u32[]{:S(2)}) copy-start(bf16[128,8]{0,1:T(8,128)(2,1)} %param.25) | copy-start | bytes 6148
  85.3 11.0 %collective-permute-start = (bf16[8,1376,128]{2,1,0:T(8,128)(2,1)}, bf16[8,1376,128]{2,1,0:T(8,128)(2,1)}, u32[]{:S(2)}, u32[]{:S(2)}) collective-permute-start(bf16[8,1376,128]{2,1,0:T(8,128)(2,1)} %bitcast.40), channel_id=1, source_target_pairs={{0,16},{16,0},{1,17},{17,1},{2,18},{18,2},{3,19},{19,3},{4,20},{20... | collective-permute-start | bytes 8454152 | tf_op jit(solution)/shard_map/ppermute | solution.py:770
  90.8 1.8 copy-start.1
  104.5 15.4 %all-to-all-start.2 = ((f32[16,8,128]{2,1,0:T(8,128)}), f32[16,8,128]{2,1,0:T(8,128)S(1)}, u32[]{:S(2)}, u32[]{:S(2)}) async-start(f32[16,8,128]{2,1,0:T(8,128)} %get-tuple-element.33), calls=%async_computation.2 | async-start | bytes 131072 | tf_op jit(solution)/shard_map/all_to_all | solution.py:36
  124.0 5.4 %collective-permute-start.1 = (bf16[16,32,896]{2,1,0:T(8,128)(2,1)S(1)}, bf16[16,32,896]{2,1,0:T(8,128)(2,1)S(1)}, u32[]{:S(2)}, u32[]{:S(2)}) collective-permute-start(bf16[16,32,896]{2,1,0:T(8,128)(2,1)S(1)} %get-tuple-element.38), channel_id=1, source_target_pairs={{0,16},{16,0},{1,17},{17,1},{2,18},{18,2},{3,19},{19,3},{4,20},{20... | collective-permute-start | bytes 2752520 | tf_op jit(solution)/shard_map/ppermute | solution.py:858
  130.6 30.9 %all-to-all-start.3 = ((bf16[16,32,896]{2,1,0:T(8,128)(2,1)}), bf16[16,32,896]{2,1,0:T(8,128)(2,1)S(1)}, u32[]{:S(2)}, u32[]{:S(2)}) async-start(bf16[16,32,896]{2,1,0:T(8,128)(2,1)} %add_convert_fusion), calls=%async_computation.4 | async-start | bytes 1835008 | tf_op jit(solution)/shard_map/all_to_all | solution.py:36
  138.2 38.2 %reduce-scatter.2.cloned.1.call-start = ((), (), s32[]{:S(2)}) async-start(), calls=%async_computation.6 | async-start | bytes 958464 | tf_op jit(solution)/shard_map/reduce_scatter | solution.py:872
  164.0 26.7 %all-to-all-start.4 = ((bf16[16,224,128]{2,1,0:T(8,128)(2,1)}), bf16[16,224,128]{2,1,0:T(8,128)(2,1)S(1)}, u32[]{:S(2)}, u32[]{:S(2)}) async-start(bf16[16,224,128]{2,1,0:T(8,128)(2,1)} %shard_map.163), calls=%async_computation.5 | async-start | bytes 1835008 | tf_op jit(solution)/shard_map/all_to_all | solution.py:36
  177.2 5.5 %collective-permute-start.2 = (bf16[208,128]{1,0:T(8,128)(2,1)S(1)}, bf16[208,128]{1,0:T(8,128)(2,1)S(1)}, u32[]{:S(2)}, u32[]{:S(2)}) collective-permute-start(bf16[208,128]{1,0:T(8,128)(2,1)S(1)} %get-tuple-element.48), channel_id=1, source_target_pairs={{0,1},{1,0},{2,3},{3,2},{4,5},{5,4},{6,7},{7,6},{8,9},{9,8},{10,11... | collective-permute-start | bytes 159752 | tf_op jit(solution)/shard_map/ppermute | solution.py:877
Sparse Core Ops, SparseCore 0:
  40.9 44.3 all-gather.3
  142.1 34.1 reduce-scatter.1

commit v8 on v7

--- a/solution.py
+++ b/solution.py
@@ -69,6 +69,20 @@
     return lax.dot_general(
         left, right, (((1,), (1,)), ((), ())), precision=precise, preferred_element_type=f32
     )
+
+
+def in_terms(values):
+    parts, rest = [], values
+    for _ in range(3):
+        low = rest.astype(bf16).astype(f32)
+        parts.append(low)
+        rest = rest - low
+    return jnp.concatenate(parts, axis=0).astype(bf16)
+
+
+def of_terms(stacked):
+    rows = stacked.shape[0] // 3
+    return stacked[:rows] + stacked[rows : 2 * rows] + stacked[2 * rows :]
 
 
 def hot_rows(ids, count):
@@ -371,9 +385,9 @@
     gating = (value / (1.0 + jnp.exp(-value))).astype(bf16)
     logits = half_dot(attention_t[...], gating)
     weight = jnp.where(ids[2:3, :] > 0, jnp.exp(logits), 0.0)
-    target = hot_rows(ids[1:2, :], count)
-    own_sum = nt_full(weight, target)
-    at_edges = full_dot(own_sum, target)
+    target = hot_rows(ids[1:2, :], count).astype(bf16)
+    own_sum = of_terms(nt_dot(in_terms(weight), target))
+    at_edges = of_terms(half_dot(in_terms(own_sum), target))
     own_norm = weight / jnp.where(at_edges > 0.0, at_edges, 1.0)
     norm[...] = widen(own_norm, channels)
 
@@ -382,10 +396,11 @@
         own = norm[at, :]
         total = jnp.zeros((CHUNK, edges), f32)
         for l in range(LMAX + 1):
+            fields = [y[rows_at(k, start), :] for k in ROWS_OF[l]]
             for j in COEFS_OF[l]:
                 acc = None
-                for k in ROWS_OF[l]:
-                    term = wide[j, k : k + 1, :] * y[rows_at(k, start), :]
+                for k, field in zip(ROWS_OF[l], fields):
+                    term = wide[j, k : k + 1, :] * field
                     acc = term if acc is None else acc + term
                 total = total + acc * grad_edge[j, at, :].astype(f32)
                 msg[j, at, :] = (acc * own).astype(bf16)
@@ -396,7 +411,7 @@
     copy = pltpu.make_async_copy(msg, part_of(spill, MESSAGE_PART), out_sem.at[0])
     copy.start()
     grad_norm = jnp.sum(heads_acc[...].reshape(heads, channels // heads, edges), axis=1)
-    own_shared = nt_full(own_norm * grad_norm, target)
+    own_shared = of_terms(nt_dot(in_terms(own_norm * grad_norm), target))
     sums = jnp.concatenate([own_sum, own_shared], axis=1)
     stats[...] = sums
     for owner in range(group):
@@ -443,14 +458,17 @@
     shares = every[:, :, :count] / total[None]
     shared = jnp.sum(shares * every[:, :, count:], axis=0)
     own_share = stats[:, :count] / total
-    target = hot_rows(ids[1:2, :], count)
-    normalized = per_edge[:heads, :] * full_dot(own_share, target)
-    grad_logit = normalized * (per_edge[heads:, :] - full_dot(shared, target))
+    target = hot_rows(ids[1:2, :], count).astype(bf16)
+    at_edges = jnp.concatenate([own_share, shared], axis=0)
+    at_edges = of_terms(half_dot(in_terms(at_edges), target))
+    normalized = per_edge[:heads, :] * at_edges[:heads]
+    grad_logit = normalized * (per_edge[heads:, :] - at_edges[heads:])
     value = scalar[...]
     sigmoid = 1.0 / (1.0 + jnp.exp(-value))
-    gating = (value / (1.0 + jnp.exp(-value))).astype(bf16).astype(f32)
-    att = nt_full(grad_logit, gating)
-    grad_gating = full_dot(attention[...].astype(f32), grad_logit)
+    gating = (value / (1.0 + jnp.exp(-value))).astype(bf16)
+    logit_terms = in_terms(grad_logit)
+    att = of_terms(nt_dot(logit_terms, gating))
+    grad_gating = half_dot(attention[...], logit_terms)
     grad_scalar = grad_gating * sigmoid * (1.0 + value * (1.0 - sigmoid))
     norm[...] = widen(normalized, channels)
 
@@ -575,10 +593,11 @@
     def body(start):
         at = pl.ds(start, CHUNK)
         for l in range(LMAX + 1):
+            fields = [dz[k, at, :] for k in ROWS_OF[l]]
             for j in COEFS_OF[l]:
                 acc = None
-                for k in ROWS_OF[l]:
-                    term = wide[j, k : k + 1, :] * dz[k, at, :]
+                for k, field in zip(ROWS_OF[l], fields):
+                    term = wide[j, k : k + 1, :] * field
                     acc = term if acc is None else acc + term
                 gp[j, at, :] = acc.astype(bf16)
 
@@ -853,7 +872,7 @@
         ],
         input_output_aliases={7: 0},
         compiler_params=LARGE,
-    )(first, ids, stats, every, scalar, per_edge, rotation, spill, attention, attention_t)
+    )(first, ids, stats, every, scalar, per_edge, rotation, spill, jnp.tile(attention, (1, 3)), attention_t)
 
     theirs = lax.ppermute(theirs, "core", [(0, 1), (1, 0)])
     mine = (mine.astype(f32) + theirs.astype(f32)).astype(bf16)

time: 202 us -> 201 us (level)
  no operation moved by 1% of the time
where the time goes in v8:
time: 201 us; the launch traced here: 198 us
  blocking collectives  72.2 us (36%)
  waiting for transfers between devices  40.4 us (20%)
  Pallas kernels  35.1 us (17%)
  starting transfers between devices  29.7 us (15%)
  between operations  15.7 us (8%)
  local copies, waits for them, and re-layouts  3.22 us (2%)
  other arithmetic  2.09 us (1%)
    all_to_all x2, blocking collectives, gather(): return lax.all_to_all(copies, axes, split_axis=0, concat_axis=0, tiled=True)  63.6 us
    all_to_all x3, waiting for transfers between devices, exchange(): return lax.all_to_all(blocks, axes, split_axis=0, concat_axis=0, tiled=True)  25.5 us
    all_to_all x3, starting transfers between devices, exchange(): return lax.all_to_all(blocks, axes, split_axis=0, concat_axis=0, tiled=True)  18.7 us
    pallas_call x1, Pallas kernels, on_device(): pl.pallas_call(functools.partial(scatter_kernel, places, group, row_count...  8.9 us
    reduce_scatter x1, waiting for transfers between devices, on_device(): lax.psum_scatter(message_sums, 'y', scatter_dimension=0, tiled=True)  8.73 us
    all_gather x1, blocking collectives, gather_weights(): near = lax.all_gather(packed, 'core')  8.58 us
    pallas_call x1, Pallas kernels, on_device(): pl.pallas_call(functools.partial(forward_kernel, places, group), out_shap...  8.05 us
    ppermute x1, starting transfers between devices, on_device(): other = lax.ppermute(half, 'core', [(0, 1), (1, 0)])  4.8 us
  transfers between devices with their start and end apart: 8, of which 7 were waited for; matrix products, arithmetic and copies ran while one was open for 1% of the time, Pallas kernels for 9%

profile of v8, /device:TPU:1, one launch (start us, length us, event | category | flops | bytes accessed | tf_op | source)
XLA Modules:
  0.0 198.3 jit_solution(12932112816650118669)
XLA Ops:
  7.2 2.0 shard_map.156
  9.2 8.6 %all-gather = bf16[64,256]{1,0:T(8,128)(2,1)S(1)} all-gather(bf16[32,256]{1,0:T(8,128)(2,1)} %shard_map.156), channel_id=2, replica_groups=mesh['xh'=2,'z'=8,'core'=2,'y'=8,'xl'=2] {'core'}, dimensions={0}, use_global_device_ids=true | all-gather | bytes 49152 | tf_op jit(solution)/shard_map/all_gather | solution.py:726
  17.9 21.5 %all_to_all.25.slabs = bf16[32,64,128]{2,1,0:T(8,128)(2,1)S(1)} all-to-all(bf16[32,64,128]{2,1,0:T(8,128)(2,1)S(1)} %broadcast_in_dim.39), channel_id=1, replica_groups=mesh['xh'=2,'z'=8,'core'=2,'y'=8,'xl'=2] {'xh','y','xl'}, dimensions={0} | all-to-all | bytes 1048576 | tf_op jit(solution)/shard_map/all_to_all | solution.py:32
  39.4 1.4 shard_map.157
  41.7 0.2 broadcast_in_dim.42
  42.0 42.1 %all_to_all.26.nodes = bf16[16,400,128]{2,1,0:T(8,128)(2,1)S(1)} all-to-all(bf16[16,400,128]{2,1,0:T(8,128)(2,1)S(1)} %broadcast_in_dim.42), channel_id=1, replica_groups=mesh['xh'=2,'z'=8,'core'=2,'y'=8,'xl'=2] {'y','xl'}, dimensions={0} | all-to-all | bytes 3276800 | tf_op jit(solution)/shard_map/all_to_all | solution.py:32
  84.1 1.2 all-gather.4.cloned.1.call-done
  85.3 4.8 %collective-permute-start = (bf16[8,1376,128]{2,1,0:T(8,128)(2,1)}, bf16[8,1376,128]{2,1,0:T(8,128)(2,1)}, u32[]{:S(2)}, u32[]{:S(2)}) collective-permute-start(bf16[8,1376,128]{2,1,0:T(8,128)(2,1)} %bitcast.42), channel_id=1, source_target_pairs={{0,16},{16,0},{1,17},{17,1},{2,18},{18,2},{3,19},{19,3},{4,20},{20... | collective-permute-start | bytes 8454152 | tf_op jit(solution)/shard_map/ppermute | solution.py:789
  90.8 1.8 copy-done.1
  92.6 3.7 %shard_map.158 = (bf16[29,128,128]{2,1,0:T(8,128)(2,1)S(1)}, bf16[600,128,128]{2,1,0:T(8,128)(2,1)}, bf16[7,8,1376,128]{3,2,1,0:T(8,128)(2,1)}) custom-call(s32[8,128]{1,0:T(8,128)S(1)} %stack.12.ids, bf16[16,400,128]{2,1,0:T(8,128)(2,1)S(1)} %all_to_all.26.nodes, bf16[49,29,128]{2,1,0:T(8,128)(2,1)S(1)} %bitcast.38, bf16[8,1376,128]{2,1,0:T(8,128)(2,1)S(1)} %bitcast.43), custom_call_target="tpu_custom_call" | custom-call | tf_op jit(solution)/shard_map/pallas_call | solution.py:799
  96.3 8.1 %shard_map.159 = (bf16[600,128,128]{2,1,0:T(8,128)(2,1)}, bf16[7,8,1376,128]{3,2,1,0:T(8,128)(2,1)}, f32[8,128]{1,0:T(8,128)S(1)}, f32[16,8,128]{2,1,0:T(8,128)}...) custom-call(s32[1,1]{1,0:T(1,128)} %bitcast.2.first, ...), custom_call_target="tpu_custom_call", output_to_operand_aliasing={{0}: (4, {}), {1}: (6, {})} | custom-call | tf_op jit(solution)/shard_map/pallas_call | solution.py:821
  104.4 7.5 %all-to-all-start.2 = ((f32[16,8,128]{2,1,0:T(8,128)}), f32[16,8,128]{2,1,0:T(8,128)S(1)}, u32[]{:S(2)}, u32[]{:S(2)}) async-start(f32[16,8,128]{2,1,0:T(8,128)} %get-tuple-element.33), calls=%async_computation.2 | async-start | bytes 131072 | tf_op jit(solution)/shard_map/all_to_all | solution.py:36
  111.9 0.1 copy.23.attention
  112.0 7.8 %all-to-all-done.2.every = f32[16,8,128]{2,1,0:T(8,128)S(1)} async-done(((f32[16,8,128]{2,1,0:T(8,128)}), f32[16,8,128]{2,1,0:T(8,128)S(1)}, u32[]{:S(2)}, u32[]{:S(2)}) %all-to-all-start.2) | async-done | bytes 65568 | tf_op jit(solution)/shard_map/all_to_all | solution.py:36
  119.7 4.1 %shard_map.160 = (bf16[600,128,128]{2,1,0:T(8,128)(2,1)}, bf16[16,32,896]{2,1,0:T(8,128)(2,1)S(1)}, bf16[16,32,896]{2,1,0:T(8,128)(2,1)S(1)}) custom-call(s32[1,1]{1,0:T(1,128)} %bitcast.2.first, s32[8,128]{1,0:T(8,128)S(1)} %stack.12.ids, f32[8,128]{1,0:T(8,128)S(1)} %get-tuple-element.32.stats, ...), custom_call_target="tpu_custom_call", output_to_operand_aliasing={{0}: (7, {})} | custom-call | tf_op jit(solution)/shard_map/pallas_call | solution.py:854
  123.9 3.3 %collective-permute-start.1 = (bf16[16,32,896]{2,1,0:T(8,128)(2,1)S(1)}, bf16[16,32,896]{2,1,0:T(8,128)(2,1)S(1)}, u32[]{:S(2)}, u32[]{:S(2)}) collective-permute-start(bf16[16,32,896]{2,1,0:T(8,128)(2,1)S(1)} %get-tuple-element.38), channel_id=1, source_target_pairs={{0,16},{16,0},{1,17},{17,1},{2,18},{18,2},{3,19},{19,3},{4,20},{20... | collective-permute-start | bytes 2752520 | tf_op jit(solution)/shard_map/ppermute | solution.py:877
  127.3 2.1 %collective-permute-done.1 = bf16[16,32,896]{2,1,0:T(8,128)(2,1)S(1)} collective-permute-done((bf16[16,32,896]{2,1,0:T(8,128)(2,1)S(1)}, bf16[16,32,896]{2,1,0:T(8,128)(2,1)S(1)}, u32[]{:S(2)}, u32[]{:S(2)}) %collective-permute-start.1) | collective-permute-done | bytes 917536 | tf_op jit(solution)/shard_map/ppermute | solution.py:877
  129.3 1.2 add_convert_fusion
  130.5 7.6 %all-to-all-start.3 = ((bf16[16,32,896]{2,1,0:T(8,128)(2,1)}), bf16[16,32,896]{2,1,0:T(8,128)(2,1)S(1)}, u32[]{:S(2)}, u32[]{:S(2)}) async-start(bf16[16,32,896]{2,1,0:T(8,128)(2,1)} %add_convert_fusion), calls=%async_computation.4 | async-start | bytes 1835008 | tf_op jit(solution)/shard_map/all_to_all | solution.py:36
  138.1 0.2 reduce-scatter.2.cloned.1.call-start
  138.3 3.6 %shard_map.161 = bf16[16,208,128]{2,1,0:T(8,128)(2,1)} custom-call(s32[8,128]{1,0:T(8,128)S(1)} %stack.12.ids, f32[8,128]{1,0:T(8,128)S(1)} %get-tuple-element.32.stats, f32[16,8,128]{2,1,0:T(8,128)S(1)} %all-to-all-done.2.every, bf16[600,128,128]{2,1,0:T(8,128)(2,1)} %get-tuple-element.43.spill), custom_call_target="tpu_custom_call" | custom-call | tf_op jit(solution)/shard_map/pallas_call | solution.py:881
  141.9 8.9 %shard_map.162.spill = bf16[600,128,128]{2,1,0:T(8,128)(2,1)} custom-call(s32[8,128]{1,0:T(8,128)S(1)} %stack.12.ids, bf16[600,128,128]{2,1,0:T(8,128)(2,1)} %get-tuple-element.43.spill, bf16[49,29,128]{2,1,0:T(8,128)(2,1)S(1)} %bitcast.41, bf16[7,8,1376,128]{3,2,1,0:T(8,128)(2,1)} %get-tuple-element.44.maps), custom_call_target="tpu_custom_call", output_to_operand_aliasing={{}: (1, {})} | custom-call | tf_op jit(solution)/shard_map/pallas_call | solution.py:903
  150.8 10.6 %all-to-all-done.3.parts = bf16[16,32,896]{2,1,0:T(8,128)(2,1)S(1)} async-done(((bf16[16,32,896]{2,1,0:T(8,128)(2,1)}), bf16[16,32,896]{2,1,0:T(8,128)(2,1)S(1)}, u32[]{:S(2)}, u32[]{:S(2)}) %all-to-all-start.3) | async-done | bytes 917536 | tf_op jit(solution)/shard_map/all_to_all | solution.py:36
  161.4 2.5 %shard_map.163 = bf16[16,224,128]{2,1,0:T(8,128)(2,1)} custom-call(bf16[16,32,896]{2,1,0:T(8,128)(2,1)S(1)} %all-to-all-done.3.parts, bf16[600,128,128]{2,1,0:T(8,128)(2,1)} %shard_map.162.spill), custom_call_target="tpu_custom_call" | custom-call | tf_op jit(solution)/shard_map/pallas_call | solution.py:927
  163.9 3.6 %all-to-all-start.4 = ((bf16[16,224,128]{2,1,0:T(8,128)(2,1)}), bf16[16,224,128]{2,1,0:T(8,128)(2,1)S(1)}, u32[]{:S(2)}, u32[]{:S(2)}) async-start(bf16[16,224,128]{2,1,0:T(8,128)(2,1)} %shard_map.163), calls=%async_computation.5 | async-start | bytes 1835008 | tf_op jit(solution)/shard_map/all_to_all | solution.py:36
  167.5 8.7 %reduce-scatter.2.cloned.1.call-done = bf16[1,416,128]{2,1,0:T(8,128)(2,1)} async-done(((bf16[8,416,128]{2,1,0:T(8,128)(2,1)}), bf16[1,416,128]{2,1,0:T(8,128)(2,1)}) %reduce-scatter.2.cloned.1.call-update) | async-done | bytes 106512 | tf_op jit(solution)/shard_map/reduce_scatter | solution.py:891
  176.3 0.8 dynamic-slice_bitcast_fusion
  177.1 2.6 %collective-permute-start.2 = (bf16[208,128]{1,0:T(8,128)(2,1)S(1)}, bf16[208,128]{1,0:T(8,128)(2,1)S(1)}, u32[]{:S(2)}, u32[]{:S(2)}) collective-permute-start(bf16[208,128]{1,0:T(8,128)(2,1)S(1)} %get-tuple-element.48), channel_id=1, source_target_pairs={{0,1},{1,0},{2,3},{3,2},{4,5},{5,4},{6,7},{7,6},{8,9},{9,8},{10,11... | collective-permute-start | bytes 159752 | tf_op jit(solution)/shard_map/ppermute | solution.py:896
  179.7 3.0 %collective-permute-done.2 = bf16[208,128]{1,0:T(8,128)(2,1)S(1)} collective-permute-done((bf16[208,128]{1,0:T(8,128)(2,1)S(1)}, bf16[208,128]{1,0:T(8,128)(2,1)S(1)}, u32[]{:S(2)}, u32[]{:S(2)}) %collective-permute-start.2) | collective-permute-done | bytes 53280 | tf_op jit(solution)/shard_map/ppermute | solution.py:896
  182.7 0.7 fusion
  183.4 7.1 %all-to-all-done.4.parts = bf16[16,224,128]{2,1,0:T(8,128)(2,1)S(1)} async-done(((bf16[16,224,128]{2,1,0:T(8,128)(2,1)}), bf16[16,224,128]{2,1,0:T(8,128)(2,1)S(1)}, u32[]{:S(2)}, u32[]{:S(2)}) %all-to-all-start.4) | async-done | bytes 917536 | tf_op jit(solution)/shard_map/all_to_all | solution.py:36
  190.6 0.9 shard_map.164
  (31 shorter events, 0.5 us)
Async XLA Ops:
  7.2 34.3 %copy-start.3 = (f32[1,4,49,128]{3,1,2,0:T(4,128)S(1)}, f32[1,4,49,128]{3,1,2,0:T(4,128)}, u32[]{:S(2)}) copy-start(f32[1,4,49,128]{3,1,2,0:T(4,128)} %param.19) | copy-start | bytes 301060
  7.2 34.4 %copy-start.4 = (bf16[1,4,49,128]{3,1,2,0:T(4,128)(2,1)S(1)}, bf16[1,4,49,128]{3,1,2,0:T(4,128)(2,1)}, u32[]{:S(2)}) copy-start(bf16[1,4,49,128]{3,1,2,0:T(4,128)(2,1)} %param.13) | copy-start | bytes 150532
  7.2 78.1 %all-gather.4.cloned.1.call-start = ((), (), s32[]{:S(2)}) async-start(), calls=%async_computation.7 | async-start | bytes 3170304 | tf_op jit(solution)/shard_map/all_gather | solution.py:747
  41.6 49.2 %copy-start.5 = (s32[1,128]{1,0:T(1,128)S(1)}, s32[1,128]{1,0:T(1,128)}, u32[]{:S(2)}) copy-start(s32[1,128]{1,0:T(1,128)} %param.16) | copy-start | bytes 1540
  41.6 49.2 %copy-start.6 = (s32[1,128]{1,0:T(1,128)S(1)}, s32[1,128]{1,0:T(1,128)}, u32[]{:S(2)}) copy-start(s32[1,128]{1,0:T(1,128)} %param.17) | copy-start | bytes 1540
  41.6 49.2 %copy-start = (bf16[1,29,49,128]{3,1,2,0:T(8,128)(2,1)S(1)}, bf16[1,29,49,128]{3,1,2,0:T(8,128)(2,1)}, u32[]{:S(2)}) copy-start(bf16[1,29,49,128]{3,1,2,0:T(8,128)(2,1)} %param.18) | copy-start | bytes 1091332
  84.1 12.2 %copy-start.2 = (bf16[128,8]{0,1:T(8,128)(2,1)S(1)}, bf16[128,8]{0,1:T(8,128)(2,1)}, u32[]{:S(2)}) copy-start(bf16[128,8]{0,1:T(8,128)(2,1)} %param.25) | copy-start | bytes 6148
  85.3 11.0 %collective-permute-start = (bf16[8,1376,128]{2,1,0:T(8,128)(2,1)}, bf16[8,1376,128]{2,1,0:T(8,128)(2,1)}, u32[]{:S(2)}, u32[]{:S(2)}) collective-permute-start(bf16[8,1376,128]{2,1,0:T(8,128)(2,1)} %bitcast.42), channel_id=1, source_target_pairs={{0,16},{16,0},{1,17},{17,1},{2,18},{18,2},{3,19},{19,3},{4,20},{20... | collective-permute-start | bytes 8454152 | tf_op jit(solution)/shard_map/ppermute | solution.py:789
  90.8 1.8 copy-start.1
  104.4 15.4 %all-to-all-start.2 = ((f32[16,8,128]{2,1,0:T(8,128)}), f32[16,8,128]{2,1,0:T(8,128)S(1)}, u32[]{:S(2)}, u32[]{:S(2)}) async-start(f32[16,8,128]{2,1,0:T(8,128)} %get-tuple-element.33), calls=%async_computation.2 | async-start | bytes 131072 | tf_op jit(solution)/shard_map/all_to_all | solution.py:36
  123.9 5.4 %collective-permute-start.1 = (bf16[16,32,896]{2,1,0:T(8,128)(2,1)S(1)}, bf16[16,32,896]{2,1,0:T(8,128)(2,1)S(1)}, u32[]{:S(2)}, u32[]{:S(2)}) collective-permute-start(bf16[16,32,896]{2,1,0:T(8,128)(2,1)S(1)} %get-tuple-element.38), channel_id=1, source_target_pairs={{0,16},{16,0},{1,17},{17,1},{2,18},{18,2},{3,19},{19,3},{4,20},{20... | collective-permute-start | bytes 2752520 | tf_op jit(solution)/shard_map/ppermute | solution.py:877
  130.5 30.8 %all-to-all-start.3 = ((bf16[16,32,896]{2,1,0:T(8,128)(2,1)}), bf16[16,32,896]{2,1,0:T(8,128)(2,1)S(1)}, u32[]{:S(2)}, u32[]{:S(2)}) async-start(bf16[16,32,896]{2,1,0:T(8,128)(2,1)} %add_convert_fusion), calls=%async_computation.4 | async-start | bytes 1835008 | tf_op jit(solution)/shard_map/all_to_all | solution.py:36
  138.1 38.2 %reduce-scatter.2.cloned.1.call-start = ((), (), s32[]{:S(2)}) async-start(), calls=%async_computation.6 | async-start | bytes 958464 | tf_op jit(solution)/shard_map/reduce_scatter | solution.py:891
  163.9 26.7 %all-to-all-start.4 = ((bf16[16,224,128]{2,1,0:T(8,128)(2,1)}), bf16[16,224,128]{2,1,0:T(8,128)(2,1)S(1)}, u32[]{:S(2)}, u32[]{:S(2)}) async-start(bf16[16,224,128]{2,1,0:T(8,128)(2,1)} %shard_map.163), calls=%async_computation.5 | async-start | bytes 1835008 | tf_op jit(solution)/shard_map/all_to_all | solution.py:36
  177.1 5.6 %collective-permute-start.2 = (bf16[208,128]{1,0:T(8,128)(2,1)S(1)}, bf16[208,128]{1,0:T(8,128)(2,1)S(1)}, u32[]{:S(2)}, u32[]{:S(2)}) collective-permute-start(bf16[208,128]{1,0:T(8,128)(2,1)S(1)} %get-tuple-element.48), channel_id=1, source_target_pairs={{0,1},{1,0},{2,3},{3,2},{4,5},{5,4},{6,7},{7,6},{8,9},{9,8},{10,11... | collective-permute-start | bytes 159752 | tf_op jit(solution)/shard_map/ppermute | solution.py:896
Sparse Core Ops, SparseCore 0:
  40.9 44.3 all-gather.3
  142.0 34.1 reduce-scatter.1

commit v9 on v8

--- a/solution.py
+++ b/solution.py
@@ -120,9 +120,6 @@
                 halves[half].at[:, span, :], held.at[half, :, span, :], sems.at[i]
             ).start()
 
-    if first is None:
-        return go((mine, other))
-
     @pl.when(first == 0)
     def _():
         go((mine, other))
@@ -202,9 +199,14 @@
     out[...] = acc[...].astype(bf16)
 
 
-def slab_kernel(sets, first, slabs, out):
-    group, most, lanes = slabs.shape[0] // 2, slabs.shape[1] // 2, slabs.shape[2]
-    blocks = [jnp.concatenate([slabs[g], slabs[group + g]], axis=0) for g in range(group)]
+def slab_kernel(sets, fold, first, slabs, out):
+    group, lanes = slabs.shape[0] // 2, slabs.shape[2] // fold
+    most = slabs.shape[1] * fold // 2
+
+    def unfolded(i):
+        return [slabs[i][:, q * lanes : (q + 1) * lanes] for q in range(fold)]
+
+    blocks = [jnp.concatenate(unfolded(g) + unfolded(group + g), axis=0) for g in range(group)]
 
     def rolled(which):
         wide = [block.astype(f32) for block in blocks]
@@ -377,7 +379,7 @@
             acc = term if acc is None else acc + term
         spread(acc[:, :edges], held, real[2], base * channels, y)
         spread(acc[:, edges:], held, real[2], (base + rows) * channels, y)
-    maps_copy = pltpu.make_async_copy(held, maps.at[pl.ds(0, 2)], out_sem.at[2])
+    maps_copy = pltpu.make_async_copy(other, maps.at[1], out_sem.at[2])
     maps_copy.start()
     value = y[:channels, :]
     scalar[...] = value
@@ -530,6 +532,7 @@
     places,
     group,
     own,
+    first,
     ids,
     spill,
     wigner,
@@ -550,8 +553,8 @@
     count = own * group
     conv_copy = pltpu.make_async_copy(part_of(spill, CONV_PART), grad_conv, out_sem.at[1])
     conv_copy.start()
-    mine = maps.at[0]
-    start_weights(places, None, mine, maps.at[1], held, sems)
+    mine = maps.at[2]
+    start_weights(places, first[0, 0], mine, maps.at[1], held, sems)
     wide[...] = wigner[...].astype(f32)
     conv_copy.wait()
     grad[...] = grad_conv[...].astype(f32).reshape(grad.shape)
@@ -725,7 +728,9 @@
     core = lax.axis_index("core")
     near = lax.all_gather(packed, "core")
     sent = lax.dynamic_slice_in_dim(near, core * lanes, lanes, axis=2)
-    slabs = gather(sent.reshape(2 * most, lanes), ROW_GROUP)
+    fold = 4 if lanes == LANES else 1
+    sent = jnp.transpose(sent.reshape(fold, 2 * most // fold, lanes), (1, 0, 2))
+    slabs = gather(sent.reshape(2 * most // fold, fold * lanes), ROW_GROUP)
     group = slabs.shape[0] // 2
     places = [None] * len(shards)
     depth = 0
@@ -738,7 +743,7 @@
         depth = max(depth, at)
     kinds = [[(rows[i], columns[i], starts[i] - n * lanes) for i in s] for n, s in enumerate(sets)]
     tiled = pl.pallas_call(
-        functools.partial(slab_kernel, kinds),
+        functools.partial(slab_kernel, kinds, fold),
         out_shape=jax.ShapeDtypeStruct((depth, LANES), bf16),
         in_specs=[pl.BlockSpec(memory_space=pltpu.SMEM), VMEM],
         out_specs=VMEM,
@@ -903,7 +908,7 @@
     spill = pl.pallas_call(
         functools.partial(scatter_kernel, places, group, row_count),
         out_shape=spill_shape,
-        in_specs=[VMEM, HBM, VMEM, HBM],
+        in_specs=[smem, VMEM, HBM, VMEM, HBM],
         out_specs=HBM,
         scratch_shapes=[
             held,
@@ -917,9 +922,9 @@
             copies,
             two_copies,
         ],
-        input_output_aliases={1: 0},
+        input_output_aliases={2: 0},
         compiler_params=LARGE,
-    )(ids, spill, rotation, maps)
+    )(first, ids, spill, rotation, maps)
     sums_shape = (group, -(-(used + tail_rows) // 16) * 16, channels)
     nodes_shape = jax.ShapeDtypeStruct((harmonics, row_count, channels), bf16)
     batch_scale = 1.0 / (2 * columns)

time: 201 us -> 285 us (1.42)
  Pallas kernels: 35.1 us -> 119 us
    pallas_call x1, Pallas kernels: 8.05 us -> 91.8 us  [on_device(): pl.pallas_call(functools.partial(forward_kernel, places, group), out_shap...]
  transfers between devices with their start and end apart: 8 -> 8, of which waited for: 7 -> 7; matrix products, arithmetic and copies ran while one was open for 1% -> 1% of each run, Pallas kernels for 9% -> 7%
where the time goes in v9:
time: 285 us; the launch traced here: 282 us
  Pallas kernels  119 us (42%)
  blocking collectives  72.2 us (25%)
  waiting for transfers between devices  40.4 us (14%)
  starting transfers between devices  29.7 us (10%)
  between operations  15.6 us (5%)
  local copies, waits for them, and re-layouts  3.17 us (1%)
    pallas_call x1, Pallas kernels, on_device(): pl.pallas_call(functools.partial(forward_kernel, places, group), out_shap...  91.8 us
    all_to_all x2, blocking collectives, gather(): return lax.all_to_all(copies, axes, split_axis=0, concat_axis=0, tiled=True)  63.6 us
    all_to_all x3, waiting for transfers between devices, exchange(): return lax.all_to_all(blocks, axes, split_axis=0, concat_axis=0, tiled=True)  25.5 us
    all_to_all x3, starting transfers between devices, exchange(): return lax.all_to_all(blocks, axes, split_axis=0, concat_axis=0, tiled=True)  18.7 us
    pallas_call x1, Pallas kernels, on_device(): pl.pallas_call(functools.partial(scatter_kernel, places, group, row_count...  8.91 us
    reduce_scatter x1, waiting for transfers between devices, on_device(): lax.psum_scatter(message_sums, 'y', scatter_dimension=0, tiled=True)  8.73 us
    all_gather x1, blocking collectives, gather_weights(): near = lax.all_gather(packed, 'core')  8.58 us
  transfers between devices with their start and end apart: 8, of which 7 were waited for; matrix products, arithmetic and copies ran while one was open for 1% of the time, Pallas kernels for 7%

profile of v9, /device:TPU:1, one launch (start us, length us, event | category | flops | bytes accessed | tf_op | source)
XLA Modules:
  0.0 282.0 jit_solution(10940922398241382842)
XLA Ops:
  7.2 2.0 shard_map.156
  9.2 8.6 %all-gather = bf16[64,256]{1,0:T(8,128)(2,1)S(1)} all-gather(bf16[32,256]{1,0:T(8,128)(2,1)} %shard_map.156), channel_id=2, replica_groups=mesh['xh'=2,'z'=8,'core'=2,'y'=8,'xl'=2] {'core'}, dimensions={0}, use_global_device_ids=true | all-gather | bytes 49152 | tf_op jit(solution)/shard_map/all_gather | solution.py:729
  17.9 21.5 %all_to_all.25.slabs = bf16[32,16,512]{2,1,0:T(8,128)(2,1)S(1)} all-to-all(bf16[32,16,512]{2,1,0:T(8,128)(2,1)S(1)} %broadcast_in_dim.39), channel_id=1, replica_groups=mesh['xh'=2,'z'=8,'core'=2,'y'=8,'xl'=2] {'xh','y','xl'}, dimensions={0} | all-to-all | bytes 1048576 | tf_op jit(solution)/shard_map/all_to_all | solution.py:32
  39.3 1.4 shard_map.157
  41.7 0.2 broadcast_in_dim.42
  41.9 42.1 %all_to_all.26.nodes = bf16[16,400,128]{2,1,0:T(8,128)(2,1)S(1)} all-to-all(bf16[16,400,128]{2,1,0:T(8,128)(2,1)S(1)} %broadcast_in_dim.42), channel_id=1, replica_groups=mesh['xh'=2,'z'=8,'core'=2,'y'=8,'xl'=2] {'y','xl'}, dimensions={0} | all-to-all | bytes 3276800 | tf_op jit(solution)/shard_map/all_to_all | solution.py:32
  84.1 1.2 all-gather.4.cloned.1.call-done
  85.2 4.8 %collective-permute-start = (bf16[8,1376,128]{2,1,0:T(8,128)(2,1)}, bf16[8,1376,128]{2,1,0:T(8,128)(2,1)}, u32[]{:S(2)}, u32[]{:S(2)}) collective-permute-start(bf16[8,1376,128]{2,1,0:T(8,128)(2,1)} %bitcast.48), channel_id=1, source_target_pairs={{0,16},{16,0},{1,17},{17,1},{2,18},{18,2},{3,19},{19,3},{4,20},{20... | collective-permute-start | bytes 8454152 | tf_op jit(solution)/shard_map/ppermute | solution.py:794
  90.7 1.8 copy-done.1
  92.5 3.7 %shard_map.158 = (bf16[29,128,128]{2,1,0:T(8,128)(2,1)S(1)}, bf16[600,128,128]{2,1,0:T(8,128)(2,1)}, bf16[7,8,1376,128]{3,2,1,0:T(8,128)(2,1)}) custom-call(s32[8,128]{1,0:T(8,128)S(1)} %stack.12.ids, bf16[16,400,128]{2,1,0:T(8,128)(2,1)S(1)} %all_to_all.26.nodes, bf16[49,29,128]{2,1,0:T(8,128)(2,1)S(1)} %bitcast.44, bf16[8,1376,128]{2,1,0:T(8,128)(2,1)S(1)} %bitcast.49), custom_call_target="tpu_custom_call" | custom-call | tf_op jit(solution)/shard_map/pallas_call | solution.py:804
  96.3 91.8 %shard_map.159 = (bf16[600,128,128]{2,1,0:T(8,128)(2,1)}, bf16[7,8,1376,128]{3,2,1,0:T(8,128)(2,1)}, f32[8,128]{1,0:T(8,128)S(1)}, f32[16,8,128]{2,1,0:T(8,128)}...) custom-call(s32[1,1]{1,0:T(1,128)} %bitcast.2.first, ...), custom_call_target="tpu_custom_call", output_to_operand_aliasing={{0}: (4, {}), {1}: (6, {})} | custom-call | tf_op jit(solution)/shard_map/pallas_call | solution.py:826
  188.1 7.5 %all-to-all-start.2 = ((f32[16,8,128]{2,1,0:T(8,128)}), f32[16,8,128]{2,1,0:T(8,128)S(1)}, u32[]{:S(2)}, u32[]{:S(2)}) async-start(f32[16,8,128]{2,1,0:T(8,128)} %get-tuple-element.33), calls=%async_computation.2 | async-start | bytes 131072 | tf_op jit(solution)/shard_map/all_to_all | solution.py:36
  195.6 0.1 copy.26.attention
  195.7 7.8 %all-to-all-done.2.every = f32[16,8,128]{2,1,0:T(8,128)S(1)} async-done(((f32[16,8,128]{2,1,0:T(8,128)}), f32[16,8,128]{2,1,0:T(8,128)S(1)}, u32[]{:S(2)}, u32[]{:S(2)}) %all-to-all-start.2) | async-done | bytes 65568 | tf_op jit(solution)/shard_map/all_to_all | solution.py:36
  203.5 4.1 %shard_map.160 = (bf16[600,128,128]{2,1,0:T(8,128)(2,1)}, bf16[16,32,896]{2,1,0:T(8,128)(2,1)S(1)}, bf16[16,32,896]{2,1,0:T(8,128)(2,1)S(1)}) custom-call(s32[1,1]{1,0:T(1,128)} %bitcast.2.first, s32[8,128]{1,0:T(8,128)S(1)} %stack.12.ids, f32[8,128]{1,0:T(8,128)S(1)} %get-tuple-element.32.stats, ...), custom_call_target="tpu_custom_call", output_to_operand_aliasing={{0}: (7, {})} | custom-call | tf_op jit(solution)/shard_map/pallas_call | solution.py:859
  207.6 3.3 %collective-permute-start.1 = (bf16[16,32,896]{2,1,0:T(8,128)(2,1)S(1)}, bf16[16,32,896]{2,1,0:T(8,128)(2,1)S(1)}, u32[]{:S(2)}, u32[]{:S(2)}) collective-permute-start(bf16[16,32,896]{2,1,0:T(8,128)(2,1)S(1)} %get-tuple-element.38), channel_id=1, source_target_pairs={{0,16},{16,0},{1,17},{17,1},{2,18},{18,2},{3,19},{19,3},{4,20},{20... | collective-permute-start | bytes 2752520 | tf_op jit(solution)/shard_map/ppermute | solution.py:882
  211.0 2.1 collective-permute-done.1
  213.0 1.2 add_convert_fusion
  214.2 7.6 %all-to-all-start.3 = ((bf16[16,32,896]{2,1,0:T(8,128)(2,1)}), bf16[16,32,896]{2,1,0:T(8,128)(2,1)S(1)}, u32[]{:S(2)}, u32[]{:S(2)}) async-start(bf16[16,32,896]{2,1,0:T(8,128)(2,1)} %add_convert_fusion), calls=%async_computation.4 | async-start | bytes 1835008 | tf_op jit(solution)/shard_map/all_to_all | solution.py:36
  221.8 0.2 reduce-scatter.2.cloned.1.call-start
  222.0 3.6 %shard_map.161 = bf16[16,208,128]{2,1,0:T(8,128)(2,1)} custom-call(s32[8,128]{1,0:T(8,128)S(1)} %stack.12.ids, f32[8,128]{1,0:T(8,128)S(1)} %get-tuple-element.32.stats, f32[16,8,128]{2,1,0:T(8,128)S(1)} %all-to-all-done.2.every, bf16[600,128,128]{2,1,0:T(8,128)(2,1)} %get-tuple-element.43.spill), custom_call_target="tpu_custom_call" | custom-call | tf_op jit(solution)/shard_map/pallas_call | solution.py:886
  225.6 8.9 %shard_map.162.spill = bf16[600,128,128]{2,1,0:T(8,128)(2,1)} custom-call(s32[1,1]{1,0:T(1,128)} %bitcast.2.first, s32[8,128]{1,0:T(8,128)S(1)} %stack.12.ids, bf16[600,128,128]{2,1,0:T(8,128)(2,1)} %get-tuple-element.43.spill, bf16[49,29,128]{2,1,0:T(8,128)(2,1)S(1)} %bitcast.47, ...), custom_call_target="tpu_custom_call", output_to_operand_aliasing={{}: (2, {})} | custom-call | tf_op jit(solution)/shard_map/pallas_call | solution.py:908
  234.5 10.5 %all-to-all-done.3.parts = bf16[16,32,896]{2,1,0:T(8,128)(2,1)S(1)} async-done(((bf16[16,32,896]{2,1,0:T(8,128)(2,1)}), bf16[16,32,896]{2,1,0:T(8,128)(2,1)S(1)}, u32[]{:S(2)}, u32[]{:S(2)}) %all-to-all-start.3) | async-done | bytes 917536 | tf_op jit(solution)/shard_map/all_to_all | solution.py:36
  245.1 2.5 shard_map.163
  247.6 3.6 %all-to-all-start.4 = ((bf16[16,224,128]{2,1,0:T(8,128)(2,1)}), bf16[16,224,128]{2,1,0:T(8,128)(2,1)S(1)}, u32[]{:S(2)}, u32[]{:S(2)}) async-start(bf16[16,224,128]{2,1,0:T(8,128)(2,1)} %shard_map.163), calls=%async_computation.5 | async-start | bytes 1835008 | tf_op jit(solution)/shard_map/all_to_all | solution.py:36
  251.2 8.7 %reduce-scatter.2.cloned.1.call-done = bf16[1,416,128]{2,1,0:T(8,128)(2,1)} async-done(((bf16[8,416,128]{2,1,0:T(8,128)(2,1)}), bf16[1,416,128]{2,1,0:T(8,128)(2,1)}) %reduce-scatter.2.cloned.1.call-update) | async-done | bytes 106512 | tf_op jit(solution)/shard_map/reduce_scatter | solution.py:896
  260.0 0.8 dynamic-slice_bitcast_fusion
  260.8 2.6 collective-permute-start.2
  263.4 2.9 %collective-permute-done.2 = bf16[208,128]{1,0:T(8,128)(2,1)S(1)} collective-permute-done((bf16[208,128]{1,0:T(8,128)(2,1)S(1)}, bf16[208,128]{1,0:T(8,128)(2,1)S(1)}, u32[]{:S(2)}, u32[]{:S(2)}) %collective-permute-start.2) | collective-permute-done | bytes 53280 | tf_op jit(solution)/shard_map/ppermute | solution.py:901
  266.4 0.7 fusion
  267.1 7.2 %all-to-all-done.4.parts = bf16[16,224,128]{2,1,0:T(8,128)(2,1)S(1)} async-done(((bf16[16,224,128]{2,1,0:T(8,128)(2,1)}), bf16[16,224,128]{2,1,0:T(8,128)(2,1)S(1)}, u32[]{:S(2)}, u32[]{:S(2)}) %all-to-all-start.4) | async-done | bytes 917536 | tf_op jit(solution)/shard_map/all_to_all | solution.py:36
  274.3 0.9 shard_map.164
  (32 shorter events, 0.5 us)
Async XLA Ops:
  7.2 34.2 %copy-start.3 = (f32[1,4,49,128]{3,1,2,0:T(4,128)S(1)}, f32[1,4,49,128]{3,1,2,0:T(4,128)}, u32[]{:S(2)}) copy-start(f32[1,4,49,128]{3,1,2,0:T(4,128)} %param.19) | copy-start | bytes 301060
  7.2 34.3 %copy-start.4 = (bf16[1,4,49,128]{3,1,2,0:T(4,128)(2,1)S(1)}, bf16[1,4,49,128]{3,1,2,0:T(4,128)(2,1)}, u32[]{:S(2)}) copy-start(bf16[1,4,49,128]{3,1,2,0:T(4,128)(2,1)} %param.13) | copy-start | bytes 150532
  7.2 78.0 %all-gather.4.cloned.1.call-start = ((), (), s32[]{:S(2)}) async-start(), calls=%async_computation.7 | async-start | bytes 3170304 | tf_op jit(solution)/shard_map/all_gather | solution.py:752
  41.5 49.2 %copy-start.5 = (s32[1,128]{1,0:T(1,128)S(1)}, s32[1,128]{1,0:T(1,128)}, u32[]{:S(2)}) copy-start(s32[1,128]{1,0:T(1,128)} %param.16) | copy-start | bytes 1540
  41.5 49.2 %copy-start.6 = (s32[1,128]{1,0:T(1,128)S(1)}, s32[1,128]{1,0:T(1,128)}, u32[]{:S(2)}) copy-start(s32[1,128]{1,0:T(1,128)} %param.17) | copy-start | bytes 1540
  41.5 49.2 %copy-start = (bf16[1,29,49,128]{3,1,2,0:T(8,128)(2,1)S(1)}, bf16[1,29,49,128]{3,1,2,0:T(8,128)(2,1)}, u32[]{:S(2)}) copy-start(bf16[1,29,49,128]{3,1,2,0:T(8,128)(2,1)} %param.18) | copy-start | bytes 1091332
  84.0 12.2 %copy-start.2 = (bf16[128,8]{0,1:T(8,128)(2,1)S(1)}, bf16[128,8]{0,1:T(8,128)(2,1)}, u32[]{:S(2)}) copy-start(bf16[128,8]{0,1:T(8,128)(2,1)} %param.25) | copy-start | bytes 6148
  85.2 11.0 %collective-permute-start = (bf16[8,1376,128]{2,1,0:T(8,128)(2,1)}, bf16[8,1376,128]{2,1,0:T(8,128)(2,1)}, u32[]{:S(2)}, u32[]{:S(2)}) collective-permute-start(bf16[8,1376,128]{2,1,0:T(8,128)(2,1)} %bitcast.48), channel_id=1, source_target_pairs={{0,16},{16,0},{1,17},{17,1},{2,18},{18,2},{3,19},{19,3},{4,20},{20... | collective-permute-start | bytes 8454152 | tf_op jit(solution)/shard_map/ppermute | solution.py:794
  90.7 1.8 copy-start.1
  188.1 15.4 %all-to-all-start.2 = ((f32[16,8,128]{2,1,0:T(8,128)}), f32[16,8,128]{2,1,0:T(8,128)S(1)}, u32[]{:S(2)}, u32[]{:S(2)}) async-start(f32[16,8,128]{2,1,0:T(8,128)} %get-tuple-element.33), calls=%async_computation.2 | async-start | bytes 131072 | tf_op jit(solution)/shard_map/all_to_all | solution.py:36
  207.6 5.4 %collective-permute-start.1 = (bf16[16,32,896]{2,1,0:T(8,128)(2,1)S(1)}, bf16[16,32,896]{2,1,0:T(8,128)(2,1)S(1)}, u32[]{:S(2)}, u32[]{:S(2)}) collective-permute-start(bf16[16,32,896]{2,1,0:T(8,128)(2,1)S(1)} %get-tuple-element.38), channel_id=1, source_target_pairs={{0,16},{16,0},{1,17},{17,1},{2,18},{18,2},{3,19},{19,3},{4,20},{20... | collective-permute-start | bytes 2752520 | tf_op jit(solution)/shard_map/ppermute | solution.py:882
  214.2 30.8 %all-to-all-start.3 = ((bf16[16,32,896]{2,1,0:T(8,128)(2,1)}), bf16[16,32,896]{2,1,0:T(8,128)(2,1)S(1)}, u32[]{:S(2)}, u32[]{:S(2)}) async-start(bf16[16,32,896]{2,1,0:T(8,128)(2,1)} %add_convert_fusion), calls=%async_computation.4 | async-start | bytes 1835008 | tf_op jit(solution)/shard_map/all_to_all | solution.py:36
  221.8 38.2 %reduce-scatter.2.cloned.1.call-start = ((), (), s32[]{:S(2)}) async-start(), calls=%async_computation.6 | async-start | bytes 958464 | tf_op jit(solution)/shard_map/reduce_scatter | solution.py:896
  247.6 26.7 %all-to-all-start.4 = ((bf16[16,224,128]{2,1,0:T(8,128)(2,1)}), bf16[16,224,128]{2,1,0:T(8,128)(2,1)S(1)}, u32[]{:S(2)}, u32[]{:S(2)}) async-start(bf16[16,224,128]{2,1,0:T(8,128)(2,1)} %shard_map.163), calls=%async_computation.5 | async-start | bytes 1835008 | tf_op jit(solution)/shard_map/all_to_all | solution.py:36
  260.8 5.5 %collective-permute-start.2 = (bf16[208,128]{1,0:T(8,128)(2,1)S(1)}, bf16[208,128]{1,0:T(8,128)(2,1)S(1)}, u32[]{:S(2)}, u32[]{:S(2)}) collective-permute-start(bf16[208,128]{1,0:T(8,128)(2,1)S(1)} %get-tuple-element.48), channel_id=1, source_target_pairs={{0,1},{1,0},{2,3},{3,2},{4,5},{5,4},{6,7},{7,6},{8,9},{9,8},{10,11... | collective-permute-start | bytes 159752 | tf_op jit(solution)/shard_map/ppermute | solution.py:901
Sparse Core Ops, SparseCore 0:
  40.9 44.3 all-gather.3
  225.7 34.1 reduce-scatter.1
